TPU v7x, 32 devices: a whole 2x2x4 slice. The times are simulated.
32 devices in a mesh: groups: 2 (over y), dp: 8 (over z, x), tp: 2 (over core).
Axes of the slice: x: 2, y: 2, z: 4, core: 2. Of those that a mesh axis runs over, the one named last changes fastest.
Arguments:
- cache_k: bfloat16 [256, 16, 512], P(('groups', 'dp'), None, 'tp'), parts along dimension 0, may hold values from -6 to 6
- cache_v: bfloat16 [256, 16, 512], P(('groups', 'dp'), None, 'tp'), parts along dimension 0, may hold values from -6 to 6
- sel_rows: int32 [256, 5], P('groups'), parts along dimension 0, may hold values from 0 to 15, as said below
- span_home: int32 [256], P('groups'), parts along dimension 0, may hold values from 0 to 127, as said below
- request_spans: int32 [80, 12], P(('groups', 'dp')), parts along dimension 0, may hold values from 0 to 127, as said below
- fresh_q: bfloat16 [80, 12, 5, 4096], P(('groups', 'dp'), None, None, 'tp'), parts along dimension 0, may hold values from -6 to 6
- fresh_k: bfloat16 [80, 12, 5, 512], P(('groups', 'dp'), None, None, 'tp'), parts along dimension 0, may hold values from -6 to 6
- fresh_v: bfloat16 [80, 12, 5, 512], P(('groups', 'dp'), None, None, 'tp'), parts along dimension 0, may hold values from -6 to 6
- question_q: bfloat16 [80, 32, 4096], P(('groups', 'dp'), None, 'tp'), parts along dimension 0, may hold values from -6 to 6
- question_k: bfloat16 [80, 32, 512], P(('groups', 'dp'), None, 'tp'), parts along dimension 0, may hold values from -6 to 6
- question_v: bfloat16 [80, 32, 512], P(('groups', 'dp'), None, 'tp'), parts along dimension 0, may hold values from -6 to 6
- question_len: int32 [80], P(('groups', 'dp')), parts along dimension 0, may hold values from 1 to 32
Outputs:
- recomputed: bfloat16 [80, 12, 5, 4096], P(('groups', 'dp'), None, None, 'tp'), parts along dimension 0
- answer: bfloat16 [80, 32, 4096], P(('groups', 'dp'), None, 'tp'), parts along dimension 0
There are 2 independent parts, one for each index of `groups`. A program takes and returns all parts, laid end to end along the dimension named above; each array names one. Nothing has to cross between parts.
Inputs may be any that keep to these rules, and one draw needn't show every extreme that they name: `request_spans`: each index of dp holds 60 list entries; at most 8 of them name spans whose storage positions lie on one index of dp (position // 16), and some index reaches 8. `span_home`: A permutation of the positions. `sel_rows`: the rows of one position are distinct.
All inputs are finite; a program needn't handle non-finite values.
Results may differ from a plain program's by a relative error of at most 0.005.
Values may be sent and summed in bfloat16 or wider, within the bound.
No kernel may reach another device: no remote copies, remote signals or barrier semaphores. Data moves between devices by JAX's collectives and lax.ppermute only.
A program may use at most 64 MiB of HBM per device.

v0:
```python
import jax
import jax.numpy as jnp
from jax import lax
from jax.sharding import PartitionSpec as P

HEAD = 128


def attend(queries, keys, values, allowed):
    rows = queries.shape[0]
    width = keys.shape[0]
    kv_heads = keys.shape[1] // HEAD
    group = queries.shape[1] // keys.shape[1]
    q_heads = queries.reshape(rows, kv_heads, group, HEAD)
    k_heads = keys.reshape(width, kv_heads, HEAD)
    v_heads = values.reshape(width, kv_heads, HEAD)
    scores = jnp.einsum("nkgd,mkd->kgnm", q_heads, k_heads, preferred_element_type=jnp.float32)
    scores = scores * (1.0 / float(HEAD) ** 0.5)
    scores = jnp.where(allowed[None, None], scores, -1e30)
    top = jnp.max(scores, axis=-1, keepdims=True)
    exponent = jnp.exp(scores - top)
    weights = (exponent / jnp.sum(exponent, axis=-1, keepdims=True)).astype(jnp.bfloat16)
    result = jnp.einsum("kgnm,mkd->nkgd", weights, v_heads, preferred_element_type=jnp.float32)
    return result.reshape(rows, kv_heads * group * HEAD)


def request_pass(f_query, b_keys, b_values, selected, q_query, q_keys, q_values, q_length):
    lists, picks = selected.shape
    span_len = b_keys.shape[0] // lists
    total = b_keys.shape[0]
    limit = (jnp.arange(lists, dtype=jnp.int32)[:, None] * span_len + selected).reshape(-1)
    allowed = jnp.arange(total, dtype=jnp.int32)[None, :] <= limit[:, None]
    redone = attend(f_query.reshape(lists * picks, -1), b_keys, b_values, allowed)
    redone = redone.astype(jnp.bfloat16).reshape(lists, picks, -1)
    q_rows = q_query.shape[0]
    keys = jnp.concatenate([b_keys, q_keys], axis=0)
    values = jnp.concatenate([b_values, q_values], axis=0)
    column = jnp.arange(total + q_rows, dtype=jnp.int32)[None, :]
    row = jnp.arange(q_rows, dtype=jnp.int32)[:, None]
    allowed_q = (column < total) | (column - total <= row)
    spoken = attend(q_query, keys, values, allowed_q)
    spoken = jnp.where(row < q_length, spoken, 0.0).astype(jnp.bfloat16)
    return (redone, spoken)


def place_rows(rows_at, pieces, span_len):
    onehot = (jnp.arange(span_len, dtype=jnp.int32)[None, None, :] == rows_at[:, :, None]).astype(
        jnp.bfloat16
    )
    placed = jnp.einsum("spr,spw->srw", onehot, pieces, preferred_element_type=jnp.float32)
    return placed.astype(jnp.bfloat16)


def shards(
    cache_k,
    cache_v,
    sel_rows,
    span_home,
    request_spans,
    fresh_q,
    fresh_k,
    fresh_v,
    question_q,
    question_k,
    question_v,
    question_len,
):
    dp_count = lax.axis_size("dp")
    spans_dev, span_len, width = cache_k.shape
    req_count, lists = request_spans.shape
    slot_count = req_count * lists
    capacity = (slot_count + dp_count - 1) // dp_count
    positions = span_home[request_spans.reshape(slot_count)]
    owner = positions // spans_dev
    local = positions % spans_dev
    slot_ids = jnp.arange(slot_count, dtype=jnp.int32)
    same_owner = (owner[:, None] == owner[None, :]) & (slot_ids[None, :] < slot_ids[:, None])
    rank = jnp.sum(same_owner.astype(jnp.int32), axis=1)
    slot_index = owner * capacity + rank
    asking = jnp.full((dp_count * capacity,), -1, jnp.int32).at[slot_index].set(local)
    wanted = lax.all_to_all(asking, "dp", split_axis=0, concat_axis=0, tiled=True)
    wanted = jnp.maximum(wanted, 0)
    send_k = cache_k[wanted]
    send_v = cache_v[wanted]
    selected_here = sel_rows[positions]
    back_k, back_v = (
        lax.all_to_all(send_k, "dp", split_axis=0, concat_axis=0, tiled=True),
        lax.all_to_all(send_v, "dp", split_axis=0, concat_axis=0, tiled=True),
    )
    mine_k = back_k[slot_index]
    mine_v = back_v[slot_index]
    picks = selected_here.shape[1]
    replaced = jnp.any(
        jnp.arange(span_len, dtype=jnp.int32)[None, None, :] == selected_here[:, :, None], axis=1
    )[:, :, None]
    mine_k = jnp.where(
        replaced,
        place_rows(selected_here, fresh_k.reshape(slot_count, picks, width), span_len),
        mine_k,
    )
    mine_v = jnp.where(
        replaced,
        place_rows(selected_here, fresh_v.reshape(slot_count, picks, width), span_len),
        mine_v,
    )
    mine_k = mine_k.reshape(req_count, lists * span_len, width)
    mine_v = mine_v.reshape(req_count, lists * span_len, width)
    selected_req = selected_here.reshape(req_count, lists, picks)

    def one_request(items):
        return request_pass(*items)

    redone, spoken = lax.map(
        one_request,
        (fresh_q, mine_k, mine_v, selected_req, question_q, question_k, question_v, question_len),
    )
    return (redone, spoken)


def solution(mesh):
    in_specs = (
        P(("groups", "dp"), None, "tp"),
        P(("groups", "dp"), None, "tp"),
        P("groups", None),
        P("groups"),
        P(("groups", "dp"), None),
        P(("groups", "dp"), None, None, "tp"),
        P(("groups", "dp"), None, None, "tp"),
        P(("groups", "dp"), None, None, "tp"),
        P(("groups", "dp"), None, "tp"),
        P(("groups", "dp"), None, "tp"),
        P(("groups", "dp"), None, "tp"),
        P(("groups", "dp")),
    )
    out_specs = (P(("groups", "dp"), None, None, "tp"), P(("groups", "dp"), None, "tp"))
    return jax.shard_map(shards, mesh=mesh, in_specs=in_specs, out_specs=out_specs, check_vma=False)
```

profile of v0, /device:TPU:0, one launch (start us, length us, event | category | flops | bytes accessed | tf_op | source)
XLA Modules:
  0.0 114.3 jit_solution(18046875166638197747)
XLA Ops:
  0.7 0.8 reshape.364
  1.5 1.4 %gather_fusion = s32[60]{0:T(128)S(1)} fusion(s32[128]{0:T(128)} %param.17, s32[1024]{0:T(1024)S(1)} %pad_clamp_fusion.3), kind=kCustom, calls=%fused_computation | custom fusion | bytes 720 | tf_op jit(solution)/shard_map/gather | solution.py:73
  3.1 0.8 scatter_custom_fusion
  4.0 13.5 %all_to_all.19 = s32[8,8,1]{1,2,0:T(1,128)S(1)} all-to-all(s32[8,8,1]{1,2,0:T(1,128)S(1)} %bitcast.118), channel_id=1, replica_groups=mesh['groups'=2,'dp'=8,'tp'=2] {'dp'}, dimensions={0} | all-to-all | bytes 512 | tf_op jit(solution)/shard_map/all_to_all | solution.py:81
  17.6 1.4 %gather_fusion.4 = bf16[64,16,256]{2,1,0:T(8,128)(2,1)} fusion(bf16[16,16,256]{2,1,0:T(8,128)(2,1)S(1)} %copy-done, s32[1024]{0:T(1024)S(1)} %pad_clamp_fusion.1), kind=kCustom, calls=%fused_computation.4 | custom fusion | bytes 1048832 | tf_op jit(solution)/shard_map/gather | solution.py:83
  19.0 3.6 %all-to-all-start.2 = ((bf16[64,16,256]{2,1,0:T(8,128)(2,1)}), bf16[64,16,256]{2,1,0:T(8,128)(2,1)S(1)}, u32[]{:S(2)}, u32[]{:S(2)}) async-start(bf16[64,16,256]{2,1,0:T(8,128)(2,1)} %gather_fusion.4), calls=%async_computation.2 | async-start | bytes 1048576 | tf_op jit(solution)/shard_map/all_to_all | solution.py:87
  22.6 1.4 %gather_fusion.2 = bf16[64,16,256]{2,1,0:T(8,128)(2,1)} fusion(bf16[16,16,256]{2,1,0:T(8,128)(2,1)S(1)} %copy-done.1, s32[1024]{0:T(1024)S(1)} %pad_clamp_fusion.1), kind=kCustom, calls=%fused_computation.2 | custom fusion | bytes 1048832 | tf_op jit(solution)/shard_map/gather | solution.py:84
  24.0 11.8 %all-to-all-done.2 = bf16[64,16,256]{2,1,0:T(8,128)(2,1)S(1)} async-done(((bf16[64,16,256]{2,1,0:T(8,128)(2,1)}), bf16[64,16,256]{2,1,0:T(8,128)(2,1)S(1)}, u32[]{:S(2)}, u32[]{:S(2)}) %all-to-all-start.2) | async-done | bytes 524320 | tf_op jit(solution)/shard_map/all_to_all | solution.py:87
  35.9 3.7 %all-to-all-start.1 = ((bf16[64,16,256]{2,1,0:T(8,128)(2,1)}), bf16[64,16,256]{2,1,0:T(8,128)(2,1)S(1)}, u32[]{:S(2)}, u32[]{:S(2)}) async-start(bf16[64,16,256]{2,1,0:T(8,128)(2,1)} %gather_fusion.2), calls=%async_computation.1 | async-start | bytes 1048576 | tf_op jit(solution)/shard_map/all_to_all | solution.py:88
  41.9 11.5 %all-to-all-done.1 = bf16[64,16,256]{2,1,0:T(8,128)(2,1)S(1)} async-done(((bf16[64,16,256]{2,1,0:T(8,128)(2,1)}), bf16[64,16,256]{2,1,0:T(8,128)(2,1)S(1)}, u32[]{:S(2)}, u32[]{:S(2)}) %all-to-all-start.1) | async-done | bytes 524320 | tf_op jit(solution)/shard_map/all_to_all | solution.py:88
  54.7 59.6 %while.14 = (s32[]{:T(128)}, bf16[5,12,5,2048]{3,1,2,0:T(8,128)(2,1)}, bf16[5,32,2048]{2,1,0:T(8,128)(2,1)}, bf16[5,192,256]{2,1,0:T(8,128)(2,1)S(1)}, s32[5,12,...) while((s32[]{:T(128)}, ...), condition=%wide.region_8.9_spmd, body=%wide.region_3.8_spmd.sunk | while | flops 233234464 | bytes 9952601 | solution.py:113
  55.4 0.7 iota_compare_fusion.13
  56.5 0.7 constant_dynamic-slice_fusion.13
  57.3 0.9 dynamic-slice_bitcast_fusion.2
  59.1 1.0 convolution_bitcast_fusion.2
  60.2 1.0 constant_dynamic-slice_fusion.11
  62.2 0.7 fusion.92
  63.3 1.9 %fusion.88 = bf16[60,2,8,128]{3,0,2,1:T(8,128)(2,1)S(1)} fusion(f32[2,8,60]{2,1,0:T(8,128)S(1)} %fusion.86, f32[2,8,60,192]{3,2,1,0:T(8,128)S(1)} %fusion.87, bf16[192,2,128,1]{2,1,0,3:T(2,128)(2,1)S(1)} %bitcast.113), kind=kOutput, calls=%fused_computation.20.clone.1 | convolution fusion | flops 47862912 | bytes 1085184 | tf_op jit(solution)/shard_map/while/body/eval_jaxpr/kgnm,mkd->nkgd/dot_general | solution.py:23
  65.7 0.9 copy_dynamic-update-slice_fusion.2
  67.3 0.7 iota_compare_fusion.13
  68.4 0.7 constant_dynamic-slice_fusion.13
  69.2 0.9 dynamic-slice_bitcast_fusion.2
  70.9 1.0 convolution_bitcast_fusion.2
  72.1 1.0 constant_dynamic-slice_fusion.11
  74.1 0.7 fusion.92
  75.2 1.9 %fusion.88 = bf16[60,2,8,128]{3,0,2,1:T(8,128)(2,1)S(1)} fusion(f32[2,8,60]{2,1,0:T(8,128)S(1)} %fusion.86, f32[2,8,60,192]{3,2,1,0:T(8,128)S(1)} %fusion.87, bf16[192,2,128,1]{2,1,0,3:T(2,128)(2,1)S(1)} %bitcast.113), kind=kOutput, calls=%fused_computation.20.clone.1 | convolution fusion | flops 47862912 | bytes 1085184 | tf_op jit(solution)/shard_map/while/body/eval_jaxpr/kgnm,mkd->nkgd/dot_general | solution.py:23
  77.6 0.9 copy_dynamic-update-slice_fusion.2
  80.3 0.7 constant_dynamic-slice_fusion.13
  81.1 0.9 dynamic-slice_bitcast_fusion.2
  82.9 1.0 convolution_bitcast_fusion.2
  84.0 1.0 constant_dynamic-slice_fusion.11
  86.0 0.7 fusion.92
  87.1 1.9 %fusion.88 = bf16[60,2,8,128]{3,0,2,1:T(8,128)(2,1)S(1)} fusion(f32[2,8,60]{2,1,0:T(8,128)S(1)} %fusion.86, f32[2,8,60,192]{3,2,1,0:T(8,128)S(1)} %fusion.87, bf16[192,2,128,1]{2,1,0,3:T(2,128)(2,1)S(1)} %bitcast.113), kind=kOutput, calls=%fused_computation.20.clone.1 | convolution fusion | flops 47862912 | bytes 1085184 | tf_op jit(solution)/shard_map/while/body/eval_jaxpr/kgnm,mkd->nkgd/dot_general | solution.py:23
  89.5 0.9 copy_dynamic-update-slice_fusion.2
  92.2 0.7 constant_dynamic-slice_fusion.13
  93.0 0.9 dynamic-slice_bitcast_fusion.2
  94.8 1.0 convolution_bitcast_fusion.2
  95.9 1.0 constant_dynamic-slice_fusion.11
  98.0 0.7 fusion.92
  99.1 1.9 %fusion.88 = bf16[60,2,8,128]{3,0,2,1:T(8,128)(2,1)S(1)} fusion(f32[2,8,60]{2,1,0:T(8,128)S(1)} %fusion.86, f32[2,8,60,192]{3,2,1,0:T(8,128)S(1)} %fusion.87, bf16[192,2,128,1]{2,1,0,3:T(2,128)(2,1)S(1)} %bitcast.113), kind=kOutput, calls=%fused_computation.20.clone.1 | convolution fusion | flops 47862912 | bytes 1085184 | tf_op jit(solution)/shard_map/while/body/eval_jaxpr/kgnm,mkd->nkgd/dot_general | solution.py:23
  101.4 0.9 copy_dynamic-update-slice_fusion.2
  104.1 0.7 constant_dynamic-slice_fusion.13
  104.9 0.9 dynamic-slice_bitcast_fusion.2
  106.7 1.0 convolution_bitcast_fusion.2
  107.8 1.0 constant_dynamic-slice_fusion.11
  109.9 0.7 fusion.92
  111.0 1.9 %fusion.88 = bf16[60,2,8,128]{3,0,2,1:T(8,128)(2,1)S(1)} fusion(f32[2,8,60]{2,1,0:T(8,128)S(1)} %fusion.86, f32[2,8,60,192]{3,2,1,0:T(8,128)S(1)} %fusion.87, bf16[192,2,128,1]{2,1,0,3:T(2,128)(2,1)S(1)} %bitcast.113), kind=kOutput, calls=%fused_computation.20.clone.1 | convolution fusion | flops 47862912 | bytes 1085184 | tf_op jit(solution)/shard_map/while/body/eval_jaxpr/kgnm,mkd->nkgd/dot_general | solution.py:23
  113.3 0.9 copy_dynamic-update-slice_fusion.2
  (192 shorter events, 25.0 us)
Async XLA Ops:
  0.6 17.0 %copy-start = (bf16[16,16,256]{2,1,0:T(8,128)(2,1)S(1)}, bf16[16,16,256]{2,1,0:T(8,128)(2,1)}, u32[]{:S(2)}) copy-start(bf16[16,16,256]{2,1,0:T(8,128)(2,1)} %param.14) | copy-start | bytes 393220
  0.6 22.0 %copy-start.1 = (bf16[16,16,256]{2,1,0:T(8,128)(2,1)S(1)}, bf16[16,16,256]{2,1,0:T(8,128)(2,1)}, u32[]{:S(2)}) copy-start(bf16[16,16,256]{2,1,0:T(8,128)(2,1)} %param.15) | copy-start | bytes 393220
  19.0 20.6 %copy-start.4 = (s32[128,5]{0,1:T(8,128)S(1)}, s32[128,5]{0,1:T(8,128)}, u32[]{:S(2)}) copy-start(s32[128,5]{0,1:T(8,128)} %param.16) | copy-start | bytes 7684
  19.0 21.3 %copy-start.2 = (bf16[5,12,5,256]{3,1,2,0:T(8,128)(2,1)S(1)}, bf16[5,12,5,256]{3,1,2,0:T(8,128)(2,1)}, u32[]{:S(2)}) copy-start(bf16[5,12,5,256]{3,1,2,0:T(8,128)(2,1)} %param.20) | copy-start | bytes 460804
  19.0 16.9 %all-to-all-start.2 = ((bf16[64,16,256]{2,1,0:T(8,128)(2,1)}), bf16[64,16,256]{2,1,0:T(8,128)(2,1)S(1)}, u32[]{:S(2)}, u32[]{:S(2)}) async-start(bf16[64,16,256]{2,1,0:T(8,128)(2,1)} %gather_fusion.4), calls=%async_computation.2 | async-start | bytes 1048576 | tf_op jit(solution)/shard_map/all_to_all | solution.py:87
  22.6 17.7 %copy-start.3 = (bf16[5,12,5,256]{3,1,2,0:T(8,128)(2,1)S(1)}, bf16[5,12,5,256]{3,1,2,0:T(8,128)(2,1)}, u32[]{:S(2)}) copy-start(bf16[5,12,5,256]{3,1,2,0:T(8,128)(2,1)} %param.21) | copy-start | bytes 460804
  35.9 17.5 %all-to-all-start.1 = ((bf16[64,16,256]{2,1,0:T(8,128)(2,1)}), bf16[64,16,256]{2,1,0:T(8,128)(2,1)S(1)}, u32[]{:S(2)}, u32[]{:S(2)}) async-start(bf16[64,16,256]{2,1,0:T(8,128)(2,1)} %gather_fusion.2), calls=%async_computation.1 | async-start | bytes 1048576 | tf_op jit(solution)/shard_map/all_to_all | solution.py:88
  41.2 13.5 %copy-start.5 = (s32[5]{0:T(128)S(1)}, s32[5]{0:T(128)}, u32[]{:S(2)}) copy-start(s32[5]{0:T(128)} %param.25) | copy-start | bytes 64
where the time goes:
time: 116 us; the launch traced here: 114 us
  local copies, waits for them, and re-layouts  36.3 us (31%)
  matrix products  23.9 us (21%)
  waiting for transfers between devices  23.3 us (20%)
  blocking collectives  13.5 us (12%)
  other arithmetic  8.18 us (7%)
  starting transfers between devices  7.29 us (6%)
    dot_general x10, matrix products, attend(): jnp.einsum('kgnm,mkd->nkgd', weights, v_heads, preferred_element_type=jnp...  14.6 us
    all_to_all x1, blocking collectives, shards(): lax.all_to_all(asking, 'dp', split_axis=0, concat_axis=0, tiled=True)  13.5 us
    dynamic_slice x30, local copies, waits for them, and re-layouts, shards(): lax.map(one_request, (fresh_q, mine_k, mine_v, selected_req, question_q,...  12.9 us
    all_to_all x1, waiting for transfers between devices, shards(): lax.all_to_all(send_k, 'dp', split_axis=0, concat_axis=0, tiled=True)  11.8 us
    all_to_all x1, waiting for transfers between devices, shards(): lax.all_to_all(send_v, 'dp', split_axis=0, concat_axis=0, tiled=True)  11.5 us
    sub x10, matrix products, attend(): exponent = jnp.exp(scores - top)  4.94 us
    while x10, local copies, waits for them, and re-layouts  4.7 us
    dynamic_update_slice x5, local copies, waits for them, and re-layouts, shards(): lax.map(one_request, (fresh_q, mine_k, mine_v, selected_req, question_q,...  4.51 us
  transfers between devices with their start and end apart: 2, of which 2 were waited for; matrix products, arithmetic and copies ran while one was open for 3% of the time, Pallas kernels for 0%

commit v1 on v0

v1 whole, which is shorter than its diff:
```python
import functools

import jax
import jax.numpy as jnp
from jax import lax
from jax.experimental import pallas as pl
from jax.experimental.pallas import tpu as pltpu
from jax.sharding import PartitionSpec as P

HEAD = 128
LANES = 128
ROW_TILE = 16
MASKED = -1e30
RING_MAX = 16
VMEM_LIMIT = 40 * 1024 * 1024


def fetch_pool(buffers, pool, sems):
    rows = buffers[0].shape[0]
    copies = [
        pltpu.make_async_copy(ref, pool.at[pl.ds(b * rows, rows)], sems.at[b])
        for b, ref in enumerate(buffers)
    ]
    for copy in copies:
        copy.start()
    for copy in copies:
        copy.wait()


def blend(limit, slots, pool, entry_rows, fresh_ref, question_ref, base, fresh_rows):
    lists, span_len = entry_rows
    picks = fresh_ref.shape[1]
    total = lists * span_len
    for j in range(lists):
        base[j * span_len : (j + 1) * span_len, :] = pool[slots(j)]
    fresh_rows[0:picks, 0:lists, :] = fresh_ref[0]
    q_rows = question_ref.shape[1]
    fresh_rows[picks : picks + q_rows // ROW_TILE] = question_ref[0].reshape(
        q_rows // ROW_TILE, ROW_TILE, -1
    )
    padded = base.shape[0]
    key = lax.broadcasted_iota(jnp.int32, (padded, LANES), 0)
    here = jnp.where(key == limit, 1.0, 0.0)
    placed = jnp.dot(
        here.astype(jnp.bfloat16),
        fresh_rows[...].reshape(LANES, -1),
        preferred_element_type=jnp.float32,
    )
    replaced = jnp.max(here, axis=1, keepdims=True) > 0.5
    del total
    return jnp.where(replaced, placed, base[...].astype(jnp.float32)).astype(jnp.bfloat16)


def clear(*refs):
    for ref in refs:
        ref[...] = jnp.zeros_like(ref)


def weights_kernel(n_buf, lists, span_len, slot_ref, limit_ref, fq_ref, qq_ref, fk_ref, qk_ref, *rest):
    buffers = rest[:n_buf]
    out_ref, pool, base, fresh_rows, queries, sems = rest[n_buf:]
    r = pl.program_id(0)
    kv_heads = out_ref.shape[1]
    rows_head = queries.shape[2] * ROW_TILE
    heads = queries.shape[1]
    picks = fq_ref.shape[1]

    @pl.when(r == 0)
    def _():
        clear(base, fresh_rows, queries)
        row = lax.broadcasted_iota(jnp.int32, (rows_head, LANES), 0)
        column = lax.broadcasted_iota(jnp.int32, (rows_head, LANES), 1)
        unit = jnp.where(row == column, 1.0, 0.0).astype(jnp.bfloat16)
        for g in range(kv_heads):
            for h in range(heads):
                queries[g, h, :, :, HEAD:] = unit.reshape(-1, ROW_TILE, LANES)
        fetch_pool(buffers, pool, sems)

    limit = limit_ref[0]
    keys = blend(
        limit,
        lambda j: slot_ref[r * lists + j],
        pool,
        (lists, span_len),
        fk_ref,
        qk_ref,
        base,
        fresh_rows,
    )
    key = lax.broadcasted_iota(jnp.int32, (keys.shape[0], LANES), 0)
    bias = jnp.where(key <= limit, 0.0, MASKED).astype(jnp.bfloat16)
    scale = 1.4426950408889634 / float(HEAD) ** 0.5
    for g in range(kv_heads):
        for h in range(heads):
            at = (g * heads + h) * HEAD
            queries[g, h, 0:picks, 0:lists, 0:HEAD] = fq_ref[0, :, :, at : at + HEAD]
            queries[g, h, picks:, :, 0:HEAD] = qq_ref[0, :, at : at + HEAD].reshape(-1, ROW_TILE, HEAD)
        table = jnp.concatenate([keys[:, g * HEAD : (g + 1) * HEAD], bias], axis=1)
        scores = lax.dot_general(
            queries[g].reshape(heads * rows_head, 2 * HEAD),
            table,
            (((1,), (1,)), ((), ())),
            preferred_element_type=jnp.float32,
        )
        top = jnp.max(scores, axis=1, keepdims=True)
        out_ref[0, g] = jnp.exp2((scores - top) * scale).astype(jnp.bfloat16)


def values_kernel(n_buf, lists, span_len, slot_ref, length_ref, limit_ref, w_ref, fv_ref, qv_ref, *rest):
    buffers = rest[:n_buf]
    redone_ref, spoken_ref, pool, base, fresh_rows, sems = rest[n_buf:]
    r = pl.program_id(0)
    kv_heads = w_ref.shape[1]
    picks = fv_ref.shape[1]
    q_rows = spoken_ref.shape[1]
    heads = spoken_ref.shape[2] // HEAD // kv_heads
    rows_head = picks * ROW_TILE + q_rows

    @pl.when(r == 0)
    def _():
        clear(base, fresh_rows)
        fetch_pool(buffers, pool, sems)

    values = blend(
        limit_ref[0],
        lambda j: slot_ref[r * lists + j],
        pool,
        (lists, span_len),
        fv_ref,
        qv_ref,
        base,
        fresh_rows,
    )
    ones = jnp.ones((values.shape[0], LANES), jnp.bfloat16)
    live = lax.broadcasted_iota(jnp.int32, (q_rows, HEAD), 0) < length_ref[r]
    for g in range(kv_heads):
        table = jnp.concatenate([values[:, g * HEAD : (g + 1) * HEAD], ones], axis=1)
        both = jnp.dot(w_ref[0, g], table, preferred_element_type=jnp.float32)
        result = both[:, :HEAD] / both[:, HEAD:]
        for h in range(heads):
            at = (g * heads + h) * HEAD
            row = h * rows_head
            fresh = result[row : row + picks * ROW_TILE].astype(jnp.bfloat16)
            redone_ref[0, :, :, at : at + HEAD] = fresh.reshape(picks, ROW_TILE, HEAD)[:, :lists, :]
            spoken = result[row + picks * ROW_TILE : row + rows_head]
            spoken_ref[0, :, at : at + HEAD] = jnp.where(live, spoken, 0.0).astype(jnp.bfloat16)


def attend(slots, limit, lengths, k_pieces, v_pieces, fresh_q, fresh_k, fresh_v, question_q, question_k, question_v):
    req_count, picks, lists, q_width = fresh_q.shape
    piece_rows, span_len, width = k_pieces[0].shape
    n_buf = len(k_pieces)
    q_rows = question_q.shape[1]
    kv_heads = width // HEAD
    heads = q_width // width
    rows_head = picks * ROW_TILE + q_rows
    padded = -(-(lists * span_len + q_rows) // LANES) * LANES

    def block(shape):
        return pl.BlockSpec((1,) + tuple(shape[1:]), lambda r, *_: (r,) + (0,) * (len(shape) - 1))

    anywhere = pl.BlockSpec(memory_space=pl.ANY)
    shared = [
        pltpu.VMEM((n_buf * piece_rows, span_len, width), jnp.bfloat16),
        pltpu.VMEM((padded, width), jnp.bfloat16),
        pltpu.VMEM((LANES // ROW_TILE, ROW_TILE, width), jnp.bfloat16),
    ]
    params = pltpu.CompilerParams(dimension_semantics=("arbitrary",), vmem_limit_bytes=VMEM_LIMIT)
    flops = 2 * req_count * kv_heads * heads * rows_head * padded * 2 * HEAD
    w_shape = (req_count, kv_heads, heads * rows_head, padded)
    weights = pl.pallas_call(
        functools.partial(weights_kernel, n_buf, lists, span_len),
        grid_spec=pltpu.PrefetchScalarGridSpec(
            num_scalar_prefetch=1,
            grid=(req_count,),
            in_specs=[
                block(limit.shape),
                block(fresh_q.shape),
                block(question_q.shape),
                block(fresh_k.shape),
                block(question_k.shape),
            ]
            + [anywhere] * n_buf,
            out_specs=block(w_shape),
            scratch_shapes=shared
            + [
                pltpu.VMEM((kv_heads, heads, rows_head // ROW_TILE, ROW_TILE, 2 * HEAD), jnp.bfloat16),
                pltpu.SemaphoreType.DMA((n_buf,)),
            ],
        ),
        out_shape=jax.ShapeDtypeStruct(w_shape, jnp.bfloat16),
        compiler_params=params,
        cost_estimate=pl.CostEstimate(flops=flops, bytes_accessed=8 << 20, transcendentals=flops // 512),
        name="span_weights",
    )(slots, limit, fresh_q, question_q, fresh_k, question_k, *k_pieces)
    return pl.pallas_call(
        functools.partial(values_kernel, n_buf, lists, span_len),
        grid_spec=pltpu.PrefetchScalarGridSpec(
            num_scalar_prefetch=2,
            grid=(req_count,),
            in_specs=[block(limit.shape), block(w_shape), block(fresh_v.shape), block(question_v.shape)]
            + [anywhere] * n_buf,
            out_specs=[block(fresh_q.shape), block(question_q.shape)],
            scratch_shapes=shared + [pltpu.SemaphoreType.DMA((n_buf,))],
        ),
        out_shape=[
            jax.ShapeDtypeStruct(fresh_q.shape, jnp.bfloat16),
            jax.ShapeDtypeStruct(question_q.shape, jnp.bfloat16),
        ],
        compiler_params=params,
        cost_estimate=pl.CostEstimate(flops=flops, bytes_accessed=8 << 20, transcendentals=0),
        name="span_values",
    )(slots, lengths, limit, weights, fresh_v, question_v, *v_pieces)


def ring_gather(keys, values, count):
    order = list(range(0, count, 2)) + list(range(1, count, 2))[::-1]
    onward = [(order[i], order[(i + 1) % count]) for i in range(count)]
    back = [(b, a) for a, b in onward]
    k_at, v_at = {0: keys}, {0: values}
    k_on = k_back = keys
    v_on = v_back = values
    half, rest = count // 2, (count - 1) // 2
    for hop in range(1, half + 1):
        k_on = lax.ppermute(k_on, "dp", onward)
        k_at[hop] = k_on
        if hop <= rest:
            k_back = lax.ppermute(k_back, "dp", back)
            k_at[count - hop] = k_back
            v_on = lax.ppermute(v_on, "dp", onward)
            v_at[hop] = v_on
        v_back = lax.ppermute(v_back, "dp", back)
        v_at[count - hop] = v_back
    return [k_at[d] for d in range(count)], [v_at[d] for d in range(count)]


def ring_slots(positions, spans_dev, count):
    def place(index):
        return jnp.where(index % 2 == 0, index // 2, count - 1 - index // 2)

    upstream = (place(lax.axis_index("dp")) - place(positions // spans_dev)) % count
    return upstream * spans_dev + positions % spans_dev


def asked_gather(keys, values, positions, spans_dev, count):
    slot_count = positions.shape[0]
    capacity = (slot_count + count - 1) // count
    owner = positions // spans_dev
    local = positions % spans_dev
    ids = jnp.arange(slot_count, dtype=jnp.int32)
    earlier = (owner[:, None] == owner[None, :]) & (ids[None, :] < ids[:, None])
    slots = owner * capacity + jnp.sum(earlier.astype(jnp.int32), axis=1)
    asking = jnp.full((count * capacity,), -1, jnp.int32).at[slots].set(local)
    wanted = jnp.maximum(lax.all_to_all(asking, "dp", split_axis=0, concat_axis=0, tiled=True), 0)
    pieces = [
        [lax.all_to_all(cache[wanted], "dp", split_axis=0, concat_axis=0, tiled=True)]
        for cache in (keys, values)
    ]
    return slots, pieces[0], pieces[1]


def shards(
    cache_k,
    cache_v,
    sel_rows,
    span_home,
    request_spans,
    fresh_q,
    fresh_k,
    fresh_v,
    question_q,
    question_k,
    question_v,
    question_len,
):
    count = lax.axis_size("dp")
    spans_dev, span_len, _ = cache_k.shape
    req_count, lists = request_spans.shape
    picks = sel_rows.shape[1]
    q_rows = question_q.shape[1]
    pool_ids = jnp.arange(span_home.shape[0], dtype=jnp.int32)
    positions = jnp.sum(
        jnp.where(request_spans[:, :, None] == pool_ids, span_home, 0), axis=-1, dtype=jnp.int32
    )
    selected = jnp.sum(
        jnp.where(positions[:, None, :, None] == pool_ids, sel_rows.T[None, :, None, :], 0),
        axis=-1,
        dtype=jnp.int32,
    )
    fresh_limit = jnp.arange(lists, dtype=jnp.int32) * span_len + selected
    fresh_limit = jnp.pad(fresh_limit, ((0, 0), (0, 0), (0, ROW_TILE - lists)), constant_values=-1)
    question_limit = lists * span_len + jnp.arange(q_rows, dtype=jnp.int32)
    limit = jnp.concatenate(
        [
            fresh_limit.reshape(req_count, picks * ROW_TILE),
            jnp.broadcast_to(question_limit, (req_count, q_rows)),
            jnp.full((req_count, LANES - picks * ROW_TILE - q_rows), -1, jnp.int32),
        ],
        axis=1,
    ).reshape(req_count, 1, LANES)
    flat = positions.reshape(-1)
    if count <= RING_MAX:
        slots = ring_slots(flat, spans_dev, count)
        k_pieces, v_pieces = ring_gather(cache_k, cache_v, count)
    else:
        slots, k_pieces, v_pieces = asked_gather(cache_k, cache_v, flat, spans_dev, count)
    turned = [jnp.transpose(a, (0, 2, 1, 3)) for a in (fresh_q, fresh_k, fresh_v)]
    redone, spoken = attend(
        slots, limit, question_len, k_pieces, v_pieces, *turned, question_q, question_k, question_v
    )
    return jnp.transpose(redone, (0, 2, 1, 3)), spoken


def solution(mesh):
    in_specs = (
        P(("groups", "dp"), None, "tp"),
        P(("groups", "dp"), None, "tp"),
        P("groups", None),
        P("groups"),
        P(("groups", "dp"), None),
        P(("groups", "dp"), None, None, "tp"),
        P(("groups", "dp"), None, None, "tp"),
        P(("groups", "dp"), None, None, "tp"),
        P(("groups", "dp"), None, "tp"),
        P(("groups", "dp"), None, "tp"),
        P(("groups", "dp"), None, "tp"),
        P(("groups", "dp")),
    )
    out_specs = (P(("groups", "dp"), None, None, "tp"), P(("groups", "dp"), None, "tp"))
    return jax.shard_map(shards, mesh=mesh, in_specs=in_specs, out_specs=out_specs, check_vma=False)
```

time: 116 us -> 44.9 us (0.39); the launches traced: 114 us -> 44.6 us
  local copies, waits for them, and re-layouts: 36.3 us -> 5.57 us
  matrix products: 23.9 us -> 0 us
  waiting for transfers between devices: 23.3 us -> 8.6 us
  blocking collectives: 13.5 us -> 0 us
  Pallas kernels: 0 us -> 11.9 us
  starting transfers between devices: 7.29 us -> 15.5 us
  other arithmetic: 8.18 us -> 2.27 us
    all_to_all x2 -> x0, waiting for transfers between devices: 23.3 us -> none  [the longest x1 11.8 us: shards(): lax.all_to_all(send_k, 'dp', split_axis=0, concat_axis=0, tiled=True)]
    dot_general x22 -> x0, matrix products: 19 us -> none  [the longest x10 14.6 us: attend(): jnp.einsum('kgnm,mkd->nkgd', weights, v_heads, preferred_element_type=jnp...]
    ppermute x0 -> x14, starting transfers between devices: none -> 15.5 us  [the longest x4 8.45 us: ring_gather(): k_on = lax.ppermute(k_on, 'dp', onward)]
    all_to_all x1 -> x0, blocking collectives: 13.5 us -> none  [shards(): lax.all_to_all(asking, 'dp', split_axis=0, concat_axis=0, tiled=True)]
    dynamic_slice x30 -> x0, local copies, waits for them, and re-layouts: 12.9 us -> none  [shards(): lax.map(one_request, (fresh_q, mine_k, mine_v, selected_req, question_q,...]
    pallas_call x0 -> x2, Pallas kernels: none -> 11.9 us  [the longest x1 6.06 us: attend(): pl.pallas_call(functools.partial(values_kernel, n_buf, lists, span_len),...]
    ppermute x0 -> x14, waiting for transfers between devices: none -> 8.6 us  [the longest x3 3.78 us: ring_gather(): k_back = lax.ppermute(k_back, 'dp', back)]
    all_to_all x2 -> x0, starting transfers between devices: 7.29 us -> none  [the longest x1 3.66 us: shards(): lax.all_to_all(send_v, 'dp', split_axis=0, concat_axis=0, tiled=True)]
  transfers between devices with their start and end apart: 2 -> 14, of which waited for: 2 -> 5; matrix products, arithmetic and copies ran while one was open for 3% -> 6% of each run, Pallas kernels for 0% -> 13%
where the time goes in v1:
time: 44.9 us; the launch traced here: 44.6 us
  starting transfers between devices  15.5 us (35%)
  Pallas kernels  11.9 us (27%)
  waiting for transfers between devices  8.6 us (19%)
  local copies, waits for them, and re-layouts  5.57 us (12%)
  other arithmetic  2.27 us (5%)
  between operations  0.76 us (2%)
    ppermute x4, starting transfers between devices, ring_gather(): k_on = lax.ppermute(k_on, 'dp', onward)  8.45 us
    pallas_call x1, Pallas kernels, attend(): pl.pallas_call(functools.partial(values_kernel, n_buf, lists, span_len),...  6.06 us
    pallas_call x1, Pallas kernels, attend(): pl.pallas_call(functools.partial(weights_kernel, n_buf, lists, span_len),...  5.79 us
    unnamed x18, local copies, waits for them, and re-layouts  5.25 us
    ppermute x3, starting transfers between devices, ring_gather(): v_on = lax.ppermute(v_on, 'dp', onward)  4.22 us
    ppermute x3, waiting for transfers between devices, ring_gather(): k_back = lax.ppermute(k_back, 'dp', back)  3.78 us
    ppermute x4, waiting for transfers between devices, ring_gather(): v_back = lax.ppermute(v_back, 'dp', back)  3.1 us
    ppermute x3, starting transfers between devices, ring_gather(): k_back = lax.ppermute(k_back, 'dp', back)  1.87 us
  transfers between devices with their start and end apart: 14, of which 5 were waited for; matrix products, arithmetic and copies ran while one was open for 6% of the time, Pallas kernels for 13%

profile of v1, /device:TPU:0, one launch (start us, length us, event | category | flops | bytes accessed | tf_op | source)
XLA Modules:
  0.0 44.6 jit_solution(16068307088762140729)
XLA Ops:
  0.6 3.1 %collective-permute-start = (bf16[16,16,256]{2,1,0:T(8,128)(2,1)}, bf16[16,16,256]{2,1,0:T(8,128)(2,1)S(1)}, u32[]{:S(2)}, u32[]{:S(2)}) collective-permute-start(bf16[16,16,256]{2,1,0:T(8,128)(2,1)} %rest_0_.2), channel_id=1, source_target_pairs={{0,4},{4,8},{8,12},{12,14},{14,10},{10,6},{6,2},{2,0},{1,5},{5,9},... | collective-permute-start | bytes 393224 | tf_op jit(solution)/shard_map/ppermute | solution.py:225
  3.7 0.0 collective-permute-start.4
  3.7 2.0 %collective-permute-start.7 = (bf16[16,16,256]{2,1,0:T(8,128)(2,1)}, bf16[16,16,256]{2,1,0:T(8,128)(2,1)S(1)}, u32[]{:S(2)}, u32[]{:S(2)}) collective-permute-start(bf16[16,16,256]{2,1,0:T(8,128)(2,1)} %rest_0_.3), channel_id=1, source_target_pairs={{0,4},{4,8},{8,12},{12,14},{14,10},{10,6},{6,2},{2,0},{1,5},{5,9},... | collective-permute-start | bytes 393224 | tf_op jit(solution)/shard_map/ppermute | solution.py:230
  5.7 0.0 collective-permute-start.10
  5.7 0.9 %select_reduce_fusion.1 = s32[5,12]{1,0:T(8,128)S(1)} fusion(s32[128]{0:T(128)} %param.15, s32[5,12]{1,0:T(8,128)} %param.16), kind=kLoop, calls=%fused_computation.2 | loop fusion | flops 22980 | bytes 992 | tf_op jit(solution)/shard_map/reduce_sum | solution.py:282
  6.7 0.1 iota_compare_fusion
  6.8 0.1 reshape.27
  6.9 0.1 pad.7.clone
  7.0 0.1 pad.6.clone
  7.0 1.2 %select_reduce_fusion = s32[5,5,12]{2,1,0:T(8,128)S(1)} fusion(s32[5,128]{1,0:T(8,128)} %bitcast.8, pred[5,12,128]{2,1,0:T(8,128)(4,1)S(1)} %iota_compare_fusion), kind=kLoop, calls=%fused_computation | loop fusion | flops 76500 | bytes 11440 | tf_op jit(solution)/shard_map/reduce_sum | solution.py:285
  8.2 0.0 collective-permute-done.rest_1_
  8.2 2.1 %collective-permute-start.1 = (bf16[16,16,256]{2,1,0:T(8,128)(2,1)S(1)}, bf16[16,16,256]{2,1,0:T(8,128)(2,1)S(1)}, u32[]{:S(2)}, u32[]{:S(2)}) collective-permute-start(bf16[16,16,256]{2,1,0:T(8,128)(2,1)S(1)} %collective-permute-done.rest_1_), channel_id=1, source_target_pairs={{0,4},{4,8},{8,12},{12,14},{14,10},{10,6},{6,2},{2,0},{1,5},{5,9},... | collective-permute-start | bytes 393224 | tf_op jit(solution)/shard_map/ppermute | solution.py:225
  10.3 1.4 %collective-permute-done.10.rest_7_ = bf16[16,16,256]{2,1,0:T(8,128)(2,1)S(1)} collective-permute-done((bf16[16,16,256]{2,1,0:T(8,128)(2,1)}, bf16[16,16,256]{2,1,0:T(8,128)(2,1)S(1)}, u32[]{:S(2)}, u32[]{:S(2)}) %collective-permute-start.10) | collective-permute-done | bytes 131104 | tf_op jit(solution)/shard_map/ppermute | solution.py:232
  11.7 0.3 collective-permute-start.11
  12.0 0.1 reshape.28
  12.1 0.0 collective-permute-done.4.rest_7_
  12.1 1.6 %collective-permute-start.5 = (bf16[16,16,256]{2,1,0:T(8,128)(2,1)S(1)}, bf16[16,16,256]{2,1,0:T(8,128)(2,1)S(1)}, u32[]{:S(2)}, u32[]{:S(2)}) collective-permute-start(bf16[16,16,256]{2,1,0:T(8,128)(2,1)S(1)} %collective-permute-done.4.rest_7_), channel_id=1, source_target_pairs={{4,0},{8,4},{12,8},{14,12},{10,14},{6,10},{2,6},{0,2},{5,1},{9,5},... | collective-permute-start | bytes 393224 | tf_op jit(solution)/shard_map/ppermute | solution.py:228
  13.7 0.0 collective-permute-done.7.rest_1_
  13.7 0.4 collective-permute-start.8
  14.1 0.0 collective-permute-done.1.rest_2_
  14.1 1.7 %collective-permute-start.2 = (bf16[16,16,256]{2,1,0:T(8,128)(2,1)S(1)}, bf16[16,16,256]{2,1,0:T(8,128)(2,1)S(1)}, u32[]{:S(2)}, u32[]{:S(2)}) collective-permute-start(bf16[16,16,256]{2,1,0:T(8,128)(2,1)S(1)} %collective-permute-done.1.rest_2_), channel_id=1, source_target_pairs={{0,4},{4,8},{8,12},{12,14},{14,10},{10,6},{6,2},{2,0},{1,5},{5,9},... | collective-permute-start | bytes 393224 | tf_op jit(solution)/shard_map/ppermute | solution.py:225
  15.9 1.7 %collective-permute-done.11.rest_6_ = bf16[16,16,256]{2,1,0:T(8,128)(2,1)S(1)} collective-permute-done((bf16[16,16,256]{2,1,0:T(8,128)(2,1)S(1)}, bf16[16,16,256]{2,1,0:T(8,128)(2,1)S(1)}, u32[]{:S(2)}, u32[]{:S(2)}) %collective-permute-start.11) | collective-permute-done | bytes 131104 | tf_op jit(solution)/shard_map/ppermute | solution.py:232
  17.6 0.2 collective-permute-start.12
  17.8 2.6 %collective-permute-done.5.rest_6_ = bf16[16,16,256]{2,1,0:T(8,128)(2,1)S(1)} collective-permute-done((bf16[16,16,256]{2,1,0:T(8,128)(2,1)S(1)}, bf16[16,16,256]{2,1,0:T(8,128)(2,1)S(1)}, u32[]{:S(2)}, u32[]{:S(2)}) %collective-permute-start.5) | collective-permute-done | bytes 131104 | tf_op jit(solution)/shard_map/ppermute | solution.py:228
  20.4 0.2 collective-permute-start.6
  20.6 0.0 collective-permute-done.8.rest_2_
  20.6 1.8 %collective-permute-start.9 = (bf16[16,16,256]{2,1,0:T(8,128)(2,1)S(1)}, bf16[16,16,256]{2,1,0:T(8,128)(2,1)S(1)}, u32[]{:S(2)}, u32[]{:S(2)}) collective-permute-start(bf16[16,16,256]{2,1,0:T(8,128)(2,1)S(1)} %collective-permute-done.8.rest_2_), channel_id=1, source_target_pairs={{0,4},{4,8},{8,12},{12,14},{14,10},{10,6},{6,2},{2,0},{1,5},{5,9},... | collective-permute-start | bytes 393224 | tf_op jit(solution)/shard_map/ppermute | solution.py:230
  22.4 0.0 collective-permute-done.2.rest_3_
  22.4 1.6 %collective-permute-start.3 = (bf16[16,16,256]{2,1,0:T(8,128)(2,1)S(1)}, bf16[16,16,256]{2,1,0:T(8,128)(2,1)S(1)}, u32[]{:S(2)}, u32[]{:S(2)}) collective-permute-start(bf16[16,16,256]{2,1,0:T(8,128)(2,1)S(1)} %collective-permute-done.2.rest_3_), channel_id=1, source_target_pairs={{0,4},{4,8},{8,12},{12,14},{14,10},{10,6},{6,2},{2,0},{1,5},{5,9},... | collective-permute-start | bytes 393224 | tf_op jit(solution)/shard_map/ppermute | solution.py:225
  24.0 0.0 collective-permute-done.12.rest_5_
  24.0 0.4 %collective-permute-start.13 = (bf16[16,16,256]{2,1,0:T(8,128)(2,1)S(1)}, bf16[16,16,256]{2,1,0:T(8,128)(2,1)S(1)}, u32[]{:S(2)}, u32[]{:S(2)}) collective-permute-start(bf16[16,16,256]{2,1,0:T(8,128)(2,1)S(1)} %collective-permute-done.12.rest_5_), channel_id=1, source_target_pairs={{4,0},{8,4},{12,8},{14,12},{10,14},{6,10},{2,6},{0,2},{5,1},{9,5},... | collective-permute-start | bytes 393224 | tf_op jit(solution)/shard_map/ppermute | solution.py:232
  24.5 1.2 %collective-permute-done.6.rest_5_ = bf16[16,16,256]{2,1,0:T(8,128)(2,1)S(1)} collective-permute-done((bf16[16,16,256]{2,1,0:T(8,128)(2,1)S(1)}, bf16[16,16,256]{2,1,0:T(8,128)(2,1)S(1)}, u32[]{:S(2)}, u32[]{:S(2)}) %collective-permute-start.6) | collective-permute-done | bytes 131104 | tf_op jit(solution)/shard_map/ppermute | solution.py:228
  25.7 1.7 %collective-permute-done.3.rest_4_ = bf16[16,16,256]{2,1,0:T(8,128)(2,1)S(1)} collective-permute-done((bf16[16,16,256]{2,1,0:T(8,128)(2,1)S(1)}, bf16[16,16,256]{2,1,0:T(8,128)(2,1)S(1)}, u32[]{:S(2)}, u32[]{:S(2)}) %collective-permute-start.3) | collective-permute-done | bytes 131104 | tf_op jit(solution)/shard_map/ppermute | solution.py:225
  27.4 0.0 copy-start
  27.4 1.4 %copy-done = bf16[5,12,5,2048]{3,1,2,0:T(8,128)(2,1)S(1)} copy-done((bf16[5,12,5,2048]{3,1,2,0:T(8,128)(2,1)S(1)}, bf16[5,12,5,2048]{3,1,2,0:T(8,128)(2,1)}, u32[]{:S(2)}) %copy-start) | copy-done | bytes 1228824
  28.8 0.0 copy-start.1
  28.8 1.1 %copy-done.1 = bf16[5,32,2048]{2,1,0:T(8,128)(2,1)S(1)} copy-done((bf16[5,32,2048]{2,1,0:T(8,128)(2,1)S(1)}, bf16[5,32,2048]{2,1,0:T(8,128)(2,1)}, u32[]{:S(2)}) %copy-start.1) | copy-done | bytes 655384
  29.9 0.9 %copy-done.2 = bf16[5,12,5,256]{3,1,2,0:T(8,128)(2,1)S(1)} copy-done((bf16[5,12,5,256]{3,1,2,0:T(8,128)(2,1)S(1)}, bf16[5,12,5,256]{3,1,2,0:T(8,128)(2,1)}, u32[]{:S(2)}) %copy-start.2) | copy-done | bytes 153624
  30.8 0.9 %copy-done.4 = bf16[16,16,256]{2,1,0:T(8,128)(2,1)S(1)} copy-done((bf16[16,16,256]{2,1,0:T(8,128)(2,1)S(1)}, bf16[16,16,256]{2,1,0:T(8,128)(2,1)}, u32[]{:S(2)}) %copy-start.4) | copy-done | bytes 131096
  31.8 0.9 %copy-done.6 = bf16[5,32,256]{2,1,0:T(8,128)(2,1)S(1)} copy-done((bf16[5,32,256]{2,1,0:T(8,128)(2,1)S(1)}, bf16[5,32,256]{2,1,0:T(8,128)(2,1)}, u32[]{:S(2)}) %copy-start.6) | copy-done | bytes 81944
  32.6 5.8 %span_weights.1.w_ref = bf16[5,2,896,256]{3,2,1,0:T(8,128)(2,1)S(1)} custom-call(s32[60]{0:T(128)S(1)} %fusion.slot_ref, s32[5,1,128]{2,1,0:T(1,128)S(1)} %reshape.29.limit_ref, bf16[5,5,12,2048]{3,2,1,0:T(8,128)(2,1)S(1)} %bitcast.5, bf16[5,32,2048]{2,1,0:T(8,128)(2,1)S(1)} %copy-done.1, bf16[5,5,12,256]{3,2,1,0:T(8,128)(2,1)S(1)} %bitcast.6, ...), custom_call_target="tpu_custom_call" | custom-call | flops 1174405120 | bytes 8388608 | tf_op jit(solution)/shard_map/span_weights/pallas_call | solution.py:171
  38.4 0.0 collective-permute-done.9.rest_3_
  38.5 0.0 collective-permute-done.13.rest_4_
  38.5 0.0 copy-done.3
  38.5 0.0 copy-done.5
  38.5 0.0 copy-done.7
  38.5 0.0 copy-done.8
  38.5 6.1 %span_values.1 = (bf16[5,5,12,2048]{3,2,1,0:T(8,128)(2,1)}, bf16[5,32,2048]{2,1,0:T(8,128)(2,1)}) custom-call(s32[60]{0:T(128)S(1)} %fusion.slot_ref, s32[5]{0:T(128)S(1)} %copy-done.8, s32[5,1,128]{2,1,0:T(1,128)S(1)} %reshape.29.limit_ref, bf16[5,2,896,256]{3,2,1,0:T(8,128)(2,1)S(1)} %span_weights.1.w_ref, bf16[5,5,12,256]{3,2,1,0:T(8,128)(2,1)S(1)} %bitcast.7, ...), custom_call_target="tpu_custom_call" | custom-call | flops 1174405120 | bytes 8388608 | tf_op jit(solution)/shard_map/span_values/pallas_call | solution.py:196
  (15 shorter events, 0.1 us)
Async XLA Ops:
  0.6 7.6 %collective-permute-start = (bf16[16,16,256]{2,1,0:T(8,128)(2,1)}, bf16[16,16,256]{2,1,0:T(8,128)(2,1)S(1)}, u32[]{:S(2)}, u32[]{:S(2)}) collective-permute-start(bf16[16,16,256]{2,1,0:T(8,128)(2,1)} %rest_0_.2), channel_id=1, source_target_pairs={{0,4},{4,8},{8,12},{12,14},{14,10},{10,6},{6,2},{2,0},{1,5},{5,9},... | collective-permute-start | bytes 393224 | tf_op jit(solution)/shard_map/ppermute | solution.py:225
  3.7 8.4 %collective-permute-start.4 = (bf16[16,16,256]{2,1,0:T(8,128)(2,1)}, bf16[16,16,256]{2,1,0:T(8,128)(2,1)S(1)}, u32[]{:S(2)}, u32[]{:S(2)}) collective-permute-start(bf16[16,16,256]{2,1,0:T(8,128)(2,1)} %rest_0_.2), channel_id=1, source_target_pairs={{4,0},{8,4},{12,8},{14,12},{10,14},{6,10},{2,6},{0,2},{5,1},{9,5},... | collective-permute-start | bytes 393224 | tf_op jit(solution)/shard_map/ppermute | solution.py:228
  3.7 10.0 %collective-permute-start.7 = (bf16[16,16,256]{2,1,0:T(8,128)(2,1)}, bf16[16,16,256]{2,1,0:T(8,128)(2,1)S(1)}, u32[]{:S(2)}, u32[]{:S(2)}) collective-permute-start(bf16[16,16,256]{2,1,0:T(8,128)(2,1)} %rest_0_.3), channel_id=1, source_target_pairs={{0,4},{4,8},{8,12},{12,14},{14,10},{10,6},{6,2},{2,0},{1,5},{5,9},... | collective-permute-start | bytes 393224 | tf_op jit(solution)/shard_map/ppermute | solution.py:230
  5.7 6.0 %collective-permute-start.10 = (bf16[16,16,256]{2,1,0:T(8,128)(2,1)}, bf16[16,16,256]{2,1,0:T(8,128)(2,1)S(1)}, u32[]{:S(2)}, u32[]{:S(2)}) collective-permute-start(bf16[16,16,256]{2,1,0:T(8,128)(2,1)} %rest_0_.3), channel_id=1, source_target_pairs={{4,0},{8,4},{12,8},{14,12},{10,14},{6,10},{2,6},{0,2},{5,1},{9,5},... | collective-permute-start | bytes 393224 | tf_op jit(solution)/shard_map/ppermute | solution.py:232
  8.2 5.9 %collective-permute-start.1 = (bf16[16,16,256]{2,1,0:T(8,128)(2,1)S(1)}, bf16[16,16,256]{2,1,0:T(8,128)(2,1)S(1)}, u32[]{:S(2)}, u32[]{:S(2)}) collective-permute-start(bf16[16,16,256]{2,1,0:T(8,128)(2,1)S(1)} %collective-permute-done.rest_1_), channel_id=1, source_target_pairs={{0,4},{4,8},{8,12},{12,14},{14,10},{10,6},{6,2},{2,0},{1,5},{5,9},... | collective-permute-start | bytes 393224 | tf_op jit(solution)/shard_map/ppermute | solution.py:225
  11.7 5.9 %collective-permute-start.11 = (bf16[16,16,256]{2,1,0:T(8,128)(2,1)S(1)}, bf16[16,16,256]{2,1,0:T(8,128)(2,1)S(1)}, u32[]{:S(2)}, u32[]{:S(2)}) collective-permute-start(bf16[16,16,256]{2,1,0:T(8,128)(2,1)S(1)} %collective-permute-done.10.rest_7_), channel_id=1, source_target_pairs={{4,0},{8,4},{12,8},{14,12},{10,14},{6,10},{2,6},{0,2},{5,1},{9,5},... | collective-permute-start | bytes 393224 | tf_op jit(solution)/shard_map/ppermute | solution.py:232
  12.1 8.3 %collective-permute-start.5 = (bf16[16,16,256]{2,1,0:T(8,128)(2,1)S(1)}, bf16[16,16,256]{2,1,0:T(8,128)(2,1)S(1)}, u32[]{:S(2)}, u32[]{:S(2)}) collective-permute-start(bf16[16,16,256]{2,1,0:T(8,128)(2,1)S(1)} %collective-permute-done.4.rest_7_), channel_id=1, source_target_pairs={{4,0},{8,4},{12,8},{14,12},{10,14},{6,10},{2,6},{0,2},{5,1},{9,5},... | collective-permute-start | bytes 393224 | tf_op jit(solution)/shard_map/ppermute | solution.py:228
  13.7 6.9 %collective-permute-start.8 = (bf16[16,16,256]{2,1,0:T(8,128)(2,1)S(1)}, bf16[16,16,256]{2,1,0:T(8,128)(2,1)S(1)}, u32[]{:S(2)}, u32[]{:S(2)}) collective-permute-start(bf16[16,16,256]{2,1,0:T(8,128)(2,1)S(1)} %collective-permute-done.7.rest_1_), channel_id=1, source_target_pairs={{0,4},{4,8},{8,12},{12,14},{14,10},{10,6},{6,2},{2,0},{1,5},{5,9},... | collective-permute-start | bytes 393224 | tf_op jit(solution)/shard_map/ppermute | solution.py:230
  14.1 8.3 %collective-permute-start.2 = (bf16[16,16,256]{2,1,0:T(8,128)(2,1)S(1)}, bf16[16,16,256]{2,1,0:T(8,128)(2,1)S(1)}, u32[]{:S(2)}, u32[]{:S(2)}) collective-permute-start(bf16[16,16,256]{2,1,0:T(8,128)(2,1)S(1)} %collective-permute-done.1.rest_2_), channel_id=1, source_target_pairs={{0,4},{4,8},{8,12},{12,14},{14,10},{10,6},{6,2},{2,0},{1,5},{5,9},... | collective-permute-start | bytes 393224 | tf_op jit(solution)/shard_map/ppermute | solution.py:225
  17.6 6.4 %collective-permute-start.12 = (bf16[16,16,256]{2,1,0:T(8,128)(2,1)S(1)}, bf16[16,16,256]{2,1,0:T(8,128)(2,1)S(1)}, u32[]{:S(2)}, u32[]{:S(2)}) collective-permute-start(bf16[16,16,256]{2,1,0:T(8,128)(2,1)S(1)} %collective-permute-done.11.rest_6_), channel_id=1, source_target_pairs={{4,0},{8,4},{12,8},{14,12},{10,14},{6,10},{2,6},{0,2},{5,1},{9,5},... | collective-permute-start | bytes 393224 | tf_op jit(solution)/shard_map/ppermute | solution.py:232
  20.4 5.3 %collective-permute-start.6 = (bf16[16,16,256]{2,1,0:T(8,128)(2,1)S(1)}, bf16[16,16,256]{2,1,0:T(8,128)(2,1)S(1)}, u32[]{:S(2)}, u32[]{:S(2)}) collective-permute-start(bf16[16,16,256]{2,1,0:T(8,128)(2,1)S(1)} %collective-permute-done.5.rest_6_), channel_id=1, source_target_pairs={{4,0},{8,4},{12,8},{14,12},{10,14},{6,10},{2,6},{0,2},{5,1},{9,5},... | collective-permute-start | bytes 393224 | tf_op jit(solution)/shard_map/ppermute | solution.py:228
  20.6 17.8 %collective-permute-start.9 = (bf16[16,16,256]{2,1,0:T(8,128)(2,1)S(1)}, bf16[16,16,256]{2,1,0:T(8,128)(2,1)S(1)}, u32[]{:S(2)}, u32[]{:S(2)}) collective-permute-start(bf16[16,16,256]{2,1,0:T(8,128)(2,1)S(1)} %collective-permute-done.8.rest_2_), channel_id=1, source_target_pairs={{0,4},{4,8},{8,12},{12,14},{14,10},{10,6},{6,2},{2,0},{1,5},{5,9},... | collective-permute-start | bytes 393224 | tf_op jit(solution)/shard_map/ppermute | solution.py:230
  22.4 5.0 %collective-permute-start.3 = (bf16[16,16,256]{2,1,0:T(8,128)(2,1)S(1)}, bf16[16,16,256]{2,1,0:T(8,128)(2,1)S(1)}, u32[]{:S(2)}, u32[]{:S(2)}) collective-permute-start(bf16[16,16,256]{2,1,0:T(8,128)(2,1)S(1)} %collective-permute-done.2.rest_3_), channel_id=1, source_target_pairs={{0,4},{4,8},{8,12},{12,14},{14,10},{10,6},{6,2},{2,0},{1,5},{5,9},... | collective-permute-start | bytes 393224 | tf_op jit(solution)/shard_map/ppermute | solution.py:225
  24.0 14.5 %collective-permute-start.13 = (bf16[16,16,256]{2,1,0:T(8,128)(2,1)S(1)}, bf16[16,16,256]{2,1,0:T(8,128)(2,1)S(1)}, u32[]{:S(2)}, u32[]{:S(2)}) collective-permute-start(bf16[16,16,256]{2,1,0:T(8,128)(2,1)S(1)} %collective-permute-done.12.rest_5_), channel_id=1, source_target_pairs={{4,0},{8,4},{12,8},{14,12},{10,14},{6,10},{2,6},{0,2},{5,1},{9,5},... | collective-permute-start | bytes 393224 | tf_op jit(solution)/shard_map/ppermute | solution.py:232
  27.4 1.4 %copy-start = (bf16[5,12,5,2048]{3,1,2,0:T(8,128)(2,1)S(1)}, bf16[5,12,5,2048]{3,1,2,0:T(8,128)(2,1)}, u32[]{:S(2)}) copy-start(bf16[5,12,5,2048]{3,1,2,0:T(8,128)(2,1)} %param.17) | copy-start | bytes 3686404
  28.8 1.1 %copy-start.1 = (bf16[5,32,2048]{2,1,0:T(8,128)(2,1)S(1)}, bf16[5,32,2048]{2,1,0:T(8,128)(2,1)}, u32[]{:S(2)}) copy-start(bf16[5,32,2048]{2,1,0:T(8,128)(2,1)} %qq_ref.1) | copy-start | bytes 1966084
  29.9 0.9 %copy-start.2 = (bf16[5,12,5,256]{3,1,2,0:T(8,128)(2,1)S(1)}, bf16[5,12,5,256]{3,1,2,0:T(8,128)(2,1)}, u32[]{:S(2)}) copy-start(bf16[5,12,5,256]{3,1,2,0:T(8,128)(2,1)} %param.18) | copy-start | bytes 460804
  30.8 0.9 %copy-start.4 = (bf16[16,16,256]{2,1,0:T(8,128)(2,1)S(1)}, bf16[16,16,256]{2,1,0:T(8,128)(2,1)}, u32[]{:S(2)}) copy-start(bf16[16,16,256]{2,1,0:T(8,128)(2,1)} %rest_0_.2) | copy-start | bytes 393220
  31.8 0.9 %copy-start.6 = (bf16[5,32,256]{2,1,0:T(8,128)(2,1)S(1)}, bf16[5,32,256]{2,1,0:T(8,128)(2,1)}, u32[]{:S(2)}) copy-start(bf16[5,32,256]{2,1,0:T(8,128)(2,1)} %qk_ref.1) | copy-start | bytes 245764
  32.6 5.8 %copy-start.3 = (bf16[5,12,5,256]{3,1,2,0:T(8,128)(2,1)S(1)}, bf16[5,12,5,256]{3,1,2,0:T(8,128)(2,1)}, u32[]{:S(2)}) copy-start(bf16[5,12,5,256]{3,1,2,0:T(8,128)(2,1)} %param.19) | copy-start | bytes 460804
  32.6 5.8 %copy-start.5 = (bf16[16,16,256]{2,1,0:T(8,128)(2,1)S(1)}, bf16[16,16,256]{2,1,0:T(8,128)(2,1)}, u32[]{:S(2)}) copy-start(bf16[16,16,256]{2,1,0:T(8,128)(2,1)} %rest_0_.3) | copy-start | bytes 393220
  32.6 5.9 %copy-start.7 = (bf16[5,32,256]{2,1,0:T(8,128)(2,1)S(1)}, bf16[5,32,256]{2,1,0:T(8,128)(2,1)}, u32[]{:S(2)}) copy-start(bf16[5,32,256]{2,1,0:T(8,128)(2,1)} %qv_ref.1) | copy-start | bytes 245764
  32.6 5.9 %copy-start.8 = (s32[5]{0:T(128)S(1)}, s32[5]{0:T(128)}, u32[]{:S(2)}) copy-start(s32[5]{0:T(128)} %length_ref.1) | copy-start | bytes 64

commit v2 on v1

v2 whole, which is shorter than its diff:
```python
import functools

import jax
import jax.numpy as jnp
from jax import lax
from jax.experimental import pallas as pl
from jax.experimental.pallas import tpu as pltpu
from jax.sharding import PartitionSpec as P

HEAD = 128
LANES = 128
ROW_TILE = 16
MASKED = -1e30
RING_MAX = 16
VMEM_LIMIT = 40 * 1024 * 1024


def clear(*refs):
    for ref in refs:
        ref[...] = jnp.zeros_like(ref)


def fill_pool(pieces, pool):
    rows = pieces[0].shape[0]
    for b, piece in enumerate(pieces):
        pool[b * rows : (b + 1) * rows] = piece[...]


def blend(limit, slots, pool, lists, fresh, question, base, fresh_rows):
    span_len = pool.shape[1]
    picks = fresh.shape[0]
    for j in range(lists):
        base[j * span_len : (j + 1) * span_len, :] = pool[slots(j)]
    fresh_rows[0:picks, 0:lists, :] = fresh
    q_tiles = question.shape[0] // ROW_TILE
    fresh_rows[picks : picks + q_tiles] = question.reshape(q_tiles, ROW_TILE, -1)
    key = lax.broadcasted_iota(jnp.int32, (base.shape[0], LANES), 0)
    here = jnp.where(key == limit, 1.0, 0.0)
    placed = jnp.dot(
        here.astype(jnp.bfloat16),
        fresh_rows[...].reshape(LANES, -1),
        preferred_element_type=jnp.float32,
    )
    replaced = jnp.max(here, axis=1, keepdims=True) > 0.5
    return jnp.where(replaced, placed, base[...].astype(jnp.float32)).astype(jnp.bfloat16)


def weights_kernel(n_buf, slot_ref, limit_ref, fq_hbm, qq_hbm, fk_hbm, qk_hbm, *rest):
    pieces = rest[:n_buf]
    out_ref, fq, qq, fk, qk, pool, base, fresh_rows, queries, sems = rest[n_buf:]
    req_count, picks, lists, _ = fq.shape
    kv_heads, heads = out_ref.shape[1], queries.shape[1]
    rows_head = queries.shape[2] * ROW_TILE
    small = [
        pltpu.make_async_copy(fk_hbm, fk, sems.at[0]),
        pltpu.make_async_copy(qk_hbm, qk, sems.at[1]),
    ]
    for copy in small:
        copy.start()

    def request_copies(r):
        return [
            pltpu.make_async_copy(fq_hbm.at[r], fq.at[r], sems.at[2 + 2 * r]),
            pltpu.make_async_copy(qq_hbm.at[r], qq.at[r], sems.at[3 + 2 * r]),
        ]

    for r in range(req_count):
        for copy in request_copies(r):
            copy.start()
    clear(base, fresh_rows, queries)
    row = lax.broadcasted_iota(jnp.int32, (rows_head, LANES), 0)
    column = lax.broadcasted_iota(jnp.int32, (rows_head, LANES), 1)
    unit = jnp.where(row == column, 1.0, 0.0).astype(jnp.bfloat16)
    for g in range(kv_heads):
        for h in range(heads):
            queries[g, h, :, :, HEAD:] = unit.reshape(-1, ROW_TILE, LANES)
    fill_pool(pieces, pool)
    for copy in small:
        copy.wait()
    scale = 1.4426950408889634 / float(HEAD) ** 0.5

    def request(r):
        for copy in request_copies(r):
            copy.wait()
        limit = limit_ref[r]
        keys = blend(
            limit, lambda j: slot_ref[r * lists + j], pool, lists, fk[r], qk[r], base, fresh_rows
        )
        key = lax.broadcasted_iota(jnp.int32, (keys.shape[0], LANES), 0)
        bias = jnp.where(key <= limit, 0.0, MASKED).astype(jnp.bfloat16)
        for g in range(kv_heads):
            for h in range(heads):
                at = (g * heads + h) * HEAD
                queries[g, h, 0:picks, 0:lists, 0:HEAD] = fq[r, :, :, at : at + HEAD]
                queries[g, h, picks:, :, 0:HEAD] = qq[r, :, at : at + HEAD].reshape(-1, ROW_TILE, HEAD)
            table = jnp.concatenate([keys[:, g * HEAD : (g + 1) * HEAD], bias], axis=1)
            scores = lax.dot_general(
                queries[g].reshape(heads * rows_head, 2 * HEAD),
                table,
                (((1,), (1,)), ((), ())),
                preferred_element_type=jnp.float32,
            )
            top = jnp.max(scores, axis=1, keepdims=True)
            out_ref[r, g] = jnp.exp2((scores - top) * scale).astype(jnp.bfloat16)

    for r in range(req_count):
        request(r)


def values_kernel(n_buf, slot_ref, length_ref, limit_ref, w_ref, fv_hbm, qv_hbm, *rest):
    pieces = rest[:n_buf]
    redone_hbm, spoken_hbm, fv, qv, redone, spoken, pool, base, fresh_rows, sems, out_sems = rest[n_buf:]
    req_count, picks, lists, _ = redone.shape
    kv_heads = w_ref.shape[1]
    q_rows = spoken.shape[1]
    heads = spoken.shape[2] // HEAD // kv_heads
    rows_head = picks * ROW_TILE + q_rows
    small = [
        pltpu.make_async_copy(fv_hbm, fv, sems.at[0]),
        pltpu.make_async_copy(qv_hbm, qv, sems.at[1]),
    ]
    for copy in small:
        copy.start()
    clear(base, fresh_rows)
    fill_pool(pieces, pool)
    for copy in small:
        copy.wait()

    def out_copies(r):
        return [
            pltpu.make_async_copy(redone.at[r], redone_hbm.at[r], out_sems.at[2 * r]),
            pltpu.make_async_copy(spoken.at[r], spoken_hbm.at[r], out_sems.at[2 * r + 1]),
        ]

    def request(r):
        values = blend(
            limit_ref[r],
            lambda j: slot_ref[r * lists + j],
            pool,
            lists,
            fv[r],
            qv[r],
            base,
            fresh_rows,
        )
        ones = jnp.ones((values.shape[0], LANES), jnp.bfloat16)
        live = lax.broadcasted_iota(jnp.int32, (q_rows, HEAD), 0) < length_ref[r]
        for g in range(kv_heads):
            table = jnp.concatenate([values[:, g * HEAD : (g + 1) * HEAD], ones], axis=1)
            both = jnp.dot(w_ref[r, g], table, preferred_element_type=jnp.float32)
            result = both[:, :HEAD] / both[:, HEAD:]
            for h in range(heads):
                at = (g * heads + h) * HEAD
                row = h * rows_head
                fresh = result[row : row + picks * ROW_TILE].astype(jnp.bfloat16)
                redone[r, :, :, at : at + HEAD] = fresh.reshape(picks, ROW_TILE, HEAD)[:, :lists, :]
                asked = result[row + picks * ROW_TILE : row + rows_head]
                spoken[r, :, at : at + HEAD] = jnp.where(live, asked, 0.0).astype(jnp.bfloat16)
        for copy in out_copies(r):
            copy.start()

    for r in range(req_count):
        request(r)
    for r in range(req_count):
        for copy in out_copies(r):
            copy.wait()


def attend(slots, limit, lengths, k_pieces, v_pieces, fresh_q, fresh_k, fresh_v, question_q, question_k, question_v):
    req_count, picks, lists, q_width = fresh_q.shape
    piece_rows, span_len, width = k_pieces[0].shape
    n_buf = len(k_pieces)
    q_rows = question_q.shape[1]
    kv_heads = width // HEAD
    heads = q_width // width
    rows_head = picks * ROW_TILE + q_rows
    padded = -(-(lists * span_len + q_rows) // LANES) * LANES

    smem = pl.BlockSpec(memory_space=pltpu.SMEM)
    vmem = pl.BlockSpec(memory_space=pltpu.VMEM)
    hbm = pl.BlockSpec(memory_space=pltpu.HBM)

    def in_vmem(x):
        return pltpu.with_memory_space_constraint(x, pltpu.VMEM)

    def in_hbm(x):
        return pltpu.with_memory_space_constraint(x, pltpu.HBM)

    def like(x):
        return pltpu.VMEM(x.shape, x.dtype)

    shared = [
        pltpu.VMEM((n_buf * piece_rows, span_len, width), jnp.bfloat16),
        pltpu.VMEM((padded, width), jnp.bfloat16),
        pltpu.VMEM((LANES // ROW_TILE, ROW_TILE, width), jnp.bfloat16),
    ]
    params = pltpu.CompilerParams(vmem_limit_bytes=VMEM_LIMIT)
    flops = 2 * req_count * kv_heads * heads * rows_head * padded * 2 * HEAD
    w_shape = (req_count, kv_heads, heads * rows_head, padded)
    weights = pl.pallas_call(
        functools.partial(weights_kernel, n_buf),
        in_specs=[smem, vmem] + [hbm] * 4 + [vmem] * n_buf,
        out_specs=vmem,
        scratch_shapes=[like(fresh_q), like(question_q), like(fresh_k), like(question_k)]
        + shared
        + [
            pltpu.VMEM((kv_heads, heads, rows_head // ROW_TILE, ROW_TILE, 2 * HEAD), jnp.bfloat16),
            pltpu.SemaphoreType.DMA((2 + 2 * req_count,)),
        ],
        out_shape=pltpu.VMEM(w_shape, jnp.bfloat16),
        compiler_params=params,
        cost_estimate=pl.CostEstimate(flops=flops, bytes_accessed=8 << 20, transcendentals=flops // 512),
        name="span_weights",
    )(slots, limit, *map(in_hbm, (fresh_q, question_q, fresh_k, question_k)), *map(in_vmem, k_pieces))
    return pl.pallas_call(
        functools.partial(values_kernel, n_buf),
        in_specs=[smem, smem, vmem, vmem] + [hbm] * 2 + [vmem] * n_buf,
        out_specs=[hbm, hbm],
        scratch_shapes=[like(fresh_v), like(question_v), like(fresh_q), like(question_q)]
        + shared
        + [pltpu.SemaphoreType.DMA((2,)), pltpu.SemaphoreType.DMA((2 * req_count,))],
        out_shape=[
            jax.ShapeDtypeStruct(fresh_q.shape, jnp.bfloat16),
            jax.ShapeDtypeStruct(question_q.shape, jnp.bfloat16),
        ],
        compiler_params=params,
        cost_estimate=pl.CostEstimate(flops=flops, bytes_accessed=8 << 20, transcendentals=0),
        name="span_values",
    )(slots, lengths, limit, in_vmem(weights), *map(in_hbm, (fresh_v, question_v)), *map(in_vmem, v_pieces))


def ring_gather(keys, values, count):
    order = list(range(0, count, 2)) + list(range(1, count, 2))[::-1]
    onward = [(order[i], order[(i + 1) % count]) for i in range(count)]
    back = [(b, a) for a, b in onward]
    k_at, v_at = {0: keys}, {0: values}
    k_on = k_back = keys
    v_on = v_back = values
    half, rest = count // 2, (count - 1) // 2
    for hop in range(1, half + 1):
        k_on = lax.ppermute(k_on, "dp", onward)
        k_at[hop] = k_on
        if hop <= rest:
            k_back = lax.ppermute(k_back, "dp", back)
            k_at[count - hop] = k_back
            v_on = lax.ppermute(v_on, "dp", onward)
            v_at[hop] = v_on
        v_back = lax.ppermute(v_back, "dp", back)
        v_at[count - hop] = v_back
    return [k_at[d] for d in range(count)], [v_at[d] for d in range(count)]


def ring_slots(positions, spans_dev, count):
    def place(index):
        return jnp.where(index % 2 == 0, index // 2, count - 1 - index // 2)

    upstream = (place(lax.axis_index("dp")) - place(positions // spans_dev)) % count
    return upstream * spans_dev + positions % spans_dev


def asked_gather(keys, values, positions, spans_dev, count):
    slot_count = positions.shape[0]
    capacity = (slot_count + count - 1) // count
    owner = positions // spans_dev
    local = positions % spans_dev
    ids = jnp.arange(slot_count, dtype=jnp.int32)
    earlier = (owner[:, None] == owner[None, :]) & (ids[None, :] < ids[:, None])
    slots = owner * capacity + jnp.sum(earlier.astype(jnp.int32), axis=1)
    asking = jnp.full((count * capacity,), -1, jnp.int32).at[slots].set(local)
    wanted = jnp.maximum(lax.all_to_all(asking, "dp", split_axis=0, concat_axis=0, tiled=True), 0)
    pieces = [
        [lax.all_to_all(cache[wanted], "dp", split_axis=0, concat_axis=0, tiled=True)]
        for cache in (keys, values)
    ]
    return slots, pieces[0], pieces[1]


def shards(
    cache_k,
    cache_v,
    sel_rows,
    span_home,
    request_spans,
    fresh_q,
    fresh_k,
    fresh_v,
    question_q,
    question_k,
    question_v,
    question_len,
):
    count = lax.axis_size("dp")
    spans_dev, span_len, _ = cache_k.shape
    req_count, lists = request_spans.shape
    picks = sel_rows.shape[1]
    q_rows = question_q.shape[1]
    pool_ids = jnp.arange(span_home.shape[0], dtype=jnp.int32)
    positions = jnp.sum(
        jnp.where(request_spans[:, :, None] == pool_ids, span_home, 0), axis=-1, dtype=jnp.int32
    )
    selected = jnp.sum(
        jnp.where(positions[:, None, :, None] == pool_ids, sel_rows.T[None, :, None, :], 0),
        axis=-1,
        dtype=jnp.int32,
    )
    fresh_limit = jnp.arange(lists, dtype=jnp.int32) * span_len + selected
    fresh_limit = jnp.pad(fresh_limit, ((0, 0), (0, 0), (0, ROW_TILE - lists)), constant_values=-1)
    question_limit = lists * span_len + jnp.arange(q_rows, dtype=jnp.int32)
    limit = jnp.concatenate(
        [
            fresh_limit.reshape(req_count, picks * ROW_TILE),
            jnp.broadcast_to(question_limit, (req_count, q_rows)),
            jnp.full((req_count, LANES - picks * ROW_TILE - q_rows), -1, jnp.int32),
        ],
        axis=1,
    ).reshape(req_count, 1, LANES)
    flat = positions.reshape(-1)
    if count <= RING_MAX:
        slots = ring_slots(flat, spans_dev, count)
        k_pieces, v_pieces = ring_gather(cache_k, cache_v, count)
    else:
        slots, k_pieces, v_pieces = asked_gather(cache_k, cache_v, flat, spans_dev, count)
    turned = [jnp.transpose(a, (0, 2, 1, 3)) for a in (fresh_q, fresh_k, fresh_v)]
    redone, spoken = attend(
        slots, limit, question_len, k_pieces, v_pieces, *turned, question_q, question_k, question_v
    )
    return jnp.transpose(redone, (0, 2, 1, 3)), spoken


def solution(mesh):
    in_specs = (
        P(("groups", "dp"), None, "tp"),
        P(("groups", "dp"), None, "tp"),
        P("groups", None),
        P("groups"),
        P(("groups", "dp"), None),
        P(("groups", "dp"), None, None, "tp"),
        P(("groups", "dp"), None, None, "tp"),
        P(("groups", "dp"), None, None, "tp"),
        P(("groups", "dp"), None, "tp"),
        P(("groups", "dp"), None, "tp"),
        P(("groups", "dp"), None, "tp"),
        P(("groups", "dp")),
    )
    out_specs = (P(("groups", "dp"), None, None, "tp"), P(("groups", "dp"), None, "tp"))
    return jax.shard_map(shards, mesh=mesh, in_specs=in_specs, out_specs=out_specs, check_vma=False)
```

time: 44.9 us -> 38.6 us (0.86)
  local copies, waits for them, and re-layouts: 5.57 us -> 1.23 us
  Pallas kernels: 11.9 us -> 10 us
    unnamed x18 -> x6, local copies, waits for them, and re-layouts: 5.25 us -> 0.91 us
    pallas_call x2, Pallas kernels: 11.9 us -> 10 us  [the longest x1 5.33 us: attend(): pl.pallas_call(functools.partial(weights_kernel, n_buf), in_specs=[smem,...]
  transfers between devices with their start and end apart: 14 -> 14, of which waited for: 5 -> 5; matrix products, arithmetic and copies ran while one was open for 6% -> 7% of each run, Pallas kernels for 13% -> 14%
where the time goes in v2:
time: 38.6 us; the launch traced here: 38.4 us
  starting transfers between devices  15.5 us (40%)
  Pallas kernels  10 us (26%)
  waiting for transfers between devices  8.6 us (22%)
  other arithmetic  2.27 us (6%)
  local copies, waits for them, and re-layouts  1.23 us (3%)
  between operations  0.74 us (2%)
    ppermute x4, starting transfers between devices, ring_gather(): k_on = lax.ppermute(k_on, 'dp', onward)  8.45 us
    pallas_call x1, Pallas kernels, attend(): pl.pallas_call(functools.partial(weights_kernel, n_buf), in_specs=[smem,...  5.33 us
    pallas_call x1, Pallas kernels, attend(): pl.pallas_call(functools.partial(values_kernel, n_buf), in_specs=[smem, s...  4.69 us
    ppermute x3, starting transfers between devices, ring_gather(): v_on = lax.ppermute(v_on, 'dp', onward)  4.22 us
    ppermute x3, waiting for transfers between devices, ring_gather(): k_back = lax.ppermute(k_back, 'dp', back)  3.78 us
    ppermute x4, waiting for transfers between devices, ring_gather(): v_back = lax.ppermute(v_back, 'dp', back)  3.1 us
    ppermute x3, starting transfers between devices, ring_gather(): k_back = lax.ppermute(k_back, 'dp', back)  1.87 us
    ppermute x4, waiting for transfers between devices, ring_gather(): k_on = lax.ppermute(k_on, 'dp', onward)  1.72 us
  transfers between devices with their start and end apart: 14, of which 5 were waited for; matrix products, arithmetic and copies ran while one was open for 7% of the time, Pallas kernels for 14%

profile of v2, /device:TPU:0, one launch (start us, length us, event | category | flops | bytes accessed | tf_op | source)
XLA Modules:
  0.0 38.4 jit_solution(14327913760398132621)
XLA Ops:
  0.6 3.1 %collective-permute-start = (bf16[16,16,256]{2,1,0:T(8,128)(2,1)}, bf16[16,16,256]{2,1,0:T(8,128)(2,1)S(1)}, u32[]{:S(2)}, u32[]{:S(2)}) collective-permute-start(bf16[16,16,256]{2,1,0:T(8,128)(2,1)} %rest_0_.2), channel_id=1, source_target_pairs={{0,4},{4,8},{8,12},{12,14},{14,10},{10,6},{6,2},{2,0},{1,5},{5,9},... | collective-permute-start | bytes 393224 | tf_op jit(solution)/shard_map/ppermute | solution.py:241
  3.7 0.0 collective-permute-start.4
  3.7 2.0 %collective-permute-start.7 = (bf16[16,16,256]{2,1,0:T(8,128)(2,1)}, bf16[16,16,256]{2,1,0:T(8,128)(2,1)S(1)}, u32[]{:S(2)}, u32[]{:S(2)}) collective-permute-start(bf16[16,16,256]{2,1,0:T(8,128)(2,1)} %rest_0_.3), channel_id=1, source_target_pairs={{0,4},{4,8},{8,12},{12,14},{14,10},{10,6},{6,2},{2,0},{1,5},{5,9},... | collective-permute-start | bytes 393224 | tf_op jit(solution)/shard_map/ppermute | solution.py:246
  5.7 0.0 collective-permute-start.10
  5.7 0.9 %select_reduce_fusion.1 = s32[5,12]{1,0:T(8,128)S(1)} fusion(s32[128]{0:T(128)} %param.15, s32[5,12]{1,0:T(8,128)} %param.16), kind=kLoop, calls=%fused_computation.2 | loop fusion | flops 22980 | bytes 992 | tf_op jit(solution)/shard_map/reduce_sum | solution.py:298
  6.7 0.1 iota_compare_fusion
  6.8 0.1 reshape.27
  6.9 0.1 pad.7.clone
  7.0 0.1 pad.6.clone
  7.0 1.2 %select_reduce_fusion = s32[5,5,12]{2,1,0:T(8,128)S(1)} fusion(s32[5,128]{1,0:T(8,128)} %bitcast.8, pred[5,12,128]{2,1,0:T(8,128)(4,1)S(1)} %iota_compare_fusion), kind=kLoop, calls=%fused_computation | loop fusion | flops 76500 | bytes 11440 | tf_op jit(solution)/shard_map/reduce_sum | solution.py:301
  8.2 0.0 collective-permute-done.rest_1_
  8.2 2.1 %collective-permute-start.1 = (bf16[16,16,256]{2,1,0:T(8,128)(2,1)S(1)}, bf16[16,16,256]{2,1,0:T(8,128)(2,1)S(1)}, u32[]{:S(2)}, u32[]{:S(2)}) collective-permute-start(bf16[16,16,256]{2,1,0:T(8,128)(2,1)S(1)} %collective-permute-done.rest_1_), channel_id=1, source_target_pairs={{0,4},{4,8},{8,12},{12,14},{14,10},{10,6},{6,2},{2,0},{1,5},{5,9},... | collective-permute-start | bytes 393224 | tf_op jit(solution)/shard_map/ppermute | solution.py:241
  10.3 1.4 %collective-permute-done.10.rest_7_ = bf16[16,16,256]{2,1,0:T(8,128)(2,1)S(1)} collective-permute-done((bf16[16,16,256]{2,1,0:T(8,128)(2,1)}, bf16[16,16,256]{2,1,0:T(8,128)(2,1)S(1)}, u32[]{:S(2)}, u32[]{:S(2)}) %collective-permute-start.10) | collective-permute-done | bytes 131104 | tf_op jit(solution)/shard_map/ppermute | solution.py:248
  11.7 0.3 collective-permute-start.11
  12.0 0.1 reshape.28
  12.1 0.0 collective-permute-done.4.rest_7_
  12.1 1.6 %collective-permute-start.5 = (bf16[16,16,256]{2,1,0:T(8,128)(2,1)S(1)}, bf16[16,16,256]{2,1,0:T(8,128)(2,1)S(1)}, u32[]{:S(2)}, u32[]{:S(2)}) collective-permute-start(bf16[16,16,256]{2,1,0:T(8,128)(2,1)S(1)} %collective-permute-done.4.rest_7_), channel_id=1, source_target_pairs={{4,0},{8,4},{12,8},{14,12},{10,14},{6,10},{2,6},{0,2},{5,1},{9,5},... | collective-permute-start | bytes 393224 | tf_op jit(solution)/shard_map/ppermute | solution.py:244
  13.7 0.0 collective-permute-done.7.rest_1_
  13.7 0.4 %collective-permute-start.8 = (bf16[16,16,256]{2,1,0:T(8,128)(2,1)S(1)}, bf16[16,16,256]{2,1,0:T(8,128)(2,1)S(1)}, u32[]{:S(2)}, u32[]{:S(2)}) collective-permute-start(bf16[16,16,256]{2,1,0:T(8,128)(2,1)S(1)} %collective-permute-done.7.rest_1_), channel_id=1, source_target_pairs={{0,4},{4,8},{8,12},{12,14},{14,10},{10,6},{6,2},{2,0},{1,5},{5,9},... | collective-permute-start | bytes 393224 | tf_op jit(solution)/shard_map/ppermute | solution.py:246
  14.1 0.0 collective-permute-done.1.rest_2_
  14.1 1.7 %collective-permute-start.2 = (bf16[16,16,256]{2,1,0:T(8,128)(2,1)S(1)}, bf16[16,16,256]{2,1,0:T(8,128)(2,1)S(1)}, u32[]{:S(2)}, u32[]{:S(2)}) collective-permute-start(bf16[16,16,256]{2,1,0:T(8,128)(2,1)S(1)} %collective-permute-done.1.rest_2_), channel_id=1, source_target_pairs={{0,4},{4,8},{8,12},{12,14},{14,10},{10,6},{6,2},{2,0},{1,5},{5,9},... | collective-permute-start | bytes 393224 | tf_op jit(solution)/shard_map/ppermute | solution.py:241
  15.9 1.7 %collective-permute-done.11.rest_6_ = bf16[16,16,256]{2,1,0:T(8,128)(2,1)S(1)} collective-permute-done((bf16[16,16,256]{2,1,0:T(8,128)(2,1)S(1)}, bf16[16,16,256]{2,1,0:T(8,128)(2,1)S(1)}, u32[]{:S(2)}, u32[]{:S(2)}) %collective-permute-start.11) | collective-permute-done | bytes 131104 | tf_op jit(solution)/shard_map/ppermute | solution.py:248
  17.6 0.2 collective-permute-start.12
  17.8 2.6 %collective-permute-done.5.rest_6_ = bf16[16,16,256]{2,1,0:T(8,128)(2,1)S(1)} collective-permute-done((bf16[16,16,256]{2,1,0:T(8,128)(2,1)S(1)}, bf16[16,16,256]{2,1,0:T(8,128)(2,1)S(1)}, u32[]{:S(2)}, u32[]{:S(2)}) %collective-permute-start.5) | collective-permute-done | bytes 131104 | tf_op jit(solution)/shard_map/ppermute | solution.py:244
  20.4 0.2 collective-permute-start.6
  20.6 0.0 collective-permute-done.8.rest_2_
  20.6 1.8 %collective-permute-start.9 = (bf16[16,16,256]{2,1,0:T(8,128)(2,1)S(1)}, bf16[16,16,256]{2,1,0:T(8,128)(2,1)S(1)}, u32[]{:S(2)}, u32[]{:S(2)}) collective-permute-start(bf16[16,16,256]{2,1,0:T(8,128)(2,1)S(1)} %collective-permute-done.8.rest_2_), channel_id=1, source_target_pairs={{0,4},{4,8},{8,12},{12,14},{14,10},{10,6},{6,2},{2,0},{1,5},{5,9},... | collective-permute-start | bytes 393224 | tf_op jit(solution)/shard_map/ppermute | solution.py:246
  22.4 0.0 collective-permute-done.2.rest_3_
  22.4 1.6 %collective-permute-start.3 = (bf16[16,16,256]{2,1,0:T(8,128)(2,1)S(1)}, bf16[16,16,256]{2,1,0:T(8,128)(2,1)S(1)}, u32[]{:S(2)}, u32[]{:S(2)}) collective-permute-start(bf16[16,16,256]{2,1,0:T(8,128)(2,1)S(1)} %collective-permute-done.2.rest_3_), channel_id=1, source_target_pairs={{0,4},{4,8},{8,12},{12,14},{14,10},{10,6},{6,2},{2,0},{1,5},{5,9},... | collective-permute-start | bytes 393224 | tf_op jit(solution)/shard_map/ppermute | solution.py:241
  24.0 0.0 collective-permute-done.12.rest_5_
  24.0 0.4 %collective-permute-start.13 = (bf16[16,16,256]{2,1,0:T(8,128)(2,1)S(1)}, bf16[16,16,256]{2,1,0:T(8,128)(2,1)S(1)}, u32[]{:S(2)}, u32[]{:S(2)}) collective-permute-start(bf16[16,16,256]{2,1,0:T(8,128)(2,1)S(1)} %collective-permute-done.12.rest_5_), channel_id=1, source_target_pairs={{4,0},{8,4},{12,8},{14,12},{10,14},{6,10},{2,6},{0,2},{5,1},{9,5},... | collective-permute-start | bytes 393224 | tf_op jit(solution)/shard_map/ppermute | solution.py:248
  24.5 1.2 %collective-permute-done.6.rest_5_ = bf16[16,16,256]{2,1,0:T(8,128)(2,1)S(1)} collective-permute-done((bf16[16,16,256]{2,1,0:T(8,128)(2,1)S(1)}, bf16[16,16,256]{2,1,0:T(8,128)(2,1)S(1)}, u32[]{:S(2)}, u32[]{:S(2)}) %collective-permute-start.6) | collective-permute-done | bytes 131104 | tf_op jit(solution)/shard_map/ppermute | solution.py:244
  25.7 1.7 %collective-permute-done.3.rest_4_ = bf16[16,16,256]{2,1,0:T(8,128)(2,1)S(1)} collective-permute-done((bf16[16,16,256]{2,1,0:T(8,128)(2,1)S(1)}, bf16[16,16,256]{2,1,0:T(8,128)(2,1)S(1)}, u32[]{:S(2)}, u32[]{:S(2)}) %collective-permute-start.3) | collective-permute-done | bytes 131104 | tf_op jit(solution)/shard_map/ppermute | solution.py:241
  27.4 0.0 copy-start
  27.4 0.9 %copy-done = bf16[16,16,256]{2,1,0:T(8,128)(2,1)S(1)} copy-done((bf16[16,16,256]{2,1,0:T(8,128)(2,1)S(1)}, bf16[16,16,256]{2,1,0:T(8,128)(2,1)}, u32[]{:S(2)}) %copy-start) | copy-done | bytes 131096
  28.3 0.0 copy-start.1
  28.3 0.0 copy-start.2
  28.3 5.3 %span_weights.1.w_ref = bf16[5,2,896,256]{3,2,1,0:T(8,128)(2,1)S(1)} custom-call(s32[60]{0:T(128)S(1)} %fusion.slot_ref, s32[5,1,128]{2,1,0:T(1,128)S(1)} %reshape.29.limit_ref, bf16[5,5,12,2048]{3,2,1,0:T(8,128)(2,1)} %bitcast.5, bf16[5,32,2048]{2,1,0:T(8,128)(2,1)} %qq_hbm.1, bf16[5,5,12,256]{3,2,1,0:T(8,128)(2,1)} %bitcast.6, bf16[5,32,256]{2,1,0:T(8,128)(2,1)} %qk_hbm.1, ...), custom_call_target="tpu_custom_call" | custom-call | flops 1174405120 | bytes 8388608 | tf_op jit(solution)/shard_map/span_weights/pallas_call | solution.py:200
  33.6 0.0 collective-permute-done.9.rest_3_
  33.7 0.0 collective-permute-done.13.rest_4_
  33.7 0.0 copy-done.1
  33.7 0.0 copy-done.2
  33.7 4.7 %span_values.1 = (bf16[5,5,12,2048]{3,2,1,0:T(8,128)(2,1)}, bf16[5,32,2048]{2,1,0:T(8,128)(2,1)}) custom-call(s32[60]{0:T(128)S(1)} %fusion.slot_ref, s32[5]{0:T(128)S(1)} %copy-done.2, s32[5,1,128]{2,1,0:T(1,128)S(1)} %reshape.29.limit_ref, bf16[5,2,896,256]{3,2,1,0:T(8,128)(2,1)S(1)} %span_weights.1.w_ref, bf16[5,5,12,256]{3,2,1,0:T(8,128)(2,1)} %bitcast.7, ...), custom_call_target="tpu_custom_call" | custom-call | flops 1174405120 | bytes 8388608 | tf_op jit(solution)/shard_map/span_values/pallas_call | solution.py:215
  (8 shorter events, 0.1 us)
Async XLA Ops:
  0.6 7.6 %collective-permute-start = (bf16[16,16,256]{2,1,0:T(8,128)(2,1)}, bf16[16,16,256]{2,1,0:T(8,128)(2,1)S(1)}, u32[]{:S(2)}, u32[]{:S(2)}) collective-permute-start(bf16[16,16,256]{2,1,0:T(8,128)(2,1)} %rest_0_.2), channel_id=1, source_target_pairs={{0,4},{4,8},{8,12},{12,14},{14,10},{10,6},{6,2},{2,0},{1,5},{5,9},... | collective-permute-start | bytes 393224 | tf_op jit(solution)/shard_map/ppermute | solution.py:241
  3.7 8.4 %collective-permute-start.4 = (bf16[16,16,256]{2,1,0:T(8,128)(2,1)}, bf16[16,16,256]{2,1,0:T(8,128)(2,1)S(1)}, u32[]{:S(2)}, u32[]{:S(2)}) collective-permute-start(bf16[16,16,256]{2,1,0:T(8,128)(2,1)} %rest_0_.2), channel_id=1, source_target_pairs={{4,0},{8,4},{12,8},{14,12},{10,14},{6,10},{2,6},{0,2},{5,1},{9,5},... | collective-permute-start | bytes 393224 | tf_op jit(solution)/shard_map/ppermute | solution.py:244
  3.7 10.0 %collective-permute-start.7 = (bf16[16,16,256]{2,1,0:T(8,128)(2,1)}, bf16[16,16,256]{2,1,0:T(8,128)(2,1)S(1)}, u32[]{:S(2)}, u32[]{:S(2)}) collective-permute-start(bf16[16,16,256]{2,1,0:T(8,128)(2,1)} %rest_0_.3), channel_id=1, source_target_pairs={{0,4},{4,8},{8,12},{12,14},{14,10},{10,6},{6,2},{2,0},{1,5},{5,9},... | collective-permute-start | bytes 393224 | tf_op jit(solution)/shard_map/ppermute | solution.py:246
  5.7 6.0 %collective-permute-start.10 = (bf16[16,16,256]{2,1,0:T(8,128)(2,1)}, bf16[16,16,256]{2,1,0:T(8,128)(2,1)S(1)}, u32[]{:S(2)}, u32[]{:S(2)}) collective-permute-start(bf16[16,16,256]{2,1,0:T(8,128)(2,1)} %rest_0_.3), channel_id=1, source_target_pairs={{4,0},{8,4},{12,8},{14,12},{10,14},{6,10},{2,6},{0,2},{5,1},{9,5},... | collective-permute-start | bytes 393224 | tf_op jit(solution)/shard_map/ppermute | solution.py:248
  8.2 5.9 %collective-permute-start.1 = (bf16[16,16,256]{2,1,0:T(8,128)(2,1)S(1)}, bf16[16,16,256]{2,1,0:T(8,128)(2,1)S(1)}, u32[]{:S(2)}, u32[]{:S(2)}) collective-permute-start(bf16[16,16,256]{2,1,0:T(8,128)(2,1)S(1)} %collective-permute-done.rest_1_), channel_id=1, source_target_pairs={{0,4},{4,8},{8,12},{12,14},{14,10},{10,6},{6,2},{2,0},{1,5},{5,9},... | collective-permute-start | bytes 393224 | tf_op jit(solution)/shard_map/ppermute | solution.py:241
  11.7 5.9 %collective-permute-start.11 = (bf16[16,16,256]{2,1,0:T(8,128)(2,1)S(1)}, bf16[16,16,256]{2,1,0:T(8,128)(2,1)S(1)}, u32[]{:S(2)}, u32[]{:S(2)}) collective-permute-start(bf16[16,16,256]{2,1,0:T(8,128)(2,1)S(1)} %collective-permute-done.10.rest_7_), channel_id=1, source_target_pairs={{4,0},{8,4},{12,8},{14,12},{10,14},{6,10},{2,6},{0,2},{5,1},{9,5},... | collective-permute-start | bytes 393224 | tf_op jit(solution)/shard_map/ppermute | solution.py:248
  12.1 8.3 %collective-permute-start.5 = (bf16[16,16,256]{2,1,0:T(8,128)(2,1)S(1)}, bf16[16,16,256]{2,1,0:T(8,128)(2,1)S(1)}, u32[]{:S(2)}, u32[]{:S(2)}) collective-permute-start(bf16[16,16,256]{2,1,0:T(8,128)(2,1)S(1)} %collective-permute-done.4.rest_7_), channel_id=1, source_target_pairs={{4,0},{8,4},{12,8},{14,12},{10,14},{6,10},{2,6},{0,2},{5,1},{9,5},... | collective-permute-start | bytes 393224 | tf_op jit(solution)/shard_map/ppermute | solution.py:244
  13.7 6.9 %collective-permute-start.8 = (bf16[16,16,256]{2,1,0:T(8,128)(2,1)S(1)}, bf16[16,16,256]{2,1,0:T(8,128)(2,1)S(1)}, u32[]{:S(2)}, u32[]{:S(2)}) collective-permute-start(bf16[16,16,256]{2,1,0:T(8,128)(2,1)S(1)} %collective-permute-done.7.rest_1_), channel_id=1, source_target_pairs={{0,4},{4,8},{8,12},{12,14},{14,10},{10,6},{6,2},{2,0},{1,5},{5,9},... | collective-permute-start | bytes 393224 | tf_op jit(solution)/shard_map/ppermute | solution.py:246
  14.1 8.3 %collective-permute-start.2 = (bf16[16,16,256]{2,1,0:T(8,128)(2,1)S(1)}, bf16[16,16,256]{2,1,0:T(8,128)(2,1)S(1)}, u32[]{:S(2)}, u32[]{:S(2)}) collective-permute-start(bf16[16,16,256]{2,1,0:T(8,128)(2,1)S(1)} %collective-permute-done.1.rest_2_), channel_id=1, source_target_pairs={{0,4},{4,8},{8,12},{12,14},{14,10},{10,6},{6,2},{2,0},{1,5},{5,9},... | collective-permute-start | bytes 393224 | tf_op jit(solution)/shard_map/ppermute | solution.py:241
  17.6 6.4 %collective-permute-start.12 = (bf16[16,16,256]{2,1,0:T(8,128)(2,1)S(1)}, bf16[16,16,256]{2,1,0:T(8,128)(2,1)S(1)}, u32[]{:S(2)}, u32[]{:S(2)}) collective-permute-start(bf16[16,16,256]{2,1,0:T(8,128)(2,1)S(1)} %collective-permute-done.11.rest_6_), channel_id=1, source_target_pairs={{4,0},{8,4},{12,8},{14,12},{10,14},{6,10},{2,6},{0,2},{5,1},{9,5},... | collective-permute-start | bytes 393224 | tf_op jit(solution)/shard_map/ppermute | solution.py:248
  20.4 5.3 %collective-permute-start.6 = (bf16[16,16,256]{2,1,0:T(8,128)(2,1)S(1)}, bf16[16,16,256]{2,1,0:T(8,128)(2,1)S(1)}, u32[]{:S(2)}, u32[]{:S(2)}) collective-permute-start(bf16[16,16,256]{2,1,0:T(8,128)(2,1)S(1)} %collective-permute-done.5.rest_6_), channel_id=1, source_target_pairs={{4,0},{8,4},{12,8},{14,12},{10,14},{6,10},{2,6},{0,2},{5,1},{9,5},... | collective-permute-start | bytes 393224 | tf_op jit(solution)/shard_map/ppermute | solution.py:244
  20.6 13.0 %collective-permute-start.9 = (bf16[16,16,256]{2,1,0:T(8,128)(2,1)S(1)}, bf16[16,16,256]{2,1,0:T(8,128)(2,1)S(1)}, u32[]{:S(2)}, u32[]{:S(2)}) collective-permute-start(bf16[16,16,256]{2,1,0:T(8,128)(2,1)S(1)} %collective-permute-done.8.rest_2_), channel_id=1, source_target_pairs={{0,4},{4,8},{8,12},{12,14},{14,10},{10,6},{6,2},{2,0},{1,5},{5,9},... | collective-permute-start | bytes 393224 | tf_op jit(solution)/shard_map/ppermute | solution.py:246
  22.4 5.0 %collective-permute-start.3 = (bf16[16,16,256]{2,1,0:T(8,128)(2,1)S(1)}, bf16[16,16,256]{2,1,0:T(8,128)(2,1)S(1)}, u32[]{:S(2)}, u32[]{:S(2)}) collective-permute-start(bf16[16,16,256]{2,1,0:T(8,128)(2,1)S(1)} %collective-permute-done.2.rest_3_), channel_id=1, source_target_pairs={{0,4},{4,8},{8,12},{12,14},{14,10},{10,6},{6,2},{2,0},{1,5},{5,9},... | collective-permute-start | bytes 393224 | tf_op jit(solution)/shard_map/ppermute | solution.py:241
  24.0 9.7 %collective-permute-start.13 = (bf16[16,16,256]{2,1,0:T(8,128)(2,1)S(1)}, bf16[16,16,256]{2,1,0:T(8,128)(2,1)S(1)}, u32[]{:S(2)}, u32[]{:S(2)}) collective-permute-start(bf16[16,16,256]{2,1,0:T(8,128)(2,1)S(1)} %collective-permute-done.12.rest_5_), channel_id=1, source_target_pairs={{4,0},{8,4},{12,8},{14,12},{10,14},{6,10},{2,6},{0,2},{5,1},{9,5},... | collective-permute-start | bytes 393224 | tf_op jit(solution)/shard_map/ppermute | solution.py:248
  27.4 0.9 %copy-start = (bf16[16,16,256]{2,1,0:T(8,128)(2,1)S(1)}, bf16[16,16,256]{2,1,0:T(8,128)(2,1)}, u32[]{:S(2)}) copy-start(bf16[16,16,256]{2,1,0:T(8,128)(2,1)} %rest_0_.2) | copy-start | bytes 393220
  28.3 5.4 %copy-start.1 = (bf16[16,16,256]{2,1,0:T(8,128)(2,1)S(1)}, bf16[16,16,256]{2,1,0:T(8,128)(2,1)}, u32[]{:S(2)}) copy-start(bf16[16,16,256]{2,1,0:T(8,128)(2,1)} %rest_0_.3) | copy-start | bytes 393220
  28.3 5.4 %copy-start.2 = (s32[5]{0:T(128)S(1)}, s32[5]{0:T(128)}, u32[]{:S(2)}) copy-start(s32[5]{0:T(128)} %length_ref.1) | copy-start | bytes 64

commit v3 on v2

v3 whole, which is shorter than its diff:
```python
import functools

import jax
import jax.numpy as jnp
from jax import lax
from jax.experimental import pallas as pl
from jax.experimental.pallas import tpu as pltpu
from jax.sharding import PartitionSpec as P

HEAD = 128
LANES = 128
ROW_TILE = 16
MASKED = -1e30
RING_MAX = 16
VMEM_LIMIT = 40 * 1024 * 1024


def fill_pool(pieces, pool):
    rows = pieces[0].shape[0]
    for b, piece in enumerate(pieces):
        pool[b * rows : (b + 1) * rows] = piece[...]


def blend(first, slot_ref, pool, placed, keep, blended):
    span_len = pool.shape[1]
    total = keep.shape[0]
    for j in range(total // span_len):
        at = slice(j * span_len, (j + 1) * span_len)
        kept = jnp.concatenate([keep[at, :]] * (blended.shape[1] // LANES), axis=1)
        blended[at, :] = placed[at, :] + kept * pool[slot_ref[first + j]]
    blended[total:, :] = placed[total:, :]


def prepare_kernel(
    count, place_ref, *rest
):
    sources, rest = rest[:12], rest[12:]
    scalars, own_k, own_v, placed, keep, bias, queries, *rest = rest
    spans_ref, home_ref, sel_ref, length_ref, fk, fv, qk, qv, fq, qq, rows, limits, sems = rest
    req_count, picks, lists, width = fk.shape
    q_rows = qk.shape[1]
    spans_dev, span_len, _ = own_k.shape
    kv_heads, heads = queries.shape[1], queries.shape[2]
    total = lists * span_len
    copies = [
        pltpu.make_async_copy(source, target, sems.at[n])
        for n, (source, target) in enumerate(
            zip(
                sources,
                (spans_ref, home_ref, sel_ref, length_ref, fk, fv, qk, qv, fq, qq, own_k, own_v),
                strict=True,
            )
        )
    ]
    for copy in copies:
        copy.start()
    rows[...] = jnp.zeros_like(rows)
    queries[...] = jnp.zeros_like(queries)
    lane = lax.broadcasted_iota(jnp.int32, (1, LANES), 1)
    asked_at = lane - picks * ROW_TILE
    blank = jnp.where((asked_at >= 0) & (asked_at < q_rows), total + asked_at, -1)
    for copy in copies[:4]:
        copy.wait()
    for r in range(req_count):
        limit = blank
        for j in range(lists):
            position = home_ref[spans_ref[r, j]]
            owner = lax.div(position, spans_dev)
            half = lax.div(owner, 2)
            place = jnp.where(lax.rem(owner, 2) == 0, half, count - 1 - half)
            upstream = lax.rem(place_ref[0] - place + count, count)
            scalars[r * lists + j] = upstream * spans_dev + lax.rem(position, spans_dev)
            for i in range(picks):
                limit = jnp.where(lane == i * ROW_TILE + j, j * span_len + sel_ref[i, position], limit)
        limits[r] = limit
        scalars[req_count * lists + r] = length_ref[r]
    for copy in copies[4:8]:
        copy.wait()
    key = lax.broadcasted_iota(jnp.int32, (placed.shape[1], LANES), 0)
    for r in range(req_count):
        limit = limits[r]
        rows[0:picks, 0:lists, 0:width] = fk[r]
        rows[0:picks, 0:lists, width:] = fv[r]
        rows[picks : picks + q_rows // ROW_TILE, :, 0:width] = qk[r].reshape(-1, ROW_TILE, width)
        rows[picks : picks + q_rows // ROW_TILE, :, width:] = qv[r].reshape(-1, ROW_TILE, width)
        here = jnp.where(key == limit, 1.0, 0.0)
        placed[r] = jnp.dot(
            here.astype(jnp.bfloat16),
            rows[...].reshape(LANES, -1),
            preferred_element_type=jnp.float32,
        ).astype(jnp.bfloat16)
        taken = jnp.max(here[:total], axis=1, keepdims=True)
        keep[r] = jnp.broadcast_to(1.0 - taken, (total, LANES)).astype(jnp.bfloat16)
        bias[r] = jnp.where(key <= limit, 0.0, MASKED).astype(jnp.bfloat16)
    for copy in copies[8:]:
        copy.wait()
    for r in range(req_count):
        for g in range(kv_heads):
            for h in range(heads):
                at = (g * heads + h) * HEAD
                queries[r, g, h, 0:picks, 0:lists, :] = fq[r, :, :, at : at + HEAD]
                queries[r, g, h, picks:, :, :] = qq[r, :, at : at + HEAD].reshape(-1, ROW_TILE, HEAD)


def weights_kernel(n_buf, lists, slot_ref, placed, keep, bias, queries, *rest):
    pieces = rest[:n_buf]
    out_ref, pool, blended, units = rest[n_buf:]
    req_count, kv_heads, heads, tiles = queries.shape[:4]
    rows_head = tiles * ROW_TILE
    width = blended.shape[1]
    row = lax.broadcasted_iota(jnp.int32, (rows_head, LANES), 0)
    column = lax.broadcasted_iota(jnp.int32, (rows_head, LANES), 1)
    unit = jnp.where(row == column, 1.0, 0.0).astype(jnp.bfloat16)
    for h in range(heads):
        units[h * rows_head : (h + 1) * rows_head, :] = unit
    fill_pool(pieces, pool)
    scale = 1.4426950408889634 / float(HEAD) ** 0.5
    for r in range(req_count):
        blend(r * lists, slot_ref, pool, placed.at[r, :, 0:width], keep.at[r], blended)
        for g in range(kv_heads):
            table = jnp.concatenate([blended[:, g * HEAD : (g + 1) * HEAD], bias[r]], axis=1)
            stacked = queries[r, g].reshape(heads * rows_head, HEAD)
            scores = lax.dot_general(
                jnp.concatenate([stacked, units[...]], axis=1),
                table,
                (((1,), (1,)), ((), ())),
                preferred_element_type=jnp.float32,
            )
            top = jnp.max(scores, axis=1, keepdims=True)
            out_ref[r, g] = jnp.exp2((scores - top) * scale).astype(jnp.bfloat16)


def values_kernel(n_buf, slot_ref, w_ref, placed, keep, *rest):
    pieces = rest[:n_buf]
    redone_hbm, spoken_hbm, redone, spoken, pool, blended, out_sems = rest[n_buf:]
    req_count, picks, lists, _ = redone.shape
    kv_heads = w_ref.shape[1]
    q_rows = spoken.shape[1]
    heads = spoken.shape[2] // HEAD // kv_heads
    rows_head = picks * ROW_TILE + q_rows
    width = blended.shape[1]
    fill_pool(pieces, pool)

    def out_copies(r):
        return [
            pltpu.make_async_copy(redone.at[r], redone_hbm.at[r], out_sems.at[2 * r]),
            pltpu.make_async_copy(spoken.at[r], spoken_hbm.at[r], out_sems.at[2 * r + 1]),
        ]

    for r in range(req_count):
        blend(r * lists, slot_ref, pool, placed.at[r, :, width : 2 * width], keep.at[r], blended)
        ones = jnp.ones((blended.shape[0], LANES), jnp.bfloat16)
        length = slot_ref[req_count * lists + r]
        live = lax.broadcasted_iota(jnp.int32, (q_rows, HEAD), 0) < length
        for g in range(kv_heads):
            table = jnp.concatenate([blended[:, g * HEAD : (g + 1) * HEAD], ones], axis=1)
            both = jnp.dot(w_ref[r, g], table, preferred_element_type=jnp.float32)
            result = both[:, :HEAD] / both[:, HEAD:]
            for h in range(heads):
                at = (g * heads + h) * HEAD
                row = h * rows_head
                fresh = result[row : row + picks * ROW_TILE].astype(jnp.bfloat16)
                redone[r, :, :, at : at + HEAD] = fresh.reshape(picks, ROW_TILE, HEAD)[:, :lists, :]
                asked = result[row + picks * ROW_TILE : row + rows_head]
                spoken[r, :, at : at + HEAD] = jnp.where(live, asked, 0.0).astype(jnp.bfloat16)
        for copy in out_copies(r):
            copy.start()
    for r in range(req_count):
        for copy in out_copies(r):
            copy.wait()


SMEM_SPEC = pl.BlockSpec(memory_space=pltpu.SMEM)
VMEM_SPEC = pl.BlockSpec(memory_space=pltpu.VMEM)
HBM_SPEC = pl.BlockSpec(memory_space=pltpu.HBM)
PARAMS = pltpu.CompilerParams(vmem_limit_bytes=VMEM_LIMIT)


def in_vmem(x):
    return pltpu.with_memory_space_constraint(x, pltpu.VMEM)


def in_hbm(x):
    return pltpu.with_memory_space_constraint(x, pltpu.HBM)


def like(x):
    return pltpu.VMEM(x.shape, x.dtype)


def prepare(place, spans, home, sel, lengths, cache_k, cache_v, fresh_q, fresh_k, fresh_v, question_q, question_k, question_v):
    count = lax.axis_size("dp")
    req_count, picks, lists, q_width = fresh_q.shape
    _, span_len, width = cache_k.shape
    q_rows = question_q.shape[1]
    kv_heads, heads = width // HEAD, q_width // width
    total = lists * span_len
    padded = -(-(total + q_rows) // LANES) * LANES
    near = (spans, home, sel, lengths)
    held = (fresh_k, fresh_v, question_k, question_v, fresh_q, question_q)
    far = near + held + (cache_k, cache_v)
    bf16 = jnp.bfloat16
    return pl.pallas_call(
        functools.partial(prepare_kernel, count),
        in_specs=[SMEM_SPEC] + [HBM_SPEC] * len(far),
        out_specs=[SMEM_SPEC] + [VMEM_SPEC] * 6,
        out_shape=[
            pltpu.SMEM((req_count * lists + req_count,), jnp.int32),
            like(cache_k),
            like(cache_v),
            pltpu.VMEM((req_count, padded, 2 * width), bf16),
            pltpu.VMEM((req_count, total, LANES), bf16),
            pltpu.VMEM((req_count, padded, LANES), bf16),
            pltpu.VMEM((req_count, kv_heads, heads, picks + q_rows // ROW_TILE, ROW_TILE, HEAD), bf16),
        ],
        scratch_shapes=[pltpu.SMEM(x.shape, x.dtype) for x in near]
        + [like(x) for x in held]
        + [
            pltpu.VMEM((LANES // ROW_TILE, ROW_TILE, 2 * width), bf16),
            pltpu.VMEM((req_count, 1, LANES), jnp.int32),
            pltpu.SemaphoreType.DMA((len(far),)),
        ],
        compiler_params=PARAMS,
        cost_estimate=pl.CostEstimate(flops=0, bytes_accessed=8 << 20, transcendentals=0),
        name="span_prepare",
    )(place, *map(in_hbm, far))


def attend(scalars, placed, keep, bias, queries, k_pieces, v_pieces, redone_shape, spoken_shape):
    req_count, _, lists, _ = redone_shape
    piece_rows, span_len, width = k_pieces[0].shape
    n_buf = len(k_pieces)
    kv_heads, heads, tiles = queries.shape[1:4]
    padded = placed.shape[1]
    pool = pltpu.VMEM((n_buf * piece_rows, span_len, width), jnp.bfloat16)
    blended = pltpu.VMEM((padded, width), jnp.bfloat16)
    w_shape = (req_count, kv_heads, heads * tiles * ROW_TILE, padded)
    flops = 4 * req_count * kv_heads * heads * tiles * ROW_TILE * padded * HEAD
    weights = pl.pallas_call(
        functools.partial(weights_kernel, n_buf, lists),
        in_specs=[SMEM_SPEC] + [VMEM_SPEC] * (4 + n_buf),
        out_specs=VMEM_SPEC,
        scratch_shapes=[pool, blended, pltpu.VMEM((heads * tiles * ROW_TILE, LANES), jnp.bfloat16)],
        out_shape=pltpu.VMEM(w_shape, jnp.bfloat16),
        compiler_params=PARAMS,
        cost_estimate=pl.CostEstimate(flops=flops, bytes_accessed=8 << 20, transcendentals=flops // 512),
        name="span_weights",
    )(scalars, *map(in_vmem, (placed, keep, bias, queries)), *map(in_vmem, k_pieces))
    return pl.pallas_call(
        functools.partial(values_kernel, n_buf),
        in_specs=[SMEM_SPEC] + [VMEM_SPEC] * (3 + n_buf),
        out_specs=[HBM_SPEC, HBM_SPEC],
        scratch_shapes=[
            pltpu.VMEM(redone_shape, jnp.bfloat16),
            pltpu.VMEM(spoken_shape, jnp.bfloat16),
            pool,
            blended,
            pltpu.SemaphoreType.DMA((2 * req_count,)),
        ],
        out_shape=[
            jax.ShapeDtypeStruct(redone_shape, jnp.bfloat16),
            jax.ShapeDtypeStruct(spoken_shape, jnp.bfloat16),
        ],
        compiler_params=PARAMS,
        cost_estimate=pl.CostEstimate(flops=flops, bytes_accessed=8 << 20, transcendentals=0),
        name="span_values",
    )(scalars, *map(in_vmem, (weights, placed, keep)), *map(in_vmem, v_pieces))


def ring_gather(keys, values, count, ready):
    order = list(range(0, count, 2)) + list(range(1, count, 2))[::-1]
    onward = [(order[i], order[(i + 1) % count]) for i in range(count)]
    back = [(b, a) for a, b in onward]
    k_at, v_at = {0: keys}, {0: values}
    k_on = k_back = keys
    v_on = v_back = values
    half, rest = count // 2, (count - 1) // 2
    for hop in range(1, half + 1):
        k_on = lax.ppermute(k_on, "dp", onward)
        k_at[hop] = k_on
        if hop <= rest:
            k_back = lax.ppermute(k_back, "dp", back)
            k_at[count - hop] = k_back
            if hop == 1:
                k_back, _ = lax.optimization_barrier((k_back, ready))
            v_on = lax.ppermute(v_on, "dp", onward)
            v_at[hop] = v_on
        v_back = lax.ppermute(v_back, "dp", back)
        v_at[count - hop] = v_back
    return [k_at[d] for d in range(count)], [v_at[d] for d in range(count)]


def asked_gather(keys, values, positions, spans_dev, count):
    slot_count = positions.shape[0]
    capacity = (slot_count + count - 1) // count
    owner = positions // spans_dev
    local = positions % spans_dev
    ids = jnp.arange(slot_count, dtype=jnp.int32)
    earlier = (owner[:, None] == owner[None, :]) & (ids[None, :] < ids[:, None])
    slots = owner * capacity + jnp.sum(earlier.astype(jnp.int32), axis=1)
    asking = jnp.full((count * capacity,), -1, jnp.int32).at[slots].set(local)
    wanted = jnp.maximum(lax.all_to_all(asking, "dp", split_axis=0, concat_axis=0, tiled=True), 0)
    pieces = [
        [lax.all_to_all(cache[wanted], "dp", split_axis=0, concat_axis=0, tiled=True)]
        for cache in (keys, values)
    ]
    return slots, pieces[0], pieces[1]


def shards(
    cache_k,
    cache_v,
    sel_rows,
    span_home,
    request_spans,
    fresh_q,
    fresh_k,
    fresh_v,
    question_q,
    question_k,
    question_v,
    question_len,
):
    count = lax.axis_size("dp")
    spans_dev = cache_k.shape[0]
    turned_q, turned_k, turned_v = [jnp.transpose(x, (0, 2, 1, 3)) for x in (fresh_q, fresh_k, fresh_v)]
    me = lax.axis_index("dp")
    place = jnp.where(me % 2 == 0, me // 2, count - 1 - me // 2).astype(jnp.int32).reshape(1)
    scalars, own_k, own_v, placed, keep, bias, queries = prepare(
        place,
        request_spans,
        span_home,
        sel_rows.T,
        question_len,
        cache_k,
        cache_v,
        turned_q,
        turned_k,
        turned_v,
        question_q,
        question_k,
        question_v,
    )
    if count <= RING_MAX:
        k_pieces, v_pieces = ring_gather(cache_k, cache_v, count, own_k)
        k_pieces[0], v_pieces[0] = own_k, own_v
        scalars = pltpu.with_memory_space_constraint(scalars, pltpu.SMEM)
    else:
        pool_ids = jnp.arange(span_home.shape[0], dtype=jnp.int32)
        named = request_spans.reshape(-1, 1) == pool_ids
        positions = jnp.sum(jnp.where(named, span_home, 0), axis=-1, dtype=jnp.int32)
        slots, k_pieces, v_pieces = asked_gather(cache_k, cache_v, positions, spans_dev, count)
        scalars = jnp.concatenate([slots, question_len])
    redone, spoken = attend(
        scalars, placed, keep, bias, queries, k_pieces, v_pieces, turned_q.shape, question_q.shape
    )
    return jnp.transpose(redone, (0, 2, 1, 3)), spoken


def solution(mesh):
    in_specs = (
        P(("groups", "dp"), None, "tp"),
        P(("groups", "dp"), None, "tp"),
        P("groups", None),
        P("groups"),
        P(("groups", "dp"), None),
        P(("groups", "dp"), None, None, "tp"),
        P(("groups", "dp"), None, None, "tp"),
        P(("groups", "dp"), None, None, "tp"),
        P(("groups", "dp"), None, "tp"),
        P(("groups", "dp"), None, "tp"),
        P(("groups", "dp"), None, "tp"),
        P(("groups", "dp")),
    )
    out_specs = (P(("groups", "dp"), None, None, "tp"), P(("groups", "dp"), None, "tp"))
    return jax.shard_map(shards, mesh=mesh, in_specs=in_specs, out_specs=out_specs, check_vma=False)
```

time: 38.6 us -> 31.4 us (0.81)
  Pallas kernels: 10 us -> 6.87 us
  other arithmetic: 2.27 us -> 0 us
  waiting for transfers between devices: 8.6 us -> 6.48 us
  starting transfers between devices: 15.5 us -> 17.2 us
  local copies, waits for them, and re-layouts: 1.23 us -> 0 us
    pallas_call x2 -> x3, Pallas kernels: 10 us -> 6.87 us  [the longest x1 2.7 us: prepare(): pl.pallas_call(functools.partial(prepare_kernel, count), in_specs=[SMEM_S...]
    ppermute x4, waiting for transfers between devices: 3.1 us -> 0.76 us  [ring_gather(): v_back = lax.ppermute(v_back, 'dp', back)]
    ppermute x3, starting transfers between devices: 1.87 us -> 4.01 us  [ring_gather(): k_back = lax.ppermute(k_back, 'dp', back)]
    reduce_sum x2 -> x0, other arithmetic: 2.14 us -> none  [the longest x1 1.2 us: shards(): jnp.sum(jnp.where(positions[:, None, :, None] == pool_ids, sel_rows.T[Non...]
    ppermute x4, starting transfers between devices: 8.45 us -> 6.93 us  [ring_gather(): k_on = lax.ppermute(k_on, 'dp', onward)]
    ppermute x4, starting transfers between devices: 0.97 us -> 2.18 us  [ring_gather(): v_back = lax.ppermute(v_back, 'dp', back)]
    unnamed x6 -> x0, local copies, waits for them, and re-layouts: 0.91 us -> none
    ppermute x3, waiting for transfers between devices: 3.78 us -> 2.96 us  [ring_gather(): k_back = lax.ppermute(k_back, 'dp', back)]
  transfers between devices with their start and end apart: 14 -> 14, of which waited for: 5 -> 6; matrix products, arithmetic and copies ran while one was open for 7% -> 0% of each run, Pallas kernels for 14% -> 15%
where the time goes in v3:
time: 31.4 us; the launch traced here: 31.2 us
  starting transfers between devices  17.2 us (55%)
  Pallas kernels  6.87 us (22%)
  waiting for transfers between devices  6.48 us (21%)
  between operations  0.67 us (2%)
    ppermute x4, starting transfers between devices, ring_gather(): k_on = lax.ppermute(k_on, 'dp', onward)  6.93 us
    ppermute x3, starting transfers between devices, ring_gather(): v_on = lax.ppermute(v_on, 'dp', onward)  4.07 us
    ppermute x3, starting transfers between devices, ring_gather(): k_back = lax.ppermute(k_back, 'dp', back)  4.01 us
    ppermute x3, waiting for transfers between devices, ring_gather(): k_back = lax.ppermute(k_back, 'dp', back)  2.96 us
    pallas_call x1, Pallas kernels, prepare(): pl.pallas_call(functools.partial(prepare_kernel, count), in_specs=[SMEM_S...  2.7 us
    pallas_call x1, Pallas kernels, attend(): pl.pallas_call(functools.partial(values_kernel, n_buf), in_specs=[SMEM_SP...  2.31 us
    ppermute x4, starting transfers between devices, ring_gather(): v_back = lax.ppermute(v_back, 'dp', back)  2.18 us
    ppermute x4, waiting for transfers between devices, ring_gather(): k_on = lax.ppermute(k_on, 'dp', onward)  2.1 us
  transfers between devices with their start and end apart: 14, of which 6 were waited for; matrix products, arithmetic and copies ran while one was open for 0% of the time, Pallas kernels for 15%

profile of v3, /device:TPU:0, one launch (start us, length us, event | category | flops | bytes accessed | tf_op | source)
XLA Modules:
  0.0 31.2 jit_solution(1527893895721015587)
XLA Ops:
  0.6 3.1 %collective-permute-start = (bf16[16,16,256]{2,1,0:T(8,128)(2,1)}, bf16[16,16,256]{2,1,0:T(8,128)(2,1)S(1)}, u32[]{:S(2)}, u32[]{:S(2)}) collective-permute-start(bf16[16,16,256]{2,1,0:T(8,128)(2,1)} %rest_10_.1), channel_id=1, source_target_pairs={{0,4},{4,8},{8,12},{12,14},{14,10},{10,6},{6,2},{2,0},{1,5},{5,9},... | collective-permute-start | bytes 393224 | tf_op jit(solution)/shard_map/ppermute | solution.py:279
  3.7 0.0 collective-permute-start.10
  3.7 1.9 %collective-permute-start.4 = (bf16[16,16,256]{2,1,0:T(8,128)(2,1)}, bf16[16,16,256]{2,1,0:T(8,128)(2,1)S(1)}, u32[]{:S(2)}, u32[]{:S(2)}) collective-permute-start(bf16[16,16,256]{2,1,0:T(8,128)(2,1)} %rest_10_.1), channel_id=1, source_target_pairs={{4,0},{8,4},{12,8},{14,12},{10,14},{6,10},{2,6},{0,2},{5,1},{9,5},... | collective-permute-start | bytes 393224 | tf_op jit(solution)/shard_map/ppermute | solution.py:282
  5.7 1.7 %collective-permute-done.rest_1_ = bf16[16,16,256]{2,1,0:T(8,128)(2,1)S(1)} collective-permute-done((bf16[16,16,256]{2,1,0:T(8,128)(2,1)}, bf16[16,16,256]{2,1,0:T(8,128)(2,1)S(1)}, u32[]{:S(2)}, u32[]{:S(2)}) %collective-permute-start) | collective-permute-done | bytes 131104 | tf_op jit(solution)/shard_map/ppermute | solution.py:279
  7.3 1.8 %collective-permute-start.1 = (bf16[16,16,256]{2,1,0:T(8,128)(2,1)S(1)}, bf16[16,16,256]{2,1,0:T(8,128)(2,1)S(1)}, u32[]{:S(2)}, u32[]{:S(2)}) collective-permute-start(bf16[16,16,256]{2,1,0:T(8,128)(2,1)S(1)} %collective-permute-done.rest_1_), channel_id=1, source_target_pairs={{0,4},{4,8},{8,12},{12,14},{14,10},{10,6},{6,2},{2,0},{1,5},{5,9},... | collective-permute-start | bytes 393224 | tf_op jit(solution)/shard_map/ppermute | solution.py:279
  9.2 1.6 %collective-permute-start.7 = (bf16[16,16,256]{2,1,0:T(8,128)(2,1)}, bf16[16,16,256]{2,1,0:T(8,128)(2,1)S(1)}, u32[]{:S(2)}, u32[]{:S(2)}) collective-permute-start(bf16[16,16,256]{2,1,0:T(8,128)(2,1)} %rest_11_.1), channel_id=1, source_target_pairs={{0,4},{4,8},{8,12},{12,14},{14,10},{10,6},{6,2},{2,0},{1,5},{5,9},... | collective-permute-start | bytes 393224 | tf_op jit(solution)/shard_map/ppermute | solution.py:286
  10.7 0.0 collective-permute-done.10.rest_7_
  10.7 0.4 %collective-permute-start.11 = (bf16[16,16,256]{2,1,0:T(8,128)(2,1)S(1)}, bf16[16,16,256]{2,1,0:T(8,128)(2,1)S(1)}, u32[]{:S(2)}, u32[]{:S(2)}) collective-permute-start(bf16[16,16,256]{2,1,0:T(8,128)(2,1)S(1)} %collective-permute-done.10.rest_7_), channel_id=1, source_target_pairs={{4,0},{8,4},{12,8},{14,12},{10,14},{6,10},{2,6},{0,2},{5,1},{9,5},... | collective-permute-start | bytes 393224 | tf_op jit(solution)/shard_map/ppermute | solution.py:288
  11.2 2.7 %span_prepare.1 = (s32[65]{0:T(128)S(4)}, bf16[16,16,256]{2,1,0:T(8,128)(2,1)S(1)}, bf16[16,16,256]{2,1,0:T(8,128)(2,1)S(1)}, bf16[5,256,512]{2,1,0:T(8,128)(2,1...) custom-call(s32[1]{0:T(128)} %bitcast.place_ref, ...), custom_call_target="tpu_custom_call" | custom-call | bytes 8388608 | tf_op jit(solution)/shard_map/span_prepare/pallas_call | solution.py:203
  13.9 0.0 collective-permute-done.4.rest_7_
  13.9 1.1 %collective-permute-start.5 = (bf16[16,16,256]{2,1,0:T(8,128)(2,1)S(1)}, bf16[16,16,256]{2,1,0:T(8,128)(2,1)S(1)}, u32[]{:S(2)}, u32[]{:S(2)}) collective-permute-start(bf16[16,16,256]{2,1,0:T(8,128)(2,1)S(1)} %collective-permute-done.4.rest_7_), channel_id=1, source_target_pairs={{4,0},{8,4},{12,8},{14,12},{10,14},{6,10},{2,6},{0,2},{5,1},{9,5},... | collective-permute-start | bytes 393224 | tf_op jit(solution)/shard_map/ppermute | solution.py:282
  15.0 0.0 collective-permute-done.1.rest_2_
  15.0 1.0 %collective-permute-start.2 = (bf16[16,16,256]{2,1,0:T(8,128)(2,1)S(1)}, bf16[16,16,256]{2,1,0:T(8,128)(2,1)S(1)}, u32[]{:S(2)}, u32[]{:S(2)}) collective-permute-start(bf16[16,16,256]{2,1,0:T(8,128)(2,1)S(1)} %collective-permute-done.1.rest_2_), channel_id=1, source_target_pairs={{0,4},{4,8},{8,12},{12,14},{14,10},{10,6},{6,2},{2,0},{1,5},{5,9},... | collective-permute-start | bytes 393224 | tf_op jit(solution)/shard_map/ppermute | solution.py:279
  16.0 0.0 collective-permute-done.7.rest_1_
  16.0 1.6 %collective-permute-start.8 = (bf16[16,16,256]{2,1,0:T(8,128)(2,1)S(1)}, bf16[16,16,256]{2,1,0:T(8,128)(2,1)S(1)}, u32[]{:S(2)}, u32[]{:S(2)}) collective-permute-start(bf16[16,16,256]{2,1,0:T(8,128)(2,1)S(1)} %collective-permute-done.7.rest_1_), channel_id=1, source_target_pairs={{0,4},{4,8},{8,12},{12,14},{14,10},{10,6},{6,2},{2,0},{1,5},{5,9},... | collective-permute-start | bytes 393224 | tf_op jit(solution)/shard_map/ppermute | solution.py:286
  17.6 0.0 collective-permute-done.11.rest_6_
  17.6 0.4 %collective-permute-start.12 = (bf16[16,16,256]{2,1,0:T(8,128)(2,1)S(1)}, bf16[16,16,256]{2,1,0:T(8,128)(2,1)S(1)}, u32[]{:S(2)}, u32[]{:S(2)}) collective-permute-start(bf16[16,16,256]{2,1,0:T(8,128)(2,1)S(1)} %collective-permute-done.11.rest_6_), channel_id=1, source_target_pairs={{4,0},{8,4},{12,8},{14,12},{10,14},{6,10},{2,6},{0,2},{5,1},{9,5},... | collective-permute-start | bytes 393224 | tf_op jit(solution)/shard_map/ppermute | solution.py:288
  18.0 2.3 %collective-permute-done.5.rest_6_ = bf16[16,16,256]{2,1,0:T(8,128)(2,1)S(1)} collective-permute-done((bf16[16,16,256]{2,1,0:T(8,128)(2,1)S(1)}, bf16[16,16,256]{2,1,0:T(8,128)(2,1)S(1)}, u32[]{:S(2)}, u32[]{:S(2)}) %collective-permute-start.5) | collective-permute-done | bytes 131104 | tf_op jit(solution)/shard_map/ppermute | solution.py:282
  20.3 1.0 %collective-permute-start.6 = (bf16[16,16,256]{2,1,0:T(8,128)(2,1)S(1)}, bf16[16,16,256]{2,1,0:T(8,128)(2,1)S(1)}, u32[]{:S(2)}, u32[]{:S(2)}) collective-permute-start(bf16[16,16,256]{2,1,0:T(8,128)(2,1)S(1)} %collective-permute-done.5.rest_6_), channel_id=1, source_target_pairs={{4,0},{8,4},{12,8},{14,12},{10,14},{6,10},{2,6},{0,2},{5,1},{9,5},... | collective-permute-start | bytes 393224 | tf_op jit(solution)/shard_map/ppermute | solution.py:282
  21.3 0.0 collective-permute-done.2.rest_3_
  21.3 1.0 %collective-permute-start.3 = (bf16[16,16,256]{2,1,0:T(8,128)(2,1)S(1)}, bf16[16,16,256]{2,1,0:T(8,128)(2,1)S(1)}, u32[]{:S(2)}, u32[]{:S(2)}) collective-permute-start(bf16[16,16,256]{2,1,0:T(8,128)(2,1)S(1)} %collective-permute-done.2.rest_3_), channel_id=1, source_target_pairs={{0,4},{4,8},{8,12},{12,14},{14,10},{10,6},{6,2},{2,0},{1,5},{5,9},... | collective-permute-start | bytes 393224 | tf_op jit(solution)/shard_map/ppermute | solution.py:279
  22.4 0.7 %collective-permute-done.8.rest_2_ = bf16[16,16,256]{2,1,0:T(8,128)(2,1)S(1)} collective-permute-done((bf16[16,16,256]{2,1,0:T(8,128)(2,1)S(1)}, bf16[16,16,256]{2,1,0:T(8,128)(2,1)S(1)}, u32[]{:S(2)}, u32[]{:S(2)}) %collective-permute-start.8) | collective-permute-done | bytes 131104 | tf_op jit(solution)/shard_map/ppermute | solution.py:286
  23.0 0.9 %collective-permute-start.9 = (bf16[16,16,256]{2,1,0:T(8,128)(2,1)S(1)}, bf16[16,16,256]{2,1,0:T(8,128)(2,1)S(1)}, u32[]{:S(2)}, u32[]{:S(2)}) collective-permute-start(bf16[16,16,256]{2,1,0:T(8,128)(2,1)S(1)} %collective-permute-done.8.rest_2_), channel_id=1, source_target_pairs={{0,4},{4,8},{8,12},{12,14},{14,10},{10,6},{6,2},{2,0},{1,5},{5,9},... | collective-permute-start | bytes 393224 | tf_op jit(solution)/shard_map/ppermute | solution.py:286
  23.9 0.0 collective-permute-done.12.rest_5_
  23.9 1.3 %collective-permute-start.13 = (bf16[16,16,256]{2,1,0:T(8,128)(2,1)S(1)}, bf16[16,16,256]{2,1,0:T(8,128)(2,1)S(1)}, u32[]{:S(2)}, u32[]{:S(2)}) collective-permute-start(bf16[16,16,256]{2,1,0:T(8,128)(2,1)S(1)} %collective-permute-done.12.rest_5_), channel_id=1, source_target_pairs={{4,0},{8,4},{12,8},{14,12},{10,14},{6,10},{2,6},{0,2},{5,1},{9,5},... | collective-permute-start | bytes 393224 | tf_op jit(solution)/shard_map/ppermute | solution.py:288
  25.2 0.6 %collective-permute-done.6.rest_5_ = bf16[16,16,256]{2,1,0:T(8,128)(2,1)S(1)} collective-permute-done((bf16[16,16,256]{2,1,0:T(8,128)(2,1)S(1)}, bf16[16,16,256]{2,1,0:T(8,128)(2,1)S(1)}, u32[]{:S(2)}, u32[]{:S(2)}) %collective-permute-start.6) | collective-permute-done | bytes 131104 | tf_op jit(solution)/shard_map/ppermute | solution.py:282
  25.9 0.4 %collective-permute-done.3.rest_4_ = bf16[16,16,256]{2,1,0:T(8,128)(2,1)S(1)} collective-permute-done((bf16[16,16,256]{2,1,0:T(8,128)(2,1)S(1)}, bf16[16,16,256]{2,1,0:T(8,128)(2,1)S(1)}, u32[]{:S(2)}, u32[]{:S(2)}) %collective-permute-start.3) | collective-permute-done | bytes 131104 | tf_op jit(solution)/shard_map/ppermute | solution.py:279
  26.3 1.9 %span_weights.1.w_ref = bf16[5,2,896,256]{3,2,1,0:T(8,128)(2,1)S(1)} custom-call(s32[65]{0:T(128)S(4)} %get-tuple-element.12.slot_ref, bf16[5,256,512]{2,1,0:T(8,128)(2,1)S(1)} %get-tuple-element.13.placed, bf16[5,192,128]{2,1,0:T(8,128)(2,1)S(1)} %get-tuple-element.14.keep, bf16[5,256,128]{2,1,0:T(8,128)(2,1)S(1)} %get-tuple-element.15.bias, ...), custom_call_target="tpu_custom_call" | custom-call | flops 1174405120 | bytes 8388608 | tf_op jit(solution)/shard_map/span_weights/pallas_call | solution.py:239
  28.2 0.0 collective-permute-done.9.rest_3_
  28.2 0.7 %collective-permute-done.13.rest_4_ = bf16[16,16,256]{2,1,0:T(8,128)(2,1)S(1)} collective-permute-done((bf16[16,16,256]{2,1,0:T(8,128)(2,1)S(1)}, bf16[16,16,256]{2,1,0:T(8,128)(2,1)S(1)}, u32[]{:S(2)}, u32[]{:S(2)}) %collective-permute-start.13) | collective-permute-done | bytes 131104 | tf_op jit(solution)/shard_map/ppermute | solution.py:288
  28.9 2.3 %span_values.1 = (bf16[5,5,12,2048]{3,2,1,0:T(8,128)(2,1)}, bf16[5,32,2048]{2,1,0:T(8,128)(2,1)}) custom-call(s32[65]{0:T(128)S(4)} %get-tuple-element.12.slot_ref, bf16[5,2,896,256]{3,2,1,0:T(8,128)(2,1)S(1)} %span_weights.1.w_ref, bf16[5,256,512]{2,1,0:T(8,128)(2,1)S(1)} %get-tuple-element.13.placed, bf16[5,192,128]{2,1,0:T(8,128)(2,1)S(1)} %get-tuple-element.14.keep, ...), custom_call_target="tpu_custom_call" | custom-call | flops 1174405120 | bytes 8388608 | tf_op jit(solution)/shard_map/span_values/pallas_call | solution.py:249
Async XLA Ops:
  0.6 6.7 %collective-permute-start = (bf16[16,16,256]{2,1,0:T(8,128)(2,1)}, bf16[16,16,256]{2,1,0:T(8,128)(2,1)S(1)}, u32[]{:S(2)}, u32[]{:S(2)}) collective-permute-start(bf16[16,16,256]{2,1,0:T(8,128)(2,1)} %rest_10_.1), channel_id=1, source_target_pairs={{0,4},{4,8},{8,12},{12,14},{14,10},{10,6},{6,2},{2,0},{1,5},{5,9},... | collective-permute-start | bytes 393224 | tf_op jit(solution)/shard_map/ppermute | solution.py:279
  3.7 7.0 %collective-permute-start.10 = (bf16[16,16,256]{2,1,0:T(8,128)(2,1)}, bf16[16,16,256]{2,1,0:T(8,128)(2,1)S(1)}, u32[]{:S(2)}, u32[]{:S(2)}) collective-permute-start(bf16[16,16,256]{2,1,0:T(8,128)(2,1)} %rest_11_.1), channel_id=1, source_target_pairs={{4,0},{8,4},{12,8},{14,12},{10,14},{6,10},{2,6},{0,2},{5,1},{9,5},... | collective-permute-start | bytes 393224 | tf_op jit(solution)/shard_map/ppermute | solution.py:288
  3.7 10.2 %collective-permute-start.4 = (bf16[16,16,256]{2,1,0:T(8,128)(2,1)}, bf16[16,16,256]{2,1,0:T(8,128)(2,1)S(1)}, u32[]{:S(2)}, u32[]{:S(2)}) collective-permute-start(bf16[16,16,256]{2,1,0:T(8,128)(2,1)} %rest_10_.1), channel_id=1, source_target_pairs={{4,0},{8,4},{12,8},{14,12},{10,14},{6,10},{2,6},{0,2},{5,1},{9,5},... | collective-permute-start | bytes 393224 | tf_op jit(solution)/shard_map/ppermute | solution.py:282
  7.3 7.7 %collective-permute-start.1 = (bf16[16,16,256]{2,1,0:T(8,128)(2,1)S(1)}, bf16[16,16,256]{2,1,0:T(8,128)(2,1)S(1)}, u32[]{:S(2)}, u32[]{:S(2)}) collective-permute-start(bf16[16,16,256]{2,1,0:T(8,128)(2,1)S(1)} %collective-permute-done.rest_1_), channel_id=1, source_target_pairs={{0,4},{4,8},{8,12},{12,14},{14,10},{10,6},{6,2},{2,0},{1,5},{5,9},... | collective-permute-start | bytes 393224 | tf_op jit(solution)/shard_map/ppermute | solution.py:279
  9.2 6.8 %collective-permute-start.7 = (bf16[16,16,256]{2,1,0:T(8,128)(2,1)}, bf16[16,16,256]{2,1,0:T(8,128)(2,1)S(1)}, u32[]{:S(2)}, u32[]{:S(2)}) collective-permute-start(bf16[16,16,256]{2,1,0:T(8,128)(2,1)} %rest_11_.1), channel_id=1, source_target_pairs={{0,4},{4,8},{8,12},{12,14},{14,10},{10,6},{6,2},{2,0},{1,5},{5,9},... | collective-permute-start | bytes 393224 | tf_op jit(solution)/shard_map/ppermute | solution.py:286
  10.7 6.8 %collective-permute-start.11 = (bf16[16,16,256]{2,1,0:T(8,128)(2,1)S(1)}, bf16[16,16,256]{2,1,0:T(8,128)(2,1)S(1)}, u32[]{:S(2)}, u32[]{:S(2)}) collective-permute-start(bf16[16,16,256]{2,1,0:T(8,128)(2,1)S(1)} %collective-permute-done.10.rest_7_), channel_id=1, source_target_pairs={{4,0},{8,4},{12,8},{14,12},{10,14},{6,10},{2,6},{0,2},{5,1},{9,5},... | collective-permute-start | bytes 393224 | tf_op jit(solution)/shard_map/ppermute | solution.py:288
  13.9 6.4 %collective-permute-start.5 = (bf16[16,16,256]{2,1,0:T(8,128)(2,1)S(1)}, bf16[16,16,256]{2,1,0:T(8,128)(2,1)S(1)}, u32[]{:S(2)}, u32[]{:S(2)}) collective-permute-start(bf16[16,16,256]{2,1,0:T(8,128)(2,1)S(1)} %collective-permute-done.4.rest_7_), channel_id=1, source_target_pairs={{4,0},{8,4},{12,8},{14,12},{10,14},{6,10},{2,6},{0,2},{5,1},{9,5},... | collective-permute-start | bytes 393224 | tf_op jit(solution)/shard_map/ppermute | solution.py:282
  15.0 6.3 %collective-permute-start.2 = (bf16[16,16,256]{2,1,0:T(8,128)(2,1)S(1)}, bf16[16,16,256]{2,1,0:T(8,128)(2,1)S(1)}, u32[]{:S(2)}, u32[]{:S(2)}) collective-permute-start(bf16[16,16,256]{2,1,0:T(8,128)(2,1)S(1)} %collective-permute-done.1.rest_2_), channel_id=1, source_target_pairs={{0,4},{4,8},{8,12},{12,14},{14,10},{10,6},{6,2},{2,0},{1,5},{5,9},... | collective-permute-start | bytes 393224 | tf_op jit(solution)/shard_map/ppermute | solution.py:279
  16.0 7.0 %collective-permute-start.8 = (bf16[16,16,256]{2,1,0:T(8,128)(2,1)S(1)}, bf16[16,16,256]{2,1,0:T(8,128)(2,1)S(1)}, u32[]{:S(2)}, u32[]{:S(2)}) collective-permute-start(bf16[16,16,256]{2,1,0:T(8,128)(2,1)S(1)} %collective-permute-done.7.rest_1_), channel_id=1, source_target_pairs={{0,4},{4,8},{8,12},{12,14},{14,10},{10,6},{6,2},{2,0},{1,5},{5,9},... | collective-permute-start | bytes 393224 | tf_op jit(solution)/shard_map/ppermute | solution.py:286
  17.6 6.4 %collective-permute-start.12 = (bf16[16,16,256]{2,1,0:T(8,128)(2,1)S(1)}, bf16[16,16,256]{2,1,0:T(8,128)(2,1)S(1)}, u32[]{:S(2)}, u32[]{:S(2)}) collective-permute-start(bf16[16,16,256]{2,1,0:T(8,128)(2,1)S(1)} %collective-permute-done.11.rest_6_), channel_id=1, source_target_pairs={{4,0},{8,4},{12,8},{14,12},{10,14},{6,10},{2,6},{0,2},{5,1},{9,5},... | collective-permute-start | bytes 393224 | tf_op jit(solution)/shard_map/ppermute | solution.py:288
  20.3 5.5 %collective-permute-start.6 = (bf16[16,16,256]{2,1,0:T(8,128)(2,1)S(1)}, bf16[16,16,256]{2,1,0:T(8,128)(2,1)S(1)}, u32[]{:S(2)}, u32[]{:S(2)}) collective-permute-start(bf16[16,16,256]{2,1,0:T(8,128)(2,1)S(1)} %collective-permute-done.5.rest_6_), channel_id=1, source_target_pairs={{4,0},{8,4},{12,8},{14,12},{10,14},{6,10},{2,6},{0,2},{5,1},{9,5},... | collective-permute-start | bytes 393224 | tf_op jit(solution)/shard_map/ppermute | solution.py:282
  21.3 5.0 %collective-permute-start.3 = (bf16[16,16,256]{2,1,0:T(8,128)(2,1)S(1)}, bf16[16,16,256]{2,1,0:T(8,128)(2,1)S(1)}, u32[]{:S(2)}, u32[]{:S(2)}) collective-permute-start(bf16[16,16,256]{2,1,0:T(8,128)(2,1)S(1)} %collective-permute-done.2.rest_3_), channel_id=1, source_target_pairs={{0,4},{4,8},{8,12},{12,14},{14,10},{10,6},{6,2},{2,0},{1,5},{5,9},... | collective-permute-start | bytes 393224 | tf_op jit(solution)/shard_map/ppermute | solution.py:279
  23.0 5.1 %collective-permute-start.9 = (bf16[16,16,256]{2,1,0:T(8,128)(2,1)S(1)}, bf16[16,16,256]{2,1,0:T(8,128)(2,1)S(1)}, u32[]{:S(2)}, u32[]{:S(2)}) collective-permute-start(bf16[16,16,256]{2,1,0:T(8,128)(2,1)S(1)} %collective-permute-done.8.rest_2_), channel_id=1, source_target_pairs={{0,4},{4,8},{8,12},{12,14},{14,10},{10,6},{6,2},{2,0},{1,5},{5,9},... | collective-permute-start | bytes 393224 | tf_op jit(solution)/shard_map/ppermute | solution.py:286
  23.9 5.0 %collective-permute-start.13 = (bf16[16,16,256]{2,1,0:T(8,128)(2,1)S(1)}, bf16[16,16,256]{2,1,0:T(8,128)(2,1)S(1)}, u32[]{:S(2)}, u32[]{:S(2)}) collective-permute-start(bf16[16,16,256]{2,1,0:T(8,128)(2,1)S(1)} %collective-permute-done.12.rest_5_), channel_id=1, source_target_pairs={{4,0},{8,4},{12,8},{14,12},{10,14},{6,10},{2,6},{0,2},{5,1},{9,5},... | collective-permute-start | bytes 393224 | tf_op jit(solution)/shard_map/ppermute | solution.py:288

commit v4 on v3

--- a/solution.py
+++ b/solution.py
@@ -16,9 +16,10 @@
 
 
 def fill_pool(pieces, pool):
-    rows = pieces[0].shape[0]
-    for b, piece in enumerate(pieces):
-        pool[b * rows : (b + 1) * rows] = piece[...]
+    row = 0
+    for piece in pieces:
+        pool[row : row + piece.shape[0]] = piece[...]
+        row += piece.shape[0]
 
 
 def blend(first, slot_ref, pool, placed, keep, blended):
@@ -35,12 +36,11 @@
     count, place_ref, *rest
 ):
     sources, rest = rest[:12], rest[12:]
-    scalars, own_k, own_v, placed, keep, bias, queries, *rest = rest
-    spans_ref, home_ref, sel_ref, length_ref, fk, fv, qk, qv, fq, qq, rows, limits, sems = rest
+    scalars, own_k, own_v, placed, keep, bias, fq, qq, *rest = rest
+    spans_ref, home_ref, sel_ref, length_ref, fk, fv, qk, qv, rows, limits, sems = rest
     req_count, picks, lists, width = fk.shape
     q_rows = qk.shape[1]
     spans_dev, span_len, _ = own_k.shape
-    kv_heads, heads = queries.shape[1], queries.shape[2]
     total = lists * span_len
     copies = [
         pltpu.make_async_copy(source, target, sems.at[n])
@@ -55,7 +55,6 @@
     for copy in copies:
         copy.start()
     rows[...] = jnp.zeros_like(rows)
-    queries[...] = jnp.zeros_like(queries)
     lane = lax.broadcasted_iota(jnp.int32, (1, LANES), 1)
     asked_at = lane - picks * ROW_TILE
     blank = jnp.where((asked_at >= 0) & (asked_at < q_rows), total + asked_at, -1)
@@ -94,18 +93,13 @@
         bias[r] = jnp.where(key <= limit, 0.0, MASKED).astype(jnp.bfloat16)
     for copy in copies[8:]:
         copy.wait()
-    for r in range(req_count):
-        for g in range(kv_heads):
-            for h in range(heads):
-                at = (g * heads + h) * HEAD
-                queries[r, g, h, 0:picks, 0:lists, :] = fq[r, :, :, at : at + HEAD]
-                queries[r, g, h, picks:, :, :] = qq[r, :, at : at + HEAD].reshape(-1, ROW_TILE, HEAD)
-
-
-def weights_kernel(n_buf, lists, slot_ref, placed, keep, bias, queries, *rest):
+
+
+def weights_kernel(n_buf, slot_ref, placed, keep, bias, fq, qq, *rest):
     pieces = rest[:n_buf]
-    out_ref, pool, blended, units = rest[n_buf:]
-    req_count, kv_heads, heads, tiles = queries.shape[:4]
+    out_ref, pool, blended, units, queries = rest[n_buf:]
+    req_count, picks, lists, _ = fq.shape
+    kv_heads, heads, tiles = queries.shape[:3]
     rows_head = tiles * ROW_TILE
     width = blended.shape[1]
     row = lax.broadcasted_iota(jnp.int32, (rows_head, LANES), 0)
@@ -119,7 +113,11 @@
         blend(r * lists, slot_ref, pool, placed.at[r, :, 0:width], keep.at[r], blended)
         for g in range(kv_heads):
             table = jnp.concatenate([blended[:, g * HEAD : (g + 1) * HEAD], bias[r]], axis=1)
-            stacked = queries[r, g].reshape(heads * rows_head, HEAD)
+            for h in range(heads):
+                at = (g * heads + h) * HEAD
+                queries[g, h, 0:picks, 0:lists, :] = fq[r, :, :, at : at + HEAD]
+                queries[g, h, picks:, :, :] = qq[r, :, at : at + HEAD].reshape(-1, ROW_TILE, HEAD)
+            stacked = queries[g].reshape(heads * rows_head, HEAD)
             scores = lax.dot_general(
                 jnp.concatenate([stacked, units[...]], axis=1),
                 table,
@@ -190,20 +188,19 @@
 
 def prepare(place, spans, home, sel, lengths, cache_k, cache_v, fresh_q, fresh_k, fresh_v, question_q, question_k, question_v):
     count = lax.axis_size("dp")
-    req_count, picks, lists, q_width = fresh_q.shape
+    req_count, picks, lists, _ = fresh_q.shape
     _, span_len, width = cache_k.shape
     q_rows = question_q.shape[1]
-    kv_heads, heads = width // HEAD, q_width // width
     total = lists * span_len
     padded = -(-(total + q_rows) // LANES) * LANES
     near = (spans, home, sel, lengths)
-    held = (fresh_k, fresh_v, question_k, question_v, fresh_q, question_q)
-    far = near + held + (cache_k, cache_v)
+    held = (fresh_k, fresh_v, question_k, question_v)
+    far = near + held + (fresh_q, question_q, cache_k, cache_v)
     bf16 = jnp.bfloat16
     return pl.pallas_call(
         functools.partial(prepare_kernel, count),
         in_specs=[SMEM_SPEC] + [HBM_SPEC] * len(far),
-        out_specs=[SMEM_SPEC] + [VMEM_SPEC] * 6,
+        out_specs=[SMEM_SPEC] + [VMEM_SPEC] * 7,
         out_shape=[
             pltpu.SMEM((req_count * lists + req_count,), jnp.int32),
             like(cache_k),
@@ -211,7 +208,8 @@
             pltpu.VMEM((req_count, padded, 2 * width), bf16),
             pltpu.VMEM((req_count, total, LANES), bf16),
             pltpu.VMEM((req_count, padded, LANES), bf16),
-            pltpu.VMEM((req_count, kv_heads, heads, picks + q_rows // ROW_TILE, ROW_TILE, HEAD), bf16),
+            like(fresh_q),
+            like(question_q),
         ],
         scratch_shapes=[pltpu.SMEM(x.shape, x.dtype) for x in near]
         + [like(x) for x in held]
@@ -226,40 +224,43 @@
     )(place, *map(in_hbm, far))
 
 
-def attend(scalars, placed, keep, bias, queries, k_pieces, v_pieces, redone_shape, spoken_shape):
-    req_count, _, lists, _ = redone_shape
-    piece_rows, span_len, width = k_pieces[0].shape
+def attend(scalars, placed, keep, bias, fresh_q, question_q, k_pieces, v_pieces):
+    req_count, picks, _, q_width = fresh_q.shape
+    _, span_len, width = k_pieces[0].shape
     n_buf = len(k_pieces)
-    kv_heads, heads, tiles = queries.shape[1:4]
+    kv_heads, heads = width // HEAD, q_width // width
+    tiles = picks + question_q.shape[1] // ROW_TILE
     padded = placed.shape[1]
-    pool = pltpu.VMEM((n_buf * piece_rows, span_len, width), jnp.bfloat16)
+    pool = pltpu.VMEM((sum(x.shape[0] for x in k_pieces), span_len, width), jnp.bfloat16)
     blended = pltpu.VMEM((padded, width), jnp.bfloat16)
     w_shape = (req_count, kv_heads, heads * tiles * ROW_TILE, padded)
     flops = 4 * req_count * kv_heads * heads * tiles * ROW_TILE * padded * HEAD
     weights = pl.pallas_call(
-        functools.partial(weights_kernel, n_buf, lists),
-        in_specs=[SMEM_SPEC] + [VMEM_SPEC] * (4 + n_buf),
+        functools.partial(weights_kernel, n_buf),
+        in_specs=[SMEM_SPEC] + [VMEM_SPEC] * (5 + n_buf),
         out_specs=VMEM_SPEC,
-        scratch_shapes=[pool, blended, pltpu.VMEM((heads * tiles * ROW_TILE, LANES), jnp.bfloat16)],
+        scratch_shapes=[pool, blended, pltpu.VMEM((heads * tiles * ROW_TILE, LANES), jnp.bfloat16)]
+        + [pltpu.VMEM((kv_heads, heads, tiles, ROW_TILE, HEAD), jnp.bfloat16)],
         out_shape=pltpu.VMEM(w_shape, jnp.bfloat16),
         compiler_params=PARAMS,
         cost_estimate=pl.CostEstimate(flops=flops, bytes_accessed=8 << 20, transcendentals=flops // 512),
         name="span_weights",
-    )(scalars, *map(in_vmem, (placed, keep, bias, queries)), *map(in_vmem, k_pieces))
+    )(scalars, *map(in_vmem, (placed, keep, bias, fresh_q, question_q)), *map(in_vmem, k_pieces))
+    n_buf = len(v_pieces)
     return pl.pallas_call(
         functools.partial(values_kernel, n_buf),
         in_specs=[SMEM_SPEC] + [VMEM_SPEC] * (3 + n_buf),
         out_specs=[HBM_SPEC, HBM_SPEC],
         scratch_shapes=[
-            pltpu.VMEM(redone_shape, jnp.bfloat16),
-            pltpu.VMEM(spoken_shape, jnp.bfloat16),
+            like(fresh_q),
+            like(question_q),
             pool,
             blended,
             pltpu.SemaphoreType.DMA((2 * req_count,)),
         ],
         out_shape=[
-            jax.ShapeDtypeStruct(redone_shape, jnp.bfloat16),
-            jax.ShapeDtypeStruct(spoken_shape, jnp.bfloat16),
+            jax.ShapeDtypeStruct(fresh_q.shape, jnp.bfloat16),
+            jax.ShapeDtypeStruct(question_q.shape, jnp.bfloat16),
         ],
         compiler_params=PARAMS,
         cost_estimate=pl.CostEstimate(flops=flops, bytes_accessed=8 << 20, transcendentals=0),
@@ -271,23 +272,29 @@
     order = list(range(0, count, 2)) + list(range(1, count, 2))[::-1]
     onward = [(order[i], order[(i + 1) % count]) for i in range(count)]
     back = [(b, a) for a, b in onward]
-    k_at, v_at = {0: keys}, {0: values}
+    half, rest = count // 2, (count - 1) // 2
+    cut = keys.shape[0] // 2
+    k_at, v_at = {0: [keys]}, {0: [values]}
     k_on = k_back = keys
     v_on = v_back = values
-    half, rest = count // 2, (count - 1) // 2
-    for hop in range(1, half + 1):
+    for hop in range(1, rest + 1):
         k_on = lax.ppermute(k_on, "dp", onward)
-        k_at[hop] = k_on
-        if hop <= rest:
-            k_back = lax.ppermute(k_back, "dp", back)
-            k_at[count - hop] = k_back
-            if hop == 1:
-                k_back, _ = lax.optimization_barrier((k_back, ready))
-            v_on = lax.ppermute(v_on, "dp", onward)
-            v_at[hop] = v_on
+        k_at[hop] = [k_on]
+        k_back = lax.ppermute(k_back, "dp", back)
+        k_at[count - hop] = [k_back]
+        if hop == 1:
+            k_back, _ = lax.optimization_barrier((k_back, ready))
+        v_on = lax.ppermute(v_on, "dp", onward)
+        v_at[hop] = [v_on]
         v_back = lax.ppermute(v_back, "dp", back)
-        v_at[count - hop] = v_back
-    return [k_at[d] for d in range(count)], [v_at[d] for d in range(count)]
+        v_at[count - hop] = [v_back]
+    if half > rest:
+        k_at[half] = [lax.ppermute(k_on, "dp", onward)]
+        v_at[half] = [lax.ppermute(v_back, "dp", back)]
+    gathered = []
+    for at in (k_at, v_at):
+        gathered.append([piece for d in range(count) for piece in at[d]])
+    return gathered
 
 
 def asked_gather(keys, values, positions, spans_dev, count):
@@ -326,7 +333,7 @@
     turned_q, turned_k, turned_v = [jnp.transpose(x, (0, 2, 1, 3)) for x in (fresh_q, fresh_k, fresh_v)]
     me = lax.axis_index("dp")
     place = jnp.where(me % 2 == 0, me // 2, count - 1 - me // 2).astype(jnp.int32).reshape(1)
-    scalars, own_k, own_v, placed, keep, bias, queries = prepare(
+    scalars, own_k, own_v, placed, keep, bias, held_q, asked_q = prepare(
         place,
         request_spans,
         span_home,
@@ -352,7 +359,7 @@
         slots, k_pieces, v_pieces = asked_gather(cache_k, cache_v, positions, spans_dev, count)
         scalars = jnp.concatenate([slots, question_len])
     redone, spoken = attend(
-        scalars, placed, keep, bias, queries, k_pieces, v_pieces, turned_q.shape, question_q.shape
+        scalars, placed, keep, bias, held_q, asked_q, k_pieces, v_pieces
     )
     return jnp.transpose(redone, (0, 2, 1, 3)), spoken
 

time: 31.4 us -> 31.1 us (level)
  waiting for transfers between devices: 6.48 us -> 5.88 us
    ppermute x0 -> x2, starting transfers between devices: none -> 2.12 us  [the longest x1 1.37 us: ring_gather(): k_at[half] = [lax.ppermute(k_on, 'dp', onward)]]
    ppermute x4 -> x3, starting transfers between devices: 2.18 us -> 0.9 us  [ring_gather(): v_back = lax.ppermute(v_back, 'dp', back)]
    ppermute x4 -> x3, starting transfers between devices: 6.93 us -> 5.89 us  [ring_gather(): k_on = lax.ppermute(k_on, 'dp', onward)]
    ppermute x4 -> x3, waiting for transfers between devices: 0.76 us -> 0.01 us  [ring_gather(): v_back = lax.ppermute(v_back, 'dp', back)]
    ppermute x3, waiting for transfers between devices: 0.67 us -> 0.01 us  [ring_gather(): v_on = lax.ppermute(v_on, 'dp', onward)]
    ppermute x0 -> x2, waiting for transfers between devices: none -> 0.66 us  [the longest x1 0.55 us: ring_gather(): v_at[half] = [lax.ppermute(v_back, 'dp', back)]]
    ppermute x3, starting transfers between devices: 4.07 us -> 4.73 us  [ring_gather(): v_on = lax.ppermute(v_on, 'dp', onward)]
    ppermute x3, waiting for transfers between devices: 2.96 us -> 3.53 us  [ring_gather(): k_back = lax.ppermute(k_back, 'dp', back)]
  transfers between devices with their start and end apart: 14 -> 14, of which waited for: 6 -> 5; matrix products, arithmetic and copies ran while one was open for 0% -> 0% of each run, Pallas kernels for 15% -> 15%
where the time goes in v4:
time: 31.1 us; the launch traced here: 30.9 us
  starting transfers between devices  17.3 us (56%)
  Pallas kernels  7.01 us (23%)
  waiting for transfers between devices  5.88 us (19%)
  between operations  0.68 us (2%)
    ppermute x3, starting transfers between devices, ring_gather(): k_on = lax.ppermute(k_on, 'dp', onward)  5.89 us
    ppermute x3, starting transfers between devices, ring_gather(): v_on = lax.ppermute(v_on, 'dp', onward)  4.73 us
    ppermute x3, starting transfers between devices, ring_gather(): k_back = lax.ppermute(k_back, 'dp', back)  3.68 us
    ppermute x3, waiting for transfers between devices, ring_gather(): k_back = lax.ppermute(k_back, 'dp', back)  3.53 us
    pallas_call x1, Pallas kernels, attend(): pl.pallas_call(functools.partial(weights_kernel, n_buf), in_specs=[SMEM_S...  2.39 us
    pallas_call x1, Pallas kernels, attend(): pl.pallas_call(functools.partial(values_kernel, n_buf), in_specs=[SMEM_SP...  2.32 us
    pallas_call x1, Pallas kernels, prepare(): pl.pallas_call(functools.partial(prepare_kernel, count), in_specs=[SMEM_S...  2.3 us
    ppermute x3, waiting for transfers between devices, ring_gather(): k_on = lax.ppermute(k_on, 'dp', onward)  1.68 us
  transfers between devices with their start and end apart: 14, of which 5 were waited for; matrix products, arithmetic and copies ran while one was open for 0% of the time, Pallas kernels for 15%

profile of v4, /device:TPU:0, one launch (start us, length us, event | category | flops | bytes accessed | tf_op | source)
XLA Modules:
  0.0 30.9 jit_solution(9848063725166252782)
XLA Ops:
  0.6 3.1 %collective-permute-start = (bf16[16,16,256]{2,1,0:T(8,128)(2,1)}, bf16[16,16,256]{2,1,0:T(8,128)(2,1)S(1)}, u32[]{:S(2)}, u32[]{:S(2)}) collective-permute-start(bf16[16,16,256]{2,1,0:T(8,128)(2,1)} %rest_10_.1), channel_id=1, source_target_pairs={{0,4},{4,8},{8,12},{12,14},{14,10},{10,6},{6,2},{2,0},{1,5},{5,9},... | collective-permute-start | bytes 393224 | tf_op jit(solution)/shard_map/ppermute | solution.py:281
  3.7 0.0 collective-permute-start.10
  3.7 1.9 %collective-permute-start.4 = (bf16[16,16,256]{2,1,0:T(8,128)(2,1)}, bf16[16,16,256]{2,1,0:T(8,128)(2,1)S(1)}, u32[]{:S(2)}, u32[]{:S(2)}) collective-permute-start(bf16[16,16,256]{2,1,0:T(8,128)(2,1)} %rest_10_.1), channel_id=1, source_target_pairs={{4,0},{8,4},{12,8},{14,12},{10,14},{6,10},{2,6},{0,2},{5,1},{9,5},... | collective-permute-start | bytes 393224 | tf_op jit(solution)/shard_map/ppermute | solution.py:283
  5.7 1.7 %collective-permute-done.rest_1_ = bf16[16,16,256]{2,1,0:T(8,128)(2,1)S(1)} collective-permute-done((bf16[16,16,256]{2,1,0:T(8,128)(2,1)}, bf16[16,16,256]{2,1,0:T(8,128)(2,1)S(1)}, u32[]{:S(2)}, u32[]{:S(2)}) %collective-permute-start) | collective-permute-done | bytes 131104 | tf_op jit(solution)/shard_map/ppermute | solution.py:281
  7.3 1.8 %collective-permute-start.1 = (bf16[16,16,256]{2,1,0:T(8,128)(2,1)S(1)}, bf16[16,16,256]{2,1,0:T(8,128)(2,1)S(1)}, u32[]{:S(2)}, u32[]{:S(2)}) collective-permute-start(bf16[16,16,256]{2,1,0:T(8,128)(2,1)S(1)} %collective-permute-done.rest_1_), channel_id=1, source_target_pairs={{0,4},{4,8},{8,12},{12,14},{14,10},{10,6},{6,2},{2,0},{1,5},{5,9},... | collective-permute-start | bytes 393224 | tf_op jit(solution)/shard_map/ppermute | solution.py:281
  9.2 1.6 %collective-permute-start.7 = (bf16[16,16,256]{2,1,0:T(8,128)(2,1)}, bf16[16,16,256]{2,1,0:T(8,128)(2,1)S(1)}, u32[]{:S(2)}, u32[]{:S(2)}) collective-permute-start(bf16[16,16,256]{2,1,0:T(8,128)(2,1)} %rest_11_.1), channel_id=1, source_target_pairs={{0,4},{4,8},{8,12},{12,14},{14,10},{10,6},{6,2},{2,0},{1,5},{5,9},... | collective-permute-start | bytes 393224 | tf_op jit(solution)/shard_map/ppermute | solution.py:287
  10.7 0.0 collective-permute-done.10.rest_7_
  10.7 0.4 %collective-permute-start.11 = (bf16[16,16,256]{2,1,0:T(8,128)(2,1)S(1)}, bf16[16,16,256]{2,1,0:T(8,128)(2,1)S(1)}, u32[]{:S(2)}, u32[]{:S(2)}) collective-permute-start(bf16[16,16,256]{2,1,0:T(8,128)(2,1)S(1)} %collective-permute-done.10.rest_7_), channel_id=1, source_target_pairs={{4,0},{8,4},{12,8},{14,12},{10,14},{6,10},{2,6},{0,2},{5,1},{9,5},... | collective-permute-start | bytes 393224 | tf_op jit(solution)/shard_map/ppermute | solution.py:289
  11.2 2.3 %span_prepare.1 = (s32[65]{0:T(128)S(4)}, bf16[16,16,256]{2,1,0:T(8,128)(2,1)S(1)}, bf16[16,16,256]{2,1,0:T(8,128)(2,1)S(1)}, bf16[5,256,512]{2,1,0:T(8,128)(2,1...) custom-call(s32[1]{0:T(128)} %bitcast.place_ref, ...), custom_call_target="tpu_custom_call" | custom-call | bytes 8388608 | tf_op jit(solution)/shard_map/span_prepare/pallas_call | solution.py:200
  13.5 0.0 collective-permute-done.4.rest_7_
  13.5 1.1 %collective-permute-start.5 = (bf16[16,16,256]{2,1,0:T(8,128)(2,1)S(1)}, bf16[16,16,256]{2,1,0:T(8,128)(2,1)S(1)}, u32[]{:S(2)}, u32[]{:S(2)}) collective-permute-start(bf16[16,16,256]{2,1,0:T(8,128)(2,1)S(1)} %collective-permute-done.4.rest_7_), channel_id=1, source_target_pairs={{4,0},{8,4},{12,8},{14,12},{10,14},{6,10},{2,6},{0,2},{5,1},{9,5},... | collective-permute-start | bytes 393224 | tf_op jit(solution)/shard_map/ppermute | solution.py:283
  14.6 0.0 collective-permute-done.1.rest_2_
  14.6 1.0 %collective-permute-start.2 = (bf16[16,16,256]{2,1,0:T(8,128)(2,1)S(1)}, bf16[16,16,256]{2,1,0:T(8,128)(2,1)S(1)}, u32[]{:S(2)}, u32[]{:S(2)}) collective-permute-start(bf16[16,16,256]{2,1,0:T(8,128)(2,1)S(1)} %collective-permute-done.1.rest_2_), channel_id=1, source_target_pairs={{0,4},{4,8},{8,12},{12,14},{14,10},{10,6},{6,2},{2,0},{1,5},{5,9},... | collective-permute-start | bytes 393224 | tf_op jit(solution)/shard_map/ppermute | solution.py:281
  15.6 0.0 collective-permute-done.7.rest_1_
  15.6 1.6 %collective-permute-start.8 = (bf16[16,16,256]{2,1,0:T(8,128)(2,1)S(1)}, bf16[16,16,256]{2,1,0:T(8,128)(2,1)S(1)}, u32[]{:S(2)}, u32[]{:S(2)}) collective-permute-start(bf16[16,16,256]{2,1,0:T(8,128)(2,1)S(1)} %collective-permute-done.7.rest_1_), channel_id=1, source_target_pairs={{0,4},{4,8},{8,12},{12,14},{14,10},{10,6},{6,2},{2,0},{1,5},{5,9},... | collective-permute-start | bytes 393224 | tf_op jit(solution)/shard_map/ppermute | solution.py:287
  17.2 0.0 collective-permute-done.11.rest_6_
  17.2 0.4 %collective-permute-start.12 = (bf16[16,16,256]{2,1,0:T(8,128)(2,1)S(1)}, bf16[16,16,256]{2,1,0:T(8,128)(2,1)S(1)}, u32[]{:S(2)}, u32[]{:S(2)}) collective-permute-start(bf16[16,16,256]{2,1,0:T(8,128)(2,1)S(1)} %collective-permute-done.11.rest_6_), channel_id=1, source_target_pairs={{4,0},{8,4},{12,8},{14,12},{10,14},{6,10},{2,6},{0,2},{5,1},{9,5},... | collective-permute-start | bytes 393224 | tf_op jit(solution)/shard_map/ppermute | solution.py:289
  17.6 2.4 %collective-permute-done.5.rest_6_ = bf16[16,16,256]{2,1,0:T(8,128)(2,1)S(1)} collective-permute-done((bf16[16,16,256]{2,1,0:T(8,128)(2,1)S(1)}, bf16[16,16,256]{2,1,0:T(8,128)(2,1)S(1)}, u32[]{:S(2)}, u32[]{:S(2)}) %collective-permute-start.5) | collective-permute-done | bytes 131104 | tf_op jit(solution)/shard_map/ppermute | solution.py:283
  20.0 0.7 %collective-permute-start.6 = (bf16[16,16,256]{2,1,0:T(8,128)(2,1)S(1)}, bf16[16,16,256]{2,1,0:T(8,128)(2,1)S(1)}, u32[]{:S(2)}, u32[]{:S(2)}) collective-permute-start(bf16[16,16,256]{2,1,0:T(8,128)(2,1)S(1)} %collective-permute-done.5.rest_6_), channel_id=1, source_target_pairs={{4,0},{8,4},{12,8},{14,12},{10,14},{6,10},{2,6},{0,2},{5,1},{9,5},... | collective-permute-start | bytes 393224 | tf_op jit(solution)/shard_map/ppermute | solution.py:283
  20.6 0.0 collective-permute-done.2.rest_3_
  20.6 1.4 %collective-permute-start.3 = (bf16[16,16,256]{2,1,0:T(8,128)(2,1)S(1)}, bf16[16,16,256]{2,1,0:T(8,128)(2,1)S(1)}, u32[]{:S(2)}, u32[]{:S(2)}) collective-permute-start(bf16[16,16,256]{2,1,0:T(8,128)(2,1)S(1)} %collective-permute-done.2.rest_3_), channel_id=1, source_target_pairs={{0,4},{4,8},{8,12},{12,14},{14,10},{10,6},{6,2},{2,0},{1,5},{5,9},... | collective-permute-start | bytes 393224 | tf_op jit(solution)/shard_map/ppermute | solution.py:292
  22.0 0.0 collective-permute-done.8.rest_2_
  22.0 1.6 %collective-permute-start.9 = (bf16[16,16,256]{2,1,0:T(8,128)(2,1)S(1)}, bf16[16,16,256]{2,1,0:T(8,128)(2,1)S(1)}, u32[]{:S(2)}, u32[]{:S(2)}) collective-permute-start(bf16[16,16,256]{2,1,0:T(8,128)(2,1)S(1)} %collective-permute-done.8.rest_2_), channel_id=1, source_target_pairs={{0,4},{4,8},{8,12},{12,14},{14,10},{10,6},{6,2},{2,0},{1,5},{5,9},... | collective-permute-start | bytes 393224 | tf_op jit(solution)/shard_map/ppermute | solution.py:287
  23.6 0.0 collective-permute-done.12.rest_5_
  23.6 0.7 %collective-permute-start.13 = (bf16[16,16,256]{2,1,0:T(8,128)(2,1)S(1)}, bf16[16,16,256]{2,1,0:T(8,128)(2,1)S(1)}, u32[]{:S(2)}, u32[]{:S(2)}) collective-permute-start(bf16[16,16,256]{2,1,0:T(8,128)(2,1)S(1)} %collective-permute-done.12.rest_5_), channel_id=1, source_target_pairs={{4,0},{8,4},{12,8},{14,12},{10,14},{6,10},{2,6},{0,2},{5,1},{9,5},... | collective-permute-start | bytes 393224 | tf_op jit(solution)/shard_map/ppermute | solution.py:293
  24.4 1.1 %collective-permute-done.6.rest_5_ = bf16[16,16,256]{2,1,0:T(8,128)(2,1)S(1)} collective-permute-done((bf16[16,16,256]{2,1,0:T(8,128)(2,1)S(1)}, bf16[16,16,256]{2,1,0:T(8,128)(2,1)S(1)}, u32[]{:S(2)}, u32[]{:S(2)}) %collective-permute-start.6) | collective-permute-done | bytes 131104 | tf_op jit(solution)/shard_map/ppermute | solution.py:283
  25.5 0.1 collective-permute-done.3.rest_4_
  25.6 2.4 %span_weights.1.w_ref = bf16[5,2,896,256]{3,2,1,0:T(8,128)(2,1)S(1)} custom-call(s32[65]{0:T(128)S(4)} %get-tuple-element.13.slot_ref, bf16[5,256,512]{2,1,0:T(8,128)(2,1)S(1)} %get-tuple-element.14.placed, bf16[5,192,128]{2,1,0:T(8,128)(2,1)S(1)} %get-tuple-element.15.keep, bf16[5,256,128]{2,1,0:T(8,128)(2,1)S(1)} %get-tuple-element.16.bias, ...), custom_call_target="tpu_custom_call" | custom-call | flops 1174405120 | bytes 8388608 | tf_op jit(solution)/shard_map/span_weights/pallas_call | solution.py:238
  28.0 0.0 collective-permute-done.9.rest_3_
  28.0 0.5 %collective-permute-done.13.rest_4_ = bf16[16,16,256]{2,1,0:T(8,128)(2,1)S(1)} collective-permute-done((bf16[16,16,256]{2,1,0:T(8,128)(2,1)S(1)}, bf16[16,16,256]{2,1,0:T(8,128)(2,1)S(1)}, u32[]{:S(2)}, u32[]{:S(2)}) %collective-permute-start.13) | collective-permute-done | bytes 131104 | tf_op jit(solution)/shard_map/ppermute | solution.py:293
  28.6 2.3 %span_values.1 = (bf16[5,5,12,2048]{3,2,1,0:T(8,128)(2,1)}, bf16[5,32,2048]{2,1,0:T(8,128)(2,1)}) custom-call(s32[65]{0:T(128)S(4)} %get-tuple-element.13.slot_ref, bf16[5,2,896,256]{3,2,1,0:T(8,128)(2,1)S(1)} %span_weights.1.w_ref, bf16[5,256,512]{2,1,0:T(8,128)(2,1)S(1)} %get-tuple-element.14.placed, bf16[5,192,128]{2,1,0:T(8,128)(2,1)S(1)} %get-tuple-element.15.keep, ...), custom_call_target="tpu_custom_call" | custom-call | flops 1174405120 | bytes 8388608 | tf_op jit(solution)/shard_map/span_values/pallas_call | solution.py:250
Async XLA Ops:
  0.6 6.7 %collective-permute-start = (bf16[16,16,256]{2,1,0:T(8,128)(2,1)}, bf16[16,16,256]{2,1,0:T(8,128)(2,1)S(1)}, u32[]{:S(2)}, u32[]{:S(2)}) collective-permute-start(bf16[16,16,256]{2,1,0:T(8,128)(2,1)} %rest_10_.1), channel_id=1, source_target_pairs={{0,4},{4,8},{8,12},{12,14},{14,10},{10,6},{6,2},{2,0},{1,5},{5,9},... | collective-permute-start | bytes 393224 | tf_op jit(solution)/shard_map/ppermute | solution.py:281
  3.7 7.0 %collective-permute-start.10 = (bf16[16,16,256]{2,1,0:T(8,128)(2,1)}, bf16[16,16,256]{2,1,0:T(8,128)(2,1)S(1)}, u32[]{:S(2)}, u32[]{:S(2)}) collective-permute-start(bf16[16,16,256]{2,1,0:T(8,128)(2,1)} %rest_11_.1), channel_id=1, source_target_pairs={{4,0},{8,4},{12,8},{14,12},{10,14},{6,10},{2,6},{0,2},{5,1},{9,5},... | collective-permute-start | bytes 393224 | tf_op jit(solution)/shard_map/ppermute | solution.py:289
  3.7 9.8 %collective-permute-start.4 = (bf16[16,16,256]{2,1,0:T(8,128)(2,1)}, bf16[16,16,256]{2,1,0:T(8,128)(2,1)S(1)}, u32[]{:S(2)}, u32[]{:S(2)}) collective-permute-start(bf16[16,16,256]{2,1,0:T(8,128)(2,1)} %rest_10_.1), channel_id=1, source_target_pairs={{4,0},{8,4},{12,8},{14,12},{10,14},{6,10},{2,6},{0,2},{5,1},{9,5},... | collective-permute-start | bytes 393224 | tf_op jit(solution)/shard_map/ppermute | solution.py:283
  7.3 7.3 %collective-permute-start.1 = (bf16[16,16,256]{2,1,0:T(8,128)(2,1)S(1)}, bf16[16,16,256]{2,1,0:T(8,128)(2,1)S(1)}, u32[]{:S(2)}, u32[]{:S(2)}) collective-permute-start(bf16[16,16,256]{2,1,0:T(8,128)(2,1)S(1)} %collective-permute-done.rest_1_), channel_id=1, source_target_pairs={{0,4},{4,8},{8,12},{12,14},{14,10},{10,6},{6,2},{2,0},{1,5},{5,9},... | collective-permute-start | bytes 393224 | tf_op jit(solution)/shard_map/ppermute | solution.py:281
  9.2 6.4 %collective-permute-start.7 = (bf16[16,16,256]{2,1,0:T(8,128)(2,1)}, bf16[16,16,256]{2,1,0:T(8,128)(2,1)S(1)}, u32[]{:S(2)}, u32[]{:S(2)}) collective-permute-start(bf16[16,16,256]{2,1,0:T(8,128)(2,1)} %rest_11_.1), channel_id=1, source_target_pairs={{0,4},{4,8},{8,12},{12,14},{14,10},{10,6},{6,2},{2,0},{1,5},{5,9},... | collective-permute-start | bytes 393224 | tf_op jit(solution)/shard_map/ppermute | solution.py:287
  10.7 6.4 %collective-permute-start.11 = (bf16[16,16,256]{2,1,0:T(8,128)(2,1)S(1)}, bf16[16,16,256]{2,1,0:T(8,128)(2,1)S(1)}, u32[]{:S(2)}, u32[]{:S(2)}) collective-permute-start(bf16[16,16,256]{2,1,0:T(8,128)(2,1)S(1)} %collective-permute-done.10.rest_7_), channel_id=1, source_target_pairs={{4,0},{8,4},{12,8},{14,12},{10,14},{6,10},{2,6},{0,2},{5,1},{9,5},... | collective-permute-start | bytes 393224 | tf_op jit(solution)/shard_map/ppermute | solution.py:289
  13.5 6.5 %collective-permute-start.5 = (bf16[16,16,256]{2,1,0:T(8,128)(2,1)S(1)}, bf16[16,16,256]{2,1,0:T(8,128)(2,1)S(1)}, u32[]{:S(2)}, u32[]{:S(2)}) collective-permute-start(bf16[16,16,256]{2,1,0:T(8,128)(2,1)S(1)} %collective-permute-done.4.rest_7_), channel_id=1, source_target_pairs={{4,0},{8,4},{12,8},{14,12},{10,14},{6,10},{2,6},{0,2},{5,1},{9,5},... | collective-permute-start | bytes 393224 | tf_op jit(solution)/shard_map/ppermute | solution.py:283
  14.6 6.1 %collective-permute-start.2 = (bf16[16,16,256]{2,1,0:T(8,128)(2,1)S(1)}, bf16[16,16,256]{2,1,0:T(8,128)(2,1)S(1)}, u32[]{:S(2)}, u32[]{:S(2)}) collective-permute-start(bf16[16,16,256]{2,1,0:T(8,128)(2,1)S(1)} %collective-permute-done.1.rest_2_), channel_id=1, source_target_pairs={{0,4},{4,8},{8,12},{12,14},{14,10},{10,6},{6,2},{2,0},{1,5},{5,9},... | collective-permute-start | bytes 393224 | tf_op jit(solution)/shard_map/ppermute | solution.py:281
  15.6 6.4 %collective-permute-start.8 = (bf16[16,16,256]{2,1,0:T(8,128)(2,1)S(1)}, bf16[16,16,256]{2,1,0:T(8,128)(2,1)S(1)}, u32[]{:S(2)}, u32[]{:S(2)}) collective-permute-start(bf16[16,16,256]{2,1,0:T(8,128)(2,1)S(1)} %collective-permute-done.7.rest_1_), channel_id=1, source_target_pairs={{0,4},{4,8},{8,12},{12,14},{14,10},{10,6},{6,2},{2,0},{1,5},{5,9},... | collective-permute-start | bytes 393224 | tf_op jit(solution)/shard_map/ppermute | solution.py:287
  17.2 6.4 %collective-permute-start.12 = (bf16[16,16,256]{2,1,0:T(8,128)(2,1)S(1)}, bf16[16,16,256]{2,1,0:T(8,128)(2,1)S(1)}, u32[]{:S(2)}, u32[]{:S(2)}) collective-permute-start(bf16[16,16,256]{2,1,0:T(8,128)(2,1)S(1)} %collective-permute-done.11.rest_6_), channel_id=1, source_target_pairs={{4,0},{8,4},{12,8},{14,12},{10,14},{6,10},{2,6},{0,2},{5,1},{9,5},... | collective-permute-start | bytes 393224 | tf_op jit(solution)/shard_map/ppermute | solution.py:289
  20.0 5.5 %collective-permute-start.6 = (bf16[16,16,256]{2,1,0:T(8,128)(2,1)S(1)}, bf16[16,16,256]{2,1,0:T(8,128)(2,1)S(1)}, u32[]{:S(2)}, u32[]{:S(2)}) collective-permute-start(bf16[16,16,256]{2,1,0:T(8,128)(2,1)S(1)} %collective-permute-done.5.rest_6_), channel_id=1, source_target_pairs={{4,0},{8,4},{12,8},{14,12},{10,14},{6,10},{2,6},{0,2},{5,1},{9,5},... | collective-permute-start | bytes 393224 | tf_op jit(solution)/shard_map/ppermute | solution.py:283
  20.6 5.0 %collective-permute-start.3 = (bf16[16,16,256]{2,1,0:T(8,128)(2,1)S(1)}, bf16[16,16,256]{2,1,0:T(8,128)(2,1)S(1)}, u32[]{:S(2)}, u32[]{:S(2)}) collective-permute-start(bf16[16,16,256]{2,1,0:T(8,128)(2,1)S(1)} %collective-permute-done.2.rest_3_), channel_id=1, source_target_pairs={{0,4},{4,8},{8,12},{12,14},{14,10},{10,6},{6,2},{2,0},{1,5},{5,9},... | collective-permute-start | bytes 393224 | tf_op jit(solution)/shard_map/ppermute | solution.py:292
  22.0 6.0 %collective-permute-start.9 = (bf16[16,16,256]{2,1,0:T(8,128)(2,1)S(1)}, bf16[16,16,256]{2,1,0:T(8,128)(2,1)S(1)}, u32[]{:S(2)}, u32[]{:S(2)}) collective-permute-start(bf16[16,16,256]{2,1,0:T(8,128)(2,1)S(1)} %collective-permute-done.8.rest_2_), channel_id=1, source_target_pairs={{0,4},{4,8},{8,12},{12,14},{14,10},{10,6},{6,2},{2,0},{1,5},{5,9},... | collective-permute-start | bytes 393224 | tf_op jit(solution)/shard_map/ppermute | solution.py:287
  23.6 5.0 %collective-permute-start.13 = (bf16[16,16,256]{2,1,0:T(8,128)(2,1)S(1)}, bf16[16,16,256]{2,1,0:T(8,128)(2,1)S(1)}, u32[]{:S(2)}, u32[]{:S(2)}) collective-permute-start(bf16[16,16,256]{2,1,0:T(8,128)(2,1)S(1)} %collective-permute-done.12.rest_5_), channel_id=1, source_target_pairs={{4,0},{8,4},{12,8},{14,12},{10,14},{6,10},{2,6},{0,2},{5,1},{9,5},... | collective-permute-start | bytes 393224 | tf_op jit(solution)/shard_map/ppermute | solution.py:293

commit v5 on v4

--- a/solution.py
+++ b/solution.py
@@ -36,8 +36,8 @@
     count, place_ref, *rest
 ):
     sources, rest = rest[:12], rest[12:]
-    scalars, own_k, own_v, placed, keep, bias, fq, qq, *rest = rest
-    spans_ref, home_ref, sel_ref, length_ref, fk, fv, qk, qv, rows, limits, sems = rest
+    scalars, limits, own_k, own_v, fk, fv, qk, qv, fq, qq, *rest = rest
+    spans_ref, home_ref, sel_ref, length_ref, sems = rest
     req_count, picks, lists, width = fk.shape
     q_rows = qk.shape[1]
     spans_dev, span_len, _ = own_k.shape
@@ -54,7 +54,6 @@
     ]
     for copy in copies:
         copy.start()
-    rows[...] = jnp.zeros_like(rows)
     lane = lax.broadcasted_iota(jnp.int32, (1, LANES), 1)
     asked_at = lane - picks * ROW_TILE
     blank = jnp.where((asked_at >= 0) & (asked_at < q_rows), total + asked_at, -1)
@@ -73,8 +72,15 @@
                 limit = jnp.where(lane == i * ROW_TILE + j, j * span_len + sel_ref[i, position], limit)
         limits[r] = limit
         scalars[req_count * lists + r] = length_ref[r]
-    for copy in copies[4:8]:
+    for copy in copies[4:]:
         copy.wait()
+
+
+def place_kernel(limits, fk, fv, qk, qv, placed, keep, bias, rows):
+    req_count, picks, lists, width = fk.shape
+    q_rows = qk.shape[1]
+    total = keep.shape[1]
+    rows[...] = jnp.zeros_like(rows)
     key = lax.broadcasted_iota(jnp.int32, (placed.shape[1], LANES), 0)
     for r in range(req_count):
         limit = limits[r]
@@ -91,8 +97,6 @@
         taken = jnp.max(here[:total], axis=1, keepdims=True)
         keep[r] = jnp.broadcast_to(1.0 - taken, (total, LANES)).astype(jnp.bfloat16)
         bias[r] = jnp.where(key <= limit, 0.0, MASKED).astype(jnp.bfloat16)
-    for copy in copies[8:]:
-        copy.wait()
 
 
 def weights_kernel(n_buf, slot_ref, placed, keep, bias, fq, qq, *rest):
@@ -194,34 +198,40 @@
     total = lists * span_len
     padded = -(-(total + q_rows) // LANES) * LANES
     near = (spans, home, sel, lengths)
-    held = (fresh_k, fresh_v, question_k, question_v)
-    far = near + held + (fresh_q, question_q, cache_k, cache_v)
+    held = (fresh_k, fresh_v, question_k, question_v, fresh_q, question_q)
+    far = near + held + (cache_k, cache_v)
     bf16 = jnp.bfloat16
-    return pl.pallas_call(
+    scalars, limits, own_k, own_v, *held = pl.pallas_call(
         functools.partial(prepare_kernel, count),
         in_specs=[SMEM_SPEC] + [HBM_SPEC] * len(far),
-        out_specs=[SMEM_SPEC] + [VMEM_SPEC] * 7,
+        out_specs=[SMEM_SPEC] + [VMEM_SPEC] * (3 + len(held)),
         out_shape=[
             pltpu.SMEM((req_count * lists + req_count,), jnp.int32),
+            pltpu.VMEM((req_count, 1, LANES), jnp.int32),
             like(cache_k),
             like(cache_v),
+        ]
+        + [like(x) for x in held],
+        scratch_shapes=[pltpu.SMEM(x.shape, x.dtype) for x in near] + [pltpu.SemaphoreType.DMA((len(far),))],
+        compiler_params=PARAMS,
+        cost_estimate=pl.CostEstimate(flops=0, bytes_accessed=6 << 20, transcendentals=0),
+        name="span_prepare",
+    )(place, *map(in_hbm, far))
+    placed, keep, bias = pl.pallas_call(
+        place_kernel,
+        in_specs=[VMEM_SPEC] * 5,
+        out_specs=[VMEM_SPEC] * 3,
+        out_shape=[
             pltpu.VMEM((req_count, padded, 2 * width), bf16),
             pltpu.VMEM((req_count, total, LANES), bf16),
             pltpu.VMEM((req_count, padded, LANES), bf16),
-            like(fresh_q),
-            like(question_q),
         ],
-        scratch_shapes=[pltpu.SMEM(x.shape, x.dtype) for x in near]
-        + [like(x) for x in held]
-        + [
-            pltpu.VMEM((LANES // ROW_TILE, ROW_TILE, 2 * width), bf16),
-            pltpu.VMEM((req_count, 1, LANES), jnp.int32),
-            pltpu.SemaphoreType.DMA((len(far),)),
-        ],
+        scratch_shapes=[pltpu.VMEM((LANES // ROW_TILE, ROW_TILE, 2 * width), bf16)],
         compiler_params=PARAMS,
-        cost_estimate=pl.CostEstimate(flops=0, bytes_accessed=8 << 20, transcendentals=0),
-        name="span_prepare",
-    )(place, *map(in_hbm, far))
+        cost_estimate=pl.CostEstimate(flops=0, bytes_accessed=3 << 20, transcendentals=0),
+        name="span_place",
+    )(*map(in_vmem, (limits, *held[:4])))
+    return scalars, own_k, own_v, placed, keep, bias, held[4], held[5]
 
 
 def attend(scalars, placed, keep, bias, fresh_q, question_q, k_pieces, v_pieces):
@@ -268,7 +278,7 @@
     )(scalars, *map(in_vmem, (weights, placed, keep)), *map(in_vmem, v_pieces))
 
 
-def ring_gather(keys, values, count, ready):
+def ring_gather(keys, values, count, ready, later):
     order = list(range(0, count, 2)) + list(range(1, count, 2))[::-1]
     onward = [(order[i], order[(i + 1) % count]) for i in range(count)]
     back = [(b, a) for a, b in onward]
@@ -282,6 +292,8 @@
         k_at[hop] = [k_on]
         k_back = lax.ppermute(k_back, "dp", back)
         k_at[count - hop] = [k_back]
+        if hop == 2:
+            k_back, _ = lax.optimization_barrier((k_back, later))
         if hop == 1:
             k_back, _ = lax.optimization_barrier((k_back, ready))
         v_on = lax.ppermute(v_on, "dp", onward)
@@ -349,7 +361,7 @@
         question_v,
     )
     if count <= RING_MAX:
-        k_pieces, v_pieces = ring_gather(cache_k, cache_v, count, own_k)
+        k_pieces, v_pieces = ring_gather(cache_k, cache_v, count, own_k, bias)
         k_pieces[0], v_pieces[0] = own_k, own_v
         scalars = pltpu.with_memory_space_constraint(scalars, pltpu.SMEM)
     else:

time: 31.1 us -> 30.6 us (0.984)
  waiting for transfers between devices: 5.88 us -> 5.43 us
    ppermute x1, starting transfers between devices: 1.37 us -> 0.81 us  [ring_gather(): k_at[half] = [lax.ppermute(k_on, 'dp', onward)]]
    ppermute x3, starting transfers between devices: 3.68 us -> 4.24 us  [ring_gather(): k_back = lax.ppermute(k_back, 'dp', back)]
    ppermute x3, waiting for transfers between devices: 3.53 us -> 2.97 us  [ring_gather(): k_back = lax.ppermute(k_back, 'dp', back)]
    ppermute x1, waiting for transfers between devices: 0.55 us -> 0.01 us  [ring_gather(): v_at[half] = [lax.ppermute(v_back, 'dp', back)]]
    pallas_call x0 -> x1, Pallas kernels: none -> 0.51 us  [prepare(): pl.pallas_call(place_kernel, in_specs=[VMEM_SPEC] * 5, out_specs=[VMEM_SP...]
    ppermute x3, waiting for transfers between devices: 0.01 us -> 0.38 us  [ring_gather(): v_on = lax.ppermute(v_on, 'dp', onward)]
  transfers between devices with their start and end apart: 14 -> 14, of which waited for: 5 -> 6; matrix products, arithmetic and copies ran while one was open for 0% -> 0% of each run, Pallas kernels for 15% -> 16%
where the time goes in v5:
time: 30.6 us; the launch traced here: 30.4 us
  starting transfers between devices  17 us (56%)
  Pallas kernels  7.25 us (24%)
  waiting for transfers between devices  5.43 us (18%)
  between operations  0.69 us (2%)
    ppermute x3, starting transfers between devices, ring_gather(): k_on = lax.ppermute(k_on, 'dp', onward)  5.89 us
    ppermute x3, starting transfers between devices, ring_gather(): v_on = lax.ppermute(v_on, 'dp', onward)  4.52 us
    ppermute x3, starting transfers between devices, ring_gather(): k_back = lax.ppermute(k_back, 'dp', back)  4.24 us
    ppermute x3, waiting for transfers between devices, ring_gather(): k_back = lax.ppermute(k_back, 'dp', back)  2.97 us
    pallas_call x1, Pallas kernels, attend(): pl.pallas_call(functools.partial(weights_kernel, n_buf), in_specs=[SMEM_S...  2.39 us
    pallas_call x1, Pallas kernels, attend(): pl.pallas_call(functools.partial(values_kernel, n_buf), in_specs=[SMEM_SP...  2.32 us
    pallas_call x1, Pallas kernels, prepare(): pl.pallas_call(functools.partial(prepare_kernel, count), in_specs=[SMEM_S...  2.03 us
    ppermute x3, waiting for transfers between devices, ring_gather(): k_on = lax.ppermute(k_on, 'dp', onward)  1.68 us
  transfers between devices with their start and end apart: 14, of which 6 were waited for; matrix products, arithmetic and copies ran while one was open for 0% of the time, Pallas kernels for 16%

profile of v5, /device:TPU:0, one launch (start us, length us, event | category | flops | bytes accessed | tf_op | source)
XLA Modules:
  0.0 30.4 jit_solution(6035845979806841519)
XLA Ops:
  0.6 3.1 %collective-permute-start = (bf16[16,16,256]{2,1,0:T(8,128)(2,1)}, bf16[16,16,256]{2,1,0:T(8,128)(2,1)S(1)}, u32[]{:S(2)}, u32[]{:S(2)}) collective-permute-start(bf16[16,16,256]{2,1,0:T(8,128)(2,1)} %rest_10_.1), channel_id=1, source_target_pairs={{0,4},{4,8},{8,12},{12,14},{14,10},{10,6},{6,2},{2,0},{1,5},{5,9},... | collective-permute-start | bytes 393224 | tf_op jit(solution)/shard_map/ppermute | solution.py:291
  3.7 0.0 collective-permute-start.10
  3.7 1.9 %collective-permute-start.4 = (bf16[16,16,256]{2,1,0:T(8,128)(2,1)}, bf16[16,16,256]{2,1,0:T(8,128)(2,1)S(1)}, u32[]{:S(2)}, u32[]{:S(2)}) collective-permute-start(bf16[16,16,256]{2,1,0:T(8,128)(2,1)} %rest_10_.1), channel_id=1, source_target_pairs={{4,0},{8,4},{12,8},{14,12},{10,14},{6,10},{2,6},{0,2},{5,1},{9,5},... | collective-permute-start | bytes 393224 | tf_op jit(solution)/shard_map/ppermute | solution.py:293
  5.7 1.7 %collective-permute-done.rest_1_ = bf16[16,16,256]{2,1,0:T(8,128)(2,1)S(1)} collective-permute-done((bf16[16,16,256]{2,1,0:T(8,128)(2,1)}, bf16[16,16,256]{2,1,0:T(8,128)(2,1)S(1)}, u32[]{:S(2)}, u32[]{:S(2)}) %collective-permute-start) | collective-permute-done | bytes 131104 | tf_op jit(solution)/shard_map/ppermute | solution.py:291
  7.3 1.8 %collective-permute-start.1 = (bf16[16,16,256]{2,1,0:T(8,128)(2,1)S(1)}, bf16[16,16,256]{2,1,0:T(8,128)(2,1)S(1)}, u32[]{:S(2)}, u32[]{:S(2)}) collective-permute-start(bf16[16,16,256]{2,1,0:T(8,128)(2,1)S(1)} %collective-permute-done.rest_1_), channel_id=1, source_target_pairs={{0,4},{4,8},{8,12},{12,14},{14,10},{10,6},{6,2},{2,0},{1,5},{5,9},... | collective-permute-start | bytes 393224 | tf_op jit(solution)/shard_map/ppermute | solution.py:291
  9.2 1.6 %collective-permute-start.7 = (bf16[16,16,256]{2,1,0:T(8,128)(2,1)}, bf16[16,16,256]{2,1,0:T(8,128)(2,1)S(1)}, u32[]{:S(2)}, u32[]{:S(2)}) collective-permute-start(bf16[16,16,256]{2,1,0:T(8,128)(2,1)} %rest_11_.1), channel_id=1, source_target_pairs={{0,4},{4,8},{8,12},{12,14},{14,10},{10,6},{6,2},{2,0},{1,5},{5,9},... | collective-permute-start | bytes 393224 | tf_op jit(solution)/shard_map/ppermute | solution.py:299
  10.7 0.0 collective-permute-done.10.rest_7_
  10.7 0.4 %collective-permute-start.11 = (bf16[16,16,256]{2,1,0:T(8,128)(2,1)S(1)}, bf16[16,16,256]{2,1,0:T(8,128)(2,1)S(1)}, u32[]{:S(2)}, u32[]{:S(2)}) collective-permute-start(bf16[16,16,256]{2,1,0:T(8,128)(2,1)S(1)} %collective-permute-done.10.rest_7_), channel_id=1, source_target_pairs={{4,0},{8,4},{12,8},{14,12},{10,14},{6,10},{2,6},{0,2},{5,1},{9,5},... | collective-permute-start | bytes 393224 | tf_op jit(solution)/shard_map/ppermute | solution.py:301
  11.2 2.0 %span_prepare.1 = (s32[65]{0:T(128)S(4)}, s32[5,1,128]{2,1,0:T(1,128)S(1)}, bf16[16,16,256]{2,1,0:T(8,128)(2,1)S(1)}, bf16[16,16,256]{2,1,0:T(8,128)(2,1)S(1)}, ...) custom-call(s32[1]{0:T(128)} %bitcast.place_ref, ...), custom_call_target="tpu_custom_call" | custom-call | bytes 6291456 | tf_op jit(solution)/shard_map/span_prepare/pallas_call | solution.py:204
  13.2 0.0 collective-permute-done.4.rest_7_
  13.2 1.1 %collective-permute-start.5 = (bf16[16,16,256]{2,1,0:T(8,128)(2,1)S(1)}, bf16[16,16,256]{2,1,0:T(8,128)(2,1)S(1)}, u32[]{:S(2)}, u32[]{:S(2)}) collective-permute-start(bf16[16,16,256]{2,1,0:T(8,128)(2,1)S(1)} %collective-permute-done.4.rest_7_), channel_id=1, source_target_pairs={{4,0},{8,4},{12,8},{14,12},{10,14},{6,10},{2,6},{0,2},{5,1},{9,5},... | collective-permute-start | bytes 393224 | tf_op jit(solution)/shard_map/ppermute | solution.py:293
  14.3 0.0 collective-permute-done.1.rest_2_
  14.3 1.0 %collective-permute-start.2 = (bf16[16,16,256]{2,1,0:T(8,128)(2,1)S(1)}, bf16[16,16,256]{2,1,0:T(8,128)(2,1)S(1)}, u32[]{:S(2)}, u32[]{:S(2)}) collective-permute-start(bf16[16,16,256]{2,1,0:T(8,128)(2,1)S(1)} %collective-permute-done.1.rest_2_), channel_id=1, source_target_pairs={{0,4},{4,8},{8,12},{12,14},{14,10},{10,6},{6,2},{2,0},{1,5},{5,9},... | collective-permute-start | bytes 393224 | tf_op jit(solution)/shard_map/ppermute | solution.py:291
  15.3 0.1 collective-permute-done.7.rest_1_
  15.4 1.6 %collective-permute-start.8 = (bf16[16,16,256]{2,1,0:T(8,128)(2,1)S(1)}, bf16[16,16,256]{2,1,0:T(8,128)(2,1)S(1)}, u32[]{:S(2)}, u32[]{:S(2)}) collective-permute-start(bf16[16,16,256]{2,1,0:T(8,128)(2,1)S(1)} %collective-permute-done.7.rest_1_), channel_id=1, source_target_pairs={{0,4},{4,8},{8,12},{12,14},{14,10},{10,6},{6,2},{2,0},{1,5},{5,9},... | collective-permute-start | bytes 393224 | tf_op jit(solution)/shard_map/ppermute | solution.py:299
  17.1 0.0 collective-permute-done.11.rest_6_
  17.1 0.4 %collective-permute-start.12 = (bf16[16,16,256]{2,1,0:T(8,128)(2,1)S(1)}, bf16[16,16,256]{2,1,0:T(8,128)(2,1)S(1)}, u32[]{:S(2)}, u32[]{:S(2)}) collective-permute-start(bf16[16,16,256]{2,1,0:T(8,128)(2,1)S(1)} %collective-permute-done.11.rest_6_), channel_id=1, source_target_pairs={{4,0},{8,4},{12,8},{14,12},{10,14},{6,10},{2,6},{0,2},{5,1},{9,5},... | collective-permute-start | bytes 393224 | tf_op jit(solution)/shard_map/ppermute | solution.py:301
  17.4 0.5 %span_place.1 = (bf16[5,256,512]{2,1,0:T(8,128)(2,1)S(1)}, bf16[5,192,128]{2,1,0:T(8,128)(2,1)S(1)}, bf16[5,256,128]{2,1,0:T(8,128)(2,1)S(1)}) custom-call(s32[5,1,128]{2,1,0:T(1,128)S(1)} %get-tuple-element.20.limits, bf16[5,5,12,256]{3,2,1,0:T(8,128)(2,1)S(1)} %get-tuple-element.21.fk, bf16[5,5,12,256]{3,2,1,0:T(8,128)(2,1)S(1)} %get-tuple-element.22.fv, ...), custom_call_target="tpu_custom_call" | custom-call | bytes 3145728 | tf_op jit(solution)/shard_map/span_place/pallas_call | solution.py:220
  18.0 1.5 %collective-permute-done.5.rest_6_ = bf16[16,16,256]{2,1,0:T(8,128)(2,1)S(1)} collective-permute-done((bf16[16,16,256]{2,1,0:T(8,128)(2,1)S(1)}, bf16[16,16,256]{2,1,0:T(8,128)(2,1)S(1)}, u32[]{:S(2)}, u32[]{:S(2)}) %collective-permute-start.5) | collective-permute-done | bytes 131104 | tf_op jit(solution)/shard_map/ppermute | solution.py:293
  19.5 1.2 %collective-permute-start.6 = (bf16[16,16,256]{2,1,0:T(8,128)(2,1)S(1)}, bf16[16,16,256]{2,1,0:T(8,128)(2,1)S(1)}, u32[]{:S(2)}, u32[]{:S(2)}) collective-permute-start(bf16[16,16,256]{2,1,0:T(8,128)(2,1)S(1)} %collective-permute-done.5.rest_6_), channel_id=1, source_target_pairs={{4,0},{8,4},{12,8},{14,12},{10,14},{6,10},{2,6},{0,2},{5,1},{9,5},... | collective-permute-start | bytes 393224 | tf_op jit(solution)/shard_map/ppermute | solution.py:293
  20.7 0.0 collective-permute-done.2.rest_3_
  20.7 0.8 %collective-permute-start.3 = (bf16[16,16,256]{2,1,0:T(8,128)(2,1)S(1)}, bf16[16,16,256]{2,1,0:T(8,128)(2,1)S(1)}, u32[]{:S(2)}, u32[]{:S(2)}) collective-permute-start(bf16[16,16,256]{2,1,0:T(8,128)(2,1)S(1)} %collective-permute-done.2.rest_3_), channel_id=1, source_target_pairs={{0,4},{4,8},{8,12},{12,14},{14,10},{10,6},{6,2},{2,0},{1,5},{5,9},... | collective-permute-start | bytes 393224 | tf_op jit(solution)/shard_map/ppermute | solution.py:304
  21.5 0.3 collective-permute-done.8.rest_2_
  21.8 1.3 %collective-permute-start.9 = (bf16[16,16,256]{2,1,0:T(8,128)(2,1)S(1)}, bf16[16,16,256]{2,1,0:T(8,128)(2,1)S(1)}, u32[]{:S(2)}, u32[]{:S(2)}) collective-permute-start(bf16[16,16,256]{2,1,0:T(8,128)(2,1)S(1)} %collective-permute-done.8.rest_2_), channel_id=1, source_target_pairs={{0,4},{4,8},{8,12},{12,14},{14,10},{10,6},{6,2},{2,0},{1,5},{5,9},... | collective-permute-start | bytes 393224 | tf_op jit(solution)/shard_map/ppermute | solution.py:299
  23.1 0.0 collective-permute-done.12.rest_5_
  23.1 0.7 %collective-permute-start.13 = (bf16[16,16,256]{2,1,0:T(8,128)(2,1)S(1)}, bf16[16,16,256]{2,1,0:T(8,128)(2,1)S(1)}, u32[]{:S(2)}, u32[]{:S(2)}) collective-permute-start(bf16[16,16,256]{2,1,0:T(8,128)(2,1)S(1)} %collective-permute-done.12.rest_5_), channel_id=1, source_target_pairs={{4,0},{8,4},{12,8},{14,12},{10,14},{6,10},{2,6},{0,2},{5,1},{9,5},... | collective-permute-start | bytes 393224 | tf_op jit(solution)/shard_map/ppermute | solution.py:305
  23.8 1.4 %collective-permute-done.6.rest_5_ = bf16[16,16,256]{2,1,0:T(8,128)(2,1)S(1)} collective-permute-done((bf16[16,16,256]{2,1,0:T(8,128)(2,1)S(1)}, bf16[16,16,256]{2,1,0:T(8,128)(2,1)S(1)}, u32[]{:S(2)}, u32[]{:S(2)}) %collective-permute-start.6) | collective-permute-done | bytes 131104 | tf_op jit(solution)/shard_map/ppermute | solution.py:293
  25.3 0.4 %collective-permute-done.3.rest_4_ = bf16[16,16,256]{2,1,0:T(8,128)(2,1)S(1)} collective-permute-done((bf16[16,16,256]{2,1,0:T(8,128)(2,1)S(1)}, bf16[16,16,256]{2,1,0:T(8,128)(2,1)S(1)}, u32[]{:S(2)}, u32[]{:S(2)}) %collective-permute-start.3) | collective-permute-done | bytes 131104 | tf_op jit(solution)/shard_map/ppermute | solution.py:304
  25.7 2.4 %span_weights.1.w_ref = bf16[5,2,896,256]{3,2,1,0:T(8,128)(2,1)S(1)} custom-call(s32[65]{0:T(128)S(4)} %get-tuple-element.19.slot_ref, bf16[5,256,512]{2,1,0:T(8,128)(2,1)S(1)} %get-tuple-element.25.placed, bf16[5,192,128]{2,1,0:T(8,128)(2,1)S(1)} %get-tuple-element.26.keep, bf16[5,256,128]{2,1,0:T(8,128)(2,1)S(1)} %get-tuple-element.27.bias, ...), custom_call_target="tpu_custom_call" | custom-call | flops 1174405120 | bytes 8388608 | tf_op jit(solution)/shard_map/span_weights/pallas_call | solution.py:248
  28.1 0.0 collective-permute-done.9.rest_3_
  28.1 0.0 collective-permute-done.13.rest_4_
  28.1 2.3 %span_values.1 = (bf16[5,5,12,2048]{3,2,1,0:T(8,128)(2,1)}, bf16[5,32,2048]{2,1,0:T(8,128)(2,1)}) custom-call(s32[65]{0:T(128)S(4)} %get-tuple-element.19.slot_ref, bf16[5,2,896,256]{3,2,1,0:T(8,128)(2,1)S(1)} %span_weights.1.w_ref, bf16[5,256,512]{2,1,0:T(8,128)(2,1)S(1)} %get-tuple-element.25.placed, bf16[5,192,128]{2,1,0:T(8,128)(2,1)S(1)} %get-tuple-element.26.keep, ...), custom_call_target="tpu_custom_call" | custom-call | flops 1174405120 | bytes 8388608 | tf_op jit(solution)/shard_map/span_values/pallas_call | solution.py:260
Async XLA Ops:
  0.6 6.7 %collective-permute-start = (bf16[16,16,256]{2,1,0:T(8,128)(2,1)}, bf16[16,16,256]{2,1,0:T(8,128)(2,1)S(1)}, u32[]{:S(2)}, u32[]{:S(2)}) collective-permute-start(bf16[16,16,256]{2,1,0:T(8,128)(2,1)} %rest_10_.1), channel_id=1, source_target_pairs={{0,4},{4,8},{8,12},{12,14},{14,10},{10,6},{6,2},{2,0},{1,5},{5,9},... | collective-permute-start | bytes 393224 | tf_op jit(solution)/shard_map/ppermute | solution.py:291
  3.7 7.0 %collective-permute-start.10 = (bf16[16,16,256]{2,1,0:T(8,128)(2,1)}, bf16[16,16,256]{2,1,0:T(8,128)(2,1)S(1)}, u32[]{:S(2)}, u32[]{:S(2)}) collective-permute-start(bf16[16,16,256]{2,1,0:T(8,128)(2,1)} %rest_11_.1), channel_id=1, source_target_pairs={{4,0},{8,4},{12,8},{14,12},{10,14},{6,10},{2,6},{0,2},{5,1},{9,5},... | collective-permute-start | bytes 393224 | tf_op jit(solution)/shard_map/ppermute | solution.py:301
  3.7 9.5 %collective-permute-start.4 = (bf16[16,16,256]{2,1,0:T(8,128)(2,1)}, bf16[16,16,256]{2,1,0:T(8,128)(2,1)S(1)}, u32[]{:S(2)}, u32[]{:S(2)}) collective-permute-start(bf16[16,16,256]{2,1,0:T(8,128)(2,1)} %rest_10_.1), channel_id=1, source_target_pairs={{4,0},{8,4},{12,8},{14,12},{10,14},{6,10},{2,6},{0,2},{5,1},{9,5},... | collective-permute-start | bytes 393224 | tf_op jit(solution)/shard_map/ppermute | solution.py:293
  7.3 7.0 %collective-permute-start.1 = (bf16[16,16,256]{2,1,0:T(8,128)(2,1)S(1)}, bf16[16,16,256]{2,1,0:T(8,128)(2,1)S(1)}, u32[]{:S(2)}, u32[]{:S(2)}) collective-permute-start(bf16[16,16,256]{2,1,0:T(8,128)(2,1)S(1)} %collective-permute-done.rest_1_), channel_id=1, source_target_pairs={{0,4},{4,8},{8,12},{12,14},{14,10},{10,6},{6,2},{2,0},{1,5},{5,9},... | collective-permute-start | bytes 393224 | tf_op jit(solution)/shard_map/ppermute | solution.py:291
  9.2 6.2 %collective-permute-start.7 = (bf16[16,16,256]{2,1,0:T(8,128)(2,1)}, bf16[16,16,256]{2,1,0:T(8,128)(2,1)S(1)}, u32[]{:S(2)}, u32[]{:S(2)}) collective-permute-start(bf16[16,16,256]{2,1,0:T(8,128)(2,1)} %rest_11_.1), channel_id=1, source_target_pairs={{0,4},{4,8},{8,12},{12,14},{14,10},{10,6},{6,2},{2,0},{1,5},{5,9},... | collective-permute-start | bytes 393224 | tf_op jit(solution)/shard_map/ppermute | solution.py:299
  10.7 6.3 %collective-permute-start.11 = (bf16[16,16,256]{2,1,0:T(8,128)(2,1)S(1)}, bf16[16,16,256]{2,1,0:T(8,128)(2,1)S(1)}, u32[]{:S(2)}, u32[]{:S(2)}) collective-permute-start(bf16[16,16,256]{2,1,0:T(8,128)(2,1)S(1)} %collective-permute-done.10.rest_7_), channel_id=1, source_target_pairs={{4,0},{8,4},{12,8},{14,12},{10,14},{6,10},{2,6},{0,2},{5,1},{9,5},... | collective-permute-start | bytes 393224 | tf_op jit(solution)/shard_map/ppermute | solution.py:301
  13.2 6.2 %collective-permute-start.5 = (bf16[16,16,256]{2,1,0:T(8,128)(2,1)S(1)}, bf16[16,16,256]{2,1,0:T(8,128)(2,1)S(1)}, u32[]{:S(2)}, u32[]{:S(2)}) collective-permute-start(bf16[16,16,256]{2,1,0:T(8,128)(2,1)S(1)} %collective-permute-done.4.rest_7_), channel_id=1, source_target_pairs={{4,0},{8,4},{12,8},{14,12},{10,14},{6,10},{2,6},{0,2},{5,1},{9,5},... | collective-permute-start | bytes 393224 | tf_op jit(solution)/shard_map/ppermute | solution.py:293
  14.3 6.4 %collective-permute-start.2 = (bf16[16,16,256]{2,1,0:T(8,128)(2,1)S(1)}, bf16[16,16,256]{2,1,0:T(8,128)(2,1)S(1)}, u32[]{:S(2)}, u32[]{:S(2)}) collective-permute-start(bf16[16,16,256]{2,1,0:T(8,128)(2,1)S(1)} %collective-permute-done.1.rest_2_), channel_id=1, source_target_pairs={{0,4},{4,8},{8,12},{12,14},{14,10},{10,6},{6,2},{2,0},{1,5},{5,9},... | collective-permute-start | bytes 393224 | tf_op jit(solution)/shard_map/ppermute | solution.py:291
  15.4 6.4 %collective-permute-start.8 = (bf16[16,16,256]{2,1,0:T(8,128)(2,1)S(1)}, bf16[16,16,256]{2,1,0:T(8,128)(2,1)S(1)}, u32[]{:S(2)}, u32[]{:S(2)}) collective-permute-start(bf16[16,16,256]{2,1,0:T(8,128)(2,1)S(1)} %collective-permute-done.7.rest_1_), channel_id=1, source_target_pairs={{0,4},{4,8},{8,12},{12,14},{14,10},{10,6},{6,2},{2,0},{1,5},{5,9},... | collective-permute-start | bytes 393224 | tf_op jit(solution)/shard_map/ppermute | solution.py:299
  17.1 6.0 %collective-permute-start.12 = (bf16[16,16,256]{2,1,0:T(8,128)(2,1)S(1)}, bf16[16,16,256]{2,1,0:T(8,128)(2,1)S(1)}, u32[]{:S(2)}, u32[]{:S(2)}) collective-permute-start(bf16[16,16,256]{2,1,0:T(8,128)(2,1)S(1)} %collective-permute-done.11.rest_6_), channel_id=1, source_target_pairs={{4,0},{8,4},{12,8},{14,12},{10,14},{6,10},{2,6},{0,2},{5,1},{9,5},... | collective-permute-start | bytes 393224 | tf_op jit(solution)/shard_map/ppermute | solution.py:301
  19.5 5.8 %collective-permute-start.6 = (bf16[16,16,256]{2,1,0:T(8,128)(2,1)S(1)}, bf16[16,16,256]{2,1,0:T(8,128)(2,1)S(1)}, u32[]{:S(2)}, u32[]{:S(2)}) collective-permute-start(bf16[16,16,256]{2,1,0:T(8,128)(2,1)S(1)} %collective-permute-done.5.rest_6_), channel_id=1, source_target_pairs={{4,0},{8,4},{12,8},{14,12},{10,14},{6,10},{2,6},{0,2},{5,1},{9,5},... | collective-permute-start | bytes 393224 | tf_op jit(solution)/shard_map/ppermute | solution.py:293
  20.7 5.0 %collective-permute-start.3 = (bf16[16,16,256]{2,1,0:T(8,128)(2,1)S(1)}, bf16[16,16,256]{2,1,0:T(8,128)(2,1)S(1)}, u32[]{:S(2)}, u32[]{:S(2)}) collective-permute-start(bf16[16,16,256]{2,1,0:T(8,128)(2,1)S(1)} %collective-permute-done.2.rest_3_), channel_id=1, source_target_pairs={{0,4},{4,8},{8,12},{12,14},{14,10},{10,6},{6,2},{2,0},{1,5},{5,9},... | collective-permute-start | bytes 393224 | tf_op jit(solution)/shard_map/ppermute | solution.py:304
  21.8 6.3 %collective-permute-start.9 = (bf16[16,16,256]{2,1,0:T(8,128)(2,1)S(1)}, bf16[16,16,256]{2,1,0:T(8,128)(2,1)S(1)}, u32[]{:S(2)}, u32[]{:S(2)}) collective-permute-start(bf16[16,16,256]{2,1,0:T(8,128)(2,1)S(1)} %collective-permute-done.8.rest_2_), channel_id=1, source_target_pairs={{0,4},{4,8},{8,12},{12,14},{14,10},{10,6},{6,2},{2,0},{1,5},{5,9},... | collective-permute-start | bytes 393224 | tf_op jit(solution)/shard_map/ppermute | solution.py:299
  23.1 5.0 %collective-permute-start.13 = (bf16[16,16,256]{2,1,0:T(8,128)(2,1)S(1)}, bf16[16,16,256]{2,1,0:T(8,128)(2,1)S(1)}, u32[]{:S(2)}, u32[]{:S(2)}) collective-permute-start(bf16[16,16,256]{2,1,0:T(8,128)(2,1)S(1)} %collective-permute-done.12.rest_5_), channel_id=1, source_target_pairs={{4,0},{8,4},{12,8},{14,12},{10,14},{6,10},{2,6},{0,2},{5,1},{9,5},... | collective-permute-start | bytes 393224 | tf_op jit(solution)/shard_map/ppermute | solution.py:305

commit v6 on v5

--- a/solution.py
+++ b/solution.py
@@ -76,7 +76,7 @@
         copy.wait()
 
 
-def place_kernel(limits, fk, fv, qk, qv, placed, keep, bias, rows):
+def place_kernel(limits, fk, fv, qk, qv, fq, qq, placed, keep, bias, queries, rows):
     req_count, picks, lists, width = fk.shape
     q_rows = qk.shape[1]
     total = keep.shape[1]
@@ -97,13 +97,17 @@
         taken = jnp.max(here[:total], axis=1, keepdims=True)
         keep[r] = jnp.broadcast_to(1.0 - taken, (total, LANES)).astype(jnp.bfloat16)
         bias[r] = jnp.where(key <= limit, 0.0, MASKED).astype(jnp.bfloat16)
-
-
-def weights_kernel(n_buf, slot_ref, placed, keep, bias, fq, qq, *rest):
+        for g in range(queries.shape[1]):
+            for h in range(queries.shape[2]):
+                at = (g * queries.shape[2] + h) * HEAD
+                queries[r, g, h, 0:picks, 0:lists, :] = fq[r, :, :, at : at + HEAD]
+                queries[r, g, h, picks:, :, :] = qq[r, :, at : at + HEAD].reshape(-1, ROW_TILE, HEAD)
+
+
+def weights_kernel(n_buf, lists, slot_ref, placed, keep, bias, queries, *rest):
     pieces = rest[:n_buf]
-    out_ref, pool, blended, units, queries = rest[n_buf:]
-    req_count, picks, lists, _ = fq.shape
-    kv_heads, heads, tiles = queries.shape[:3]
+    out_ref, pool, blended, units = rest[n_buf:]
+    req_count, kv_heads, heads, tiles = queries.shape[:4]
     rows_head = tiles * ROW_TILE
     width = blended.shape[1]
     row = lax.broadcasted_iota(jnp.int32, (rows_head, LANES), 0)
@@ -117,11 +121,7 @@
         blend(r * lists, slot_ref, pool, placed.at[r, :, 0:width], keep.at[r], blended)
         for g in range(kv_heads):
             table = jnp.concatenate([blended[:, g * HEAD : (g + 1) * HEAD], bias[r]], axis=1)
-            for h in range(heads):
-                at = (g * heads + h) * HEAD
-                queries[g, h, 0:picks, 0:lists, :] = fq[r, :, :, at : at + HEAD]
-                queries[g, h, picks:, :, :] = qq[r, :, at : at + HEAD].reshape(-1, ROW_TILE, HEAD)
-            stacked = queries[g].reshape(heads * rows_head, HEAD)
+            stacked = queries[r, g].reshape(heads * rows_head, HEAD)
             scores = lax.dot_general(
                 jnp.concatenate([stacked, units[...]], axis=1),
                 table,
@@ -192,9 +192,10 @@
 
 def prepare(place, spans, home, sel, lengths, cache_k, cache_v, fresh_q, fresh_k, fresh_v, question_q, question_k, question_v):
     count = lax.axis_size("dp")
-    req_count, picks, lists, _ = fresh_q.shape
+    req_count, picks, lists, q_width = fresh_q.shape
     _, span_len, width = cache_k.shape
     q_rows = question_q.shape[1]
+    kv_heads, heads = width // HEAD, q_width // width
     total = lists * span_len
     padded = -(-(total + q_rows) // LANES) * LANES
     near = (spans, home, sel, lengths)
@@ -217,45 +218,44 @@
         cost_estimate=pl.CostEstimate(flops=0, bytes_accessed=6 << 20, transcendentals=0),
         name="span_prepare",
     )(place, *map(in_hbm, far))
-    placed, keep, bias = pl.pallas_call(
+    placed, keep, bias, queries = pl.pallas_call(
         place_kernel,
-        in_specs=[VMEM_SPEC] * 5,
-        out_specs=[VMEM_SPEC] * 3,
+        in_specs=[VMEM_SPEC] * 7,
+        out_specs=[VMEM_SPEC] * 4,
         out_shape=[
             pltpu.VMEM((req_count, padded, 2 * width), bf16),
             pltpu.VMEM((req_count, total, LANES), bf16),
             pltpu.VMEM((req_count, padded, LANES), bf16),
+            pltpu.VMEM((req_count, kv_heads, heads, picks + q_rows // ROW_TILE, ROW_TILE, HEAD), bf16),
         ],
         scratch_shapes=[pltpu.VMEM((LANES // ROW_TILE, ROW_TILE, 2 * width), bf16)],
         compiler_params=PARAMS,
         cost_estimate=pl.CostEstimate(flops=0, bytes_accessed=3 << 20, transcendentals=0),
         name="span_place",
-    )(*map(in_vmem, (limits, *held[:4])))
-    return scalars, own_k, own_v, placed, keep, bias, held[4], held[5]
-
-
-def attend(scalars, placed, keep, bias, fresh_q, question_q, k_pieces, v_pieces):
-    req_count, picks, _, q_width = fresh_q.shape
+    )(*map(in_vmem, (limits, *held)))
+    return scalars, own_k, own_v, placed, keep, bias, queries
+
+
+def attend(scalars, placed, keep, bias, queries, fresh_q, question_q, k_pieces, v_pieces):
+    req_count, _, lists, _ = fresh_q.shape
     _, span_len, width = k_pieces[0].shape
     n_buf = len(k_pieces)
-    kv_heads, heads = width // HEAD, q_width // width
-    tiles = picks + question_q.shape[1] // ROW_TILE
+    kv_heads, heads, tiles = queries.shape[1:4]
     padded = placed.shape[1]
     pool = pltpu.VMEM((sum(x.shape[0] for x in k_pieces), span_len, width), jnp.bfloat16)
     blended = pltpu.VMEM((padded, width), jnp.bfloat16)
     w_shape = (req_count, kv_heads, heads * tiles * ROW_TILE, padded)
     flops = 4 * req_count * kv_heads * heads * tiles * ROW_TILE * padded * HEAD
     weights = pl.pallas_call(
-        functools.partial(weights_kernel, n_buf),
-        in_specs=[SMEM_SPEC] + [VMEM_SPEC] * (5 + n_buf),
+        functools.partial(weights_kernel, n_buf, lists),
+        in_specs=[SMEM_SPEC] + [VMEM_SPEC] * (4 + n_buf),
         out_specs=VMEM_SPEC,
-        scratch_shapes=[pool, blended, pltpu.VMEM((heads * tiles * ROW_TILE, LANES), jnp.bfloat16)]
-        + [pltpu.VMEM((kv_heads, heads, tiles, ROW_TILE, HEAD), jnp.bfloat16)],
+        scratch_shapes=[pool, blended, pltpu.VMEM((heads * tiles * ROW_TILE, LANES), jnp.bfloat16)],
         out_shape=pltpu.VMEM(w_shape, jnp.bfloat16),
         compiler_params=PARAMS,
         cost_estimate=pl.CostEstimate(flops=flops, bytes_accessed=8 << 20, transcendentals=flops // 512),
         name="span_weights",
-    )(scalars, *map(in_vmem, (placed, keep, bias, fresh_q, question_q)), *map(in_vmem, k_pieces))
+    )(scalars, *map(in_vmem, (placed, keep, bias, queries)), *map(in_vmem, k_pieces))
     n_buf = len(v_pieces)
     return pl.pallas_call(
         functools.partial(values_kernel, n_buf),
@@ -345,7 +345,7 @@
     turned_q, turned_k, turned_v = [jnp.transpose(x, (0, 2, 1, 3)) for x in (fresh_q, fresh_k, fresh_v)]
     me = lax.axis_index("dp")
     place = jnp.where(me % 2 == 0, me // 2, count - 1 - me // 2).astype(jnp.int32).reshape(1)
-    scalars, own_k, own_v, placed, keep, bias, held_q, asked_q = prepare(
+    scalars, own_k, own_v, placed, keep, bias, queries = prepare(
         place,
         request_spans,
         span_home,
@@ -371,7 +371,7 @@
         slots, k_pieces, v_pieces = asked_gather(cache_k, cache_v, positions, spans_dev, count)
         scalars = jnp.concatenate([slots, question_len])
     redone, spoken = attend(
-        scalars, placed, keep, bias, held_q, asked_q, k_pieces, v_pieces
+        scalars, placed, keep, bias, queries, turned_q, question_q, k_pieces, v_pieces
     )
     return jnp.transpose(redone, (0, 2, 1, 3)), spoken
 

time: 30.6 us -> 30.5 us (level)
    ppermute x1, waiting for transfers between devices: 0.01 us -> 0.51 us  [ring_gather(): v_at[half] = [lax.ppermute(v_back, 'dp', back)]]
  transfers between devices with their start and end apart: 14 -> 14, of which waited for: 6 -> 7; matrix products, arithmetic and copies ran while one was open for 0% -> 0% of each run, Pallas kernels for 16% -> 15%
where the time goes in v6:
time: 30.5 us; the launch traced here: 30.4 us
  starting transfers between devices  17 us (56%)
  Pallas kernels  7.02 us (23%)
  waiting for transfers between devices  5.65 us (19%)
  between operations  0.69 us (2%)
    ppermute x3, starting transfers between devices, ring_gather(): k_on = lax.ppermute(k_on, 'dp', onward)  5.89 us
    ppermute x3, starting transfers between devices, ring_gather(): v_on = lax.ppermute(v_on, 'dp', onward)  4.52 us
    ppermute x3, starting transfers between devices, ring_gather(): k_back = lax.ppermute(k_back, 'dp', back)  4.24 us
    ppermute x3, waiting for transfers between devices, ring_gather(): k_back = lax.ppermute(k_back, 'dp', back)  2.68 us
    pallas_call x1, Pallas kernels, attend(): pl.pallas_call(functools.partial(values_kernel, n_buf), in_specs=[SMEM_SP...  2.32 us
    pallas_call x1, Pallas kernels, prepare(): pl.pallas_call(functools.partial(prepare_kernel, count), in_specs=[SMEM_S...  2.03 us
    pallas_call x1, Pallas kernels, attend(): pl.pallas_call(functools.partial(weights_kernel, n_buf, lists), in_specs=...  1.87 us
    ppermute x3, waiting for transfers between devices, ring_gather(): k_on = lax.ppermute(k_on, 'dp', onward)  1.68 us
  transfers between devices with their start and end apart: 14, of which 7 were waited for; matrix products, arithmetic and copies ran while one was open for 0% of the time, Pallas kernels for 15%

profile of v6, /device:TPU:0, one launch (start us, length us, event | category | flops | bytes accessed | tf_op | source)
XLA Modules:
  0.0 30.4 jit_solution(11155624558671158687)
XLA Ops:
  0.6 3.1 %collective-permute-start = (bf16[16,16,256]{2,1,0:T(8,128)(2,1)}, bf16[16,16,256]{2,1,0:T(8,128)(2,1)S(1)}, u32[]{:S(2)}, u32[]{:S(2)}) collective-permute-start(bf16[16,16,256]{2,1,0:T(8,128)(2,1)} %rest_10_.1), channel_id=1, source_target_pairs={{0,4},{4,8},{8,12},{12,14},{14,10},{10,6},{6,2},{2,0},{1,5},{5,9},... | collective-permute-start | bytes 393224 | tf_op jit(solution)/shard_map/ppermute | solution.py:291
  3.7 0.0 collective-permute-start.10
  3.7 1.9 %collective-permute-start.4 = (bf16[16,16,256]{2,1,0:T(8,128)(2,1)}, bf16[16,16,256]{2,1,0:T(8,128)(2,1)S(1)}, u32[]{:S(2)}, u32[]{:S(2)}) collective-permute-start(bf16[16,16,256]{2,1,0:T(8,128)(2,1)} %rest_10_.1), channel_id=1, source_target_pairs={{4,0},{8,4},{12,8},{14,12},{10,14},{6,10},{2,6},{0,2},{5,1},{9,5},... | collective-permute-start | bytes 393224 | tf_op jit(solution)/shard_map/ppermute | solution.py:293
  5.7 1.7 %collective-permute-done.rest_1_ = bf16[16,16,256]{2,1,0:T(8,128)(2,1)S(1)} collective-permute-done((bf16[16,16,256]{2,1,0:T(8,128)(2,1)}, bf16[16,16,256]{2,1,0:T(8,128)(2,1)S(1)}, u32[]{:S(2)}, u32[]{:S(2)}) %collective-permute-start) | collective-permute-done | bytes 131104 | tf_op jit(solution)/shard_map/ppermute | solution.py:291
  7.3 1.8 %collective-permute-start.1 = (bf16[16,16,256]{2,1,0:T(8,128)(2,1)S(1)}, bf16[16,16,256]{2,1,0:T(8,128)(2,1)S(1)}, u32[]{:S(2)}, u32[]{:S(2)}) collective-permute-start(bf16[16,16,256]{2,1,0:T(8,128)(2,1)S(1)} %collective-permute-done.rest_1_), channel_id=1, source_target_pairs={{0,4},{4,8},{8,12},{12,14},{14,10},{10,6},{6,2},{2,0},{1,5},{5,9},... | collective-permute-start | bytes 393224 | tf_op jit(solution)/shard_map/ppermute | solution.py:291
  9.2 1.6 %collective-permute-start.7 = (bf16[16,16,256]{2,1,0:T(8,128)(2,1)}, bf16[16,16,256]{2,1,0:T(8,128)(2,1)S(1)}, u32[]{:S(2)}, u32[]{:S(2)}) collective-permute-start(bf16[16,16,256]{2,1,0:T(8,128)(2,1)} %rest_11_.1), channel_id=1, source_target_pairs={{0,4},{4,8},{8,12},{12,14},{14,10},{10,6},{6,2},{2,0},{1,5},{5,9},... | collective-permute-start | bytes 393224 | tf_op jit(solution)/shard_map/ppermute | solution.py:299
  10.7 0.0 collective-permute-done.10.rest_7_
  10.7 0.4 %collective-permute-start.11 = (bf16[16,16,256]{2,1,0:T(8,128)(2,1)S(1)}, bf16[16,16,256]{2,1,0:T(8,128)(2,1)S(1)}, u32[]{:S(2)}, u32[]{:S(2)}) collective-permute-start(bf16[16,16,256]{2,1,0:T(8,128)(2,1)S(1)} %collective-permute-done.10.rest_7_), channel_id=1, source_target_pairs={{4,0},{8,4},{12,8},{14,12},{10,14},{6,10},{2,6},{0,2},{5,1},{9,5},... | collective-permute-start | bytes 393224 | tf_op jit(solution)/shard_map/ppermute | solution.py:301
  11.2 2.0 %span_prepare.1 = (s32[65]{0:T(128)S(4)}, s32[5,1,128]{2,1,0:T(1,128)S(1)}, bf16[16,16,256]{2,1,0:T(8,128)(2,1)S(1)}, bf16[16,16,256]{2,1,0:T(8,128)(2,1)S(1)}, ...) custom-call(s32[1]{0:T(128)} %bitcast.place_ref, ...), custom_call_target="tpu_custom_call" | custom-call | bytes 6291456 | tf_op jit(solution)/shard_map/span_prepare/pallas_call | solution.py:205
  13.2 0.0 collective-permute-done.4.rest_7_
  13.2 1.1 %collective-permute-start.5 = (bf16[16,16,256]{2,1,0:T(8,128)(2,1)S(1)}, bf16[16,16,256]{2,1,0:T(8,128)(2,1)S(1)}, u32[]{:S(2)}, u32[]{:S(2)}) collective-permute-start(bf16[16,16,256]{2,1,0:T(8,128)(2,1)S(1)} %collective-permute-done.4.rest_7_), channel_id=1, source_target_pairs={{4,0},{8,4},{12,8},{14,12},{10,14},{6,10},{2,6},{0,2},{5,1},{9,5},... | collective-permute-start | bytes 393224 | tf_op jit(solution)/shard_map/ppermute | solution.py:293
  14.3 0.0 collective-permute-done.1.rest_2_
  14.3 1.0 %collective-permute-start.2 = (bf16[16,16,256]{2,1,0:T(8,128)(2,1)S(1)}, bf16[16,16,256]{2,1,0:T(8,128)(2,1)S(1)}, u32[]{:S(2)}, u32[]{:S(2)}) collective-permute-start(bf16[16,16,256]{2,1,0:T(8,128)(2,1)S(1)} %collective-permute-done.1.rest_2_), channel_id=1, source_target_pairs={{0,4},{4,8},{8,12},{12,14},{14,10},{10,6},{6,2},{2,0},{1,5},{5,9},... | collective-permute-start | bytes 393224 | tf_op jit(solution)/shard_map/ppermute | solution.py:291
  15.3 0.1 collective-permute-done.7.rest_1_
  15.4 1.6 %collective-permute-start.8 = (bf16[16,16,256]{2,1,0:T(8,128)(2,1)S(1)}, bf16[16,16,256]{2,1,0:T(8,128)(2,1)S(1)}, u32[]{:S(2)}, u32[]{:S(2)}) collective-permute-start(bf16[16,16,256]{2,1,0:T(8,128)(2,1)S(1)} %collective-permute-done.7.rest_1_), channel_id=1, source_target_pairs={{0,4},{4,8},{8,12},{12,14},{14,10},{10,6},{6,2},{2,0},{1,5},{5,9},... | collective-permute-start | bytes 393224 | tf_op jit(solution)/shard_map/ppermute | solution.py:299
  17.1 0.0 collective-permute-done.11.rest_6_
  17.1 0.4 %collective-permute-start.12 = (bf16[16,16,256]{2,1,0:T(8,128)(2,1)S(1)}, bf16[16,16,256]{2,1,0:T(8,128)(2,1)S(1)}, u32[]{:S(2)}, u32[]{:S(2)}) collective-permute-start(bf16[16,16,256]{2,1,0:T(8,128)(2,1)S(1)} %collective-permute-done.11.rest_6_), channel_id=1, source_target_pairs={{4,0},{8,4},{12,8},{14,12},{10,14},{6,10},{2,6},{0,2},{5,1},{9,5},... | collective-permute-start | bytes 393224 | tf_op jit(solution)/shard_map/ppermute | solution.py:301
  17.4 0.8 %span_place.1 = (bf16[5,256,512]{2,1,0:T(8,128)(2,1)S(1)}, bf16[5,192,128]{2,1,0:T(8,128)(2,1)S(1)}, bf16[5,256,128]{2,1,0:T(8,128)(2,1)S(1)}, bf16[5,2,8,7,16,128]{5,4,3,2,1,0:T(8,128)(2,1)S(1)}) custom-call(s32[5,1,128]{2,1,0:T(1,128)S(1)} %get-tuple-element.21.limits, bf16[5,5,12,256]{3,2,1,0:T(8,128)(2,1)S(1)} %get-tuple-element.22.fk, ...), custom_call_target="tpu_custom_call" | custom-call | bytes 3145728 | tf_op jit(solution)/shard_map/span_place/pallas_call | solution.py:221
  18.2 1.2 %collective-permute-done.5.rest_6_ = bf16[16,16,256]{2,1,0:T(8,128)(2,1)S(1)} collective-permute-done((bf16[16,16,256]{2,1,0:T(8,128)(2,1)S(1)}, bf16[16,16,256]{2,1,0:T(8,128)(2,1)S(1)}, u32[]{:S(2)}, u32[]{:S(2)}) %collective-permute-start.5) | collective-permute-done | bytes 131104 | tf_op jit(solution)/shard_map/ppermute | solution.py:293
  19.5 1.2 %collective-permute-start.6 = (bf16[16,16,256]{2,1,0:T(8,128)(2,1)S(1)}, bf16[16,16,256]{2,1,0:T(8,128)(2,1)S(1)}, u32[]{:S(2)}, u32[]{:S(2)}) collective-permute-start(bf16[16,16,256]{2,1,0:T(8,128)(2,1)S(1)} %collective-permute-done.5.rest_6_), channel_id=1, source_target_pairs={{4,0},{8,4},{12,8},{14,12},{10,14},{6,10},{2,6},{0,2},{5,1},{9,5},... | collective-permute-start | bytes 393224 | tf_op jit(solution)/shard_map/ppermute | solution.py:293
  20.7 0.0 collective-permute-done.2.rest_3_
  20.7 0.8 %collective-permute-start.3 = (bf16[16,16,256]{2,1,0:T(8,128)(2,1)S(1)}, bf16[16,16,256]{2,1,0:T(8,128)(2,1)S(1)}, u32[]{:S(2)}, u32[]{:S(2)}) collective-permute-start(bf16[16,16,256]{2,1,0:T(8,128)(2,1)S(1)} %collective-permute-done.2.rest_3_), channel_id=1, source_target_pairs={{0,4},{4,8},{8,12},{12,14},{14,10},{10,6},{6,2},{2,0},{1,5},{5,9},... | collective-permute-start | bytes 393224 | tf_op jit(solution)/shard_map/ppermute | solution.py:304
  21.5 0.3 collective-permute-done.8.rest_2_
  21.8 1.3 %collective-permute-start.9 = (bf16[16,16,256]{2,1,0:T(8,128)(2,1)S(1)}, bf16[16,16,256]{2,1,0:T(8,128)(2,1)S(1)}, u32[]{:S(2)}, u32[]{:S(2)}) collective-permute-start(bf16[16,16,256]{2,1,0:T(8,128)(2,1)S(1)} %collective-permute-done.8.rest_2_), channel_id=1, source_target_pairs={{0,4},{4,8},{8,12},{12,14},{14,10},{10,6},{6,2},{2,0},{1,5},{5,9},... | collective-permute-start | bytes 393224 | tf_op jit(solution)/shard_map/ppermute | solution.py:299
  23.1 0.0 collective-permute-done.12.rest_5_
  23.1 0.7 %collective-permute-start.13 = (bf16[16,16,256]{2,1,0:T(8,128)(2,1)S(1)}, bf16[16,16,256]{2,1,0:T(8,128)(2,1)S(1)}, u32[]{:S(2)}, u32[]{:S(2)}) collective-permute-start(bf16[16,16,256]{2,1,0:T(8,128)(2,1)S(1)} %collective-permute-done.12.rest_5_), channel_id=1, source_target_pairs={{4,0},{8,4},{12,8},{14,12},{10,14},{6,10},{2,6},{0,2},{5,1},{9,5},... | collective-permute-start | bytes 393224 | tf_op jit(solution)/shard_map/ppermute | solution.py:305
  23.8 1.4 %collective-permute-done.6.rest_5_ = bf16[16,16,256]{2,1,0:T(8,128)(2,1)S(1)} collective-permute-done((bf16[16,16,256]{2,1,0:T(8,128)(2,1)S(1)}, bf16[16,16,256]{2,1,0:T(8,128)(2,1)S(1)}, u32[]{:S(2)}, u32[]{:S(2)}) %collective-permute-start.6) | collective-permute-done | bytes 131104 | tf_op jit(solution)/shard_map/ppermute | solution.py:293
  25.3 0.4 %collective-permute-done.3.rest_4_ = bf16[16,16,256]{2,1,0:T(8,128)(2,1)S(1)} collective-permute-done((bf16[16,16,256]{2,1,0:T(8,128)(2,1)S(1)}, bf16[16,16,256]{2,1,0:T(8,128)(2,1)S(1)}, u32[]{:S(2)}, u32[]{:S(2)}) %collective-permute-start.3) | collective-permute-done | bytes 131104 | tf_op jit(solution)/shard_map/ppermute | solution.py:304
  25.7 1.9 %span_weights.1.w_ref = bf16[5,2,896,256]{3,2,1,0:T(8,128)(2,1)S(1)} custom-call(s32[65]{0:T(128)S(4)} %get-tuple-element.20.slot_ref, bf16[5,256,512]{2,1,0:T(8,128)(2,1)S(1)} %get-tuple-element.28.placed, bf16[5,192,128]{2,1,0:T(8,128)(2,1)S(1)} %get-tuple-element.29.keep, bf16[5,256,128]{2,1,0:T(8,128)(2,1)S(1)} %get-tuple-element.30.bias, ...), custom_call_target="tpu_custom_call" | custom-call | flops 1174405120 | bytes 8388608 | tf_op jit(solution)/shard_map/span_weights/pallas_call | solution.py:249
  27.5 0.0 collective-permute-done.9.rest_3_
  27.5 0.5 %collective-permute-done.13.rest_4_ = bf16[16,16,256]{2,1,0:T(8,128)(2,1)S(1)} collective-permute-done((bf16[16,16,256]{2,1,0:T(8,128)(2,1)S(1)}, bf16[16,16,256]{2,1,0:T(8,128)(2,1)S(1)}, u32[]{:S(2)}, u32[]{:S(2)}) %collective-permute-start.13) | collective-permute-done | bytes 131104 | tf_op jit(solution)/shard_map/ppermute | solution.py:305
  28.1 2.3 %span_values.1 = (bf16[5,5,12,2048]{3,2,1,0:T(8,128)(2,1)}, bf16[5,32,2048]{2,1,0:T(8,128)(2,1)}) custom-call(s32[65]{0:T(128)S(4)} %get-tuple-element.20.slot_ref, bf16[5,2,896,256]{3,2,1,0:T(8,128)(2,1)S(1)} %span_weights.1.w_ref, bf16[5,256,512]{2,1,0:T(8,128)(2,1)S(1)} %get-tuple-element.28.placed, bf16[5,192,128]{2,1,0:T(8,128)(2,1)S(1)} %get-tuple-element.29.keep, ...), custom_call_target="tpu_custom_call" | custom-call | flops 1174405120 | bytes 8388608 | tf_op jit(solution)/shard_map/span_values/pallas_call | solution.py:260
Async XLA Ops:
  0.6 6.7 %collective-permute-start = (bf16[16,16,256]{2,1,0:T(8,128)(2,1)}, bf16[16,16,256]{2,1,0:T(8,128)(2,1)S(1)}, u32[]{:S(2)}, u32[]{:S(2)}) collective-permute-start(bf16[16,16,256]{2,1,0:T(8,128)(2,1)} %rest_10_.1), channel_id=1, source_target_pairs={{0,4},{4,8},{8,12},{12,14},{14,10},{10,6},{6,2},{2,0},{1,5},{5,9},... | collective-permute-start | bytes 393224 | tf_op jit(solution)/shard_map/ppermute | solution.py:291
  3.7 7.0 %collective-permute-start.10 = (bf16[16,16,256]{2,1,0:T(8,128)(2,1)}, bf16[16,16,256]{2,1,0:T(8,128)(2,1)S(1)}, u32[]{:S(2)}, u32[]{:S(2)}) collective-permute-start(bf16[16,16,256]{2,1,0:T(8,128)(2,1)} %rest_11_.1), channel_id=1, source_target_pairs={{4,0},{8,4},{12,8},{14,12},{10,14},{6,10},{2,6},{0,2},{5,1},{9,5},... | collective-permute-start | bytes 393224 | tf_op jit(solution)/shard_map/ppermute | solution.py:301
  3.7 9.5 %collective-permute-start.4 = (bf16[16,16,256]{2,1,0:T(8,128)(2,1)}, bf16[16,16,256]{2,1,0:T(8,128)(2,1)S(1)}, u32[]{:S(2)}, u32[]{:S(2)}) collective-permute-start(bf16[16,16,256]{2,1,0:T(8,128)(2,1)} %rest_10_.1), channel_id=1, source_target_pairs={{4,0},{8,4},{12,8},{14,12},{10,14},{6,10},{2,6},{0,2},{5,1},{9,5},... | collective-permute-start | bytes 393224 | tf_op jit(solution)/shard_map/ppermute | solution.py:293
  7.3 7.0 %collective-permute-start.1 = (bf16[16,16,256]{2,1,0:T(8,128)(2,1)S(1)}, bf16[16,16,256]{2,1,0:T(8,128)(2,1)S(1)}, u32[]{:S(2)}, u32[]{:S(2)}) collective-permute-start(bf16[16,16,256]{2,1,0:T(8,128)(2,1)S(1)} %collective-permute-done.rest_1_), channel_id=1, source_target_pairs={{0,4},{4,8},{8,12},{12,14},{14,10},{10,6},{6,2},{2,0},{1,5},{5,9},... | collective-permute-start | bytes 393224 | tf_op jit(solution)/shard_map/ppermute | solution.py:291
  9.2 6.2 %collective-permute-start.7 = (bf16[16,16,256]{2,1,0:T(8,128)(2,1)}, bf16[16,16,256]{2,1,0:T(8,128)(2,1)S(1)}, u32[]{:S(2)}, u32[]{:S(2)}) collective-permute-start(bf16[16,16,256]{2,1,0:T(8,128)(2,1)} %rest_11_.1), channel_id=1, source_target_pairs={{0,4},{4,8},{8,12},{12,14},{14,10},{10,6},{6,2},{2,0},{1,5},{5,9},... | collective-permute-start | bytes 393224 | tf_op jit(solution)/shard_map/ppermute | solution.py:299
  10.7 6.3 %collective-permute-start.11 = (bf16[16,16,256]{2,1,0:T(8,128)(2,1)S(1)}, bf16[16,16,256]{2,1,0:T(8,128)(2,1)S(1)}, u32[]{:S(2)}, u32[]{:S(2)}) collective-permute-start(bf16[16,16,256]{2,1,0:T(8,128)(2,1)S(1)} %collective-permute-done.10.rest_7_), channel_id=1, source_target_pairs={{4,0},{8,4},{12,8},{14,12},{10,14},{6,10},{2,6},{0,2},{5,1},{9,5},... | collective-permute-start | bytes 393224 | tf_op jit(solution)/shard_map/ppermute | solution.py:301
  13.2 6.2 %collective-permute-start.5 = (bf16[16,16,256]{2,1,0:T(8,128)(2,1)S(1)}, bf16[16,16,256]{2,1,0:T(8,128)(2,1)S(1)}, u32[]{:S(2)}, u32[]{:S(2)}) collective-permute-start(bf16[16,16,256]{2,1,0:T(8,128)(2,1)S(1)} %collective-permute-done.4.rest_7_), channel_id=1, source_target_pairs={{4,0},{8,4},{12,8},{14,12},{10,14},{6,10},{2,6},{0,2},{5,1},{9,5},... | collective-permute-start | bytes 393224 | tf_op jit(solution)/shard_map/ppermute | solution.py:293
  14.3 6.4 %collective-permute-start.2 = (bf16[16,16,256]{2,1,0:T(8,128)(2,1)S(1)}, bf16[16,16,256]{2,1,0:T(8,128)(2,1)S(1)}, u32[]{:S(2)}, u32[]{:S(2)}) collective-permute-start(bf16[16,16,256]{2,1,0:T(8,128)(2,1)S(1)} %collective-permute-done.1.rest_2_), channel_id=1, source_target_pairs={{0,4},{4,8},{8,12},{12,14},{14,10},{10,6},{6,2},{2,0},{1,5},{5,9},... | collective-permute-start | bytes 393224 | tf_op jit(solution)/shard_map/ppermute | solution.py:291
  15.4 6.4 %collective-permute-start.8 = (bf16[16,16,256]{2,1,0:T(8,128)(2,1)S(1)}, bf16[16,16,256]{2,1,0:T(8,128)(2,1)S(1)}, u32[]{:S(2)}, u32[]{:S(2)}) collective-permute-start(bf16[16,16,256]{2,1,0:T(8,128)(2,1)S(1)} %collective-permute-done.7.rest_1_), channel_id=1, source_target_pairs={{0,4},{4,8},{8,12},{12,14},{14,10},{10,6},{6,2},{2,0},{1,5},{5,9},... | collective-permute-start | bytes 393224 | tf_op jit(solution)/shard_map/ppermute | solution.py:299
  17.1 6.0 %collective-permute-start.12 = (bf16[16,16,256]{2,1,0:T(8,128)(2,1)S(1)}, bf16[16,16,256]{2,1,0:T(8,128)(2,1)S(1)}, u32[]{:S(2)}, u32[]{:S(2)}) collective-permute-start(bf16[16,16,256]{2,1,0:T(8,128)(2,1)S(1)} %collective-permute-done.11.rest_6_), channel_id=1, source_target_pairs={{4,0},{8,4},{12,8},{14,12},{10,14},{6,10},{2,6},{0,2},{5,1},{9,5},... | collective-permute-start | bytes 393224 | tf_op jit(solution)/shard_map/ppermute | solution.py:301
  19.5 5.8 %collective-permute-start.6 = (bf16[16,16,256]{2,1,0:T(8,128)(2,1)S(1)}, bf16[16,16,256]{2,1,0:T(8,128)(2,1)S(1)}, u32[]{:S(2)}, u32[]{:S(2)}) collective-permute-start(bf16[16,16,256]{2,1,0:T(8,128)(2,1)S(1)} %collective-permute-done.5.rest_6_), channel_id=1, source_target_pairs={{4,0},{8,4},{12,8},{14,12},{10,14},{6,10},{2,6},{0,2},{5,1},{9,5},... | collective-permute-start | bytes 393224 | tf_op jit(solution)/shard_map/ppermute | solution.py:293
  20.7 5.0 %collective-permute-start.3 = (bf16[16,16,256]{2,1,0:T(8,128)(2,1)S(1)}, bf16[16,16,256]{2,1,0:T(8,128)(2,1)S(1)}, u32[]{:S(2)}, u32[]{:S(2)}) collective-permute-start(bf16[16,16,256]{2,1,0:T(8,128)(2,1)S(1)} %collective-permute-done.2.rest_3_), channel_id=1, source_target_pairs={{0,4},{4,8},{8,12},{12,14},{14,10},{10,6},{6,2},{2,0},{1,5},{5,9},... | collective-permute-start | bytes 393224 | tf_op jit(solution)/shard_map/ppermute | solution.py:304
  21.8 5.7 %collective-permute-start.9 = (bf16[16,16,256]{2,1,0:T(8,128)(2,1)S(1)}, bf16[16,16,256]{2,1,0:T(8,128)(2,1)S(1)}, u32[]{:S(2)}, u32[]{:S(2)}) collective-permute-start(bf16[16,16,256]{2,1,0:T(8,128)(2,1)S(1)} %collective-permute-done.8.rest_2_), channel_id=1, source_target_pairs={{0,4},{4,8},{8,12},{12,14},{14,10},{10,6},{6,2},{2,0},{1,5},{5,9},... | collective-permute-start | bytes 393224 | tf_op jit(solution)/shard_map/ppermute | solution.py:299
  23.1 5.0 %collective-permute-start.13 = (bf16[16,16,256]{2,1,0:T(8,128)(2,1)S(1)}, bf16[16,16,256]{2,1,0:T(8,128)(2,1)S(1)}, u32[]{:S(2)}, u32[]{:S(2)}) collective-permute-start(bf16[16,16,256]{2,1,0:T(8,128)(2,1)S(1)} %collective-permute-done.12.rest_5_), channel_id=1, source_target_pairs={{4,0},{8,4},{12,8},{14,12},{10,14},{6,10},{2,6},{0,2},{5,1},{9,5},... | collective-permute-start | bytes 393224 | tf_op jit(solution)/shard_map/ppermute | solution.py:305
